TPU v7x, 32 devices: a whole 2x2x4 slice. The times are simulated.
32 devices in a mesh: groups: 2 (over x), seq: 2 (over core), tensor: 8 (over z, y).
Axes of the slice: x: 2, y: 2, z: 4, core: 2. Of those that a mesh axis runs over, the one named last changes fastest.
Arguments:
- queries: bfloat16 [1536, 16384], P(('groups', 'seq'), 'tensor'), parts along dimension 0, may hold values from -400 to 400
- keys: bfloat16 [1536, 1024], P(('groups', 'seq')), parts along dimension 0, may hold values from -4 to 4
- values: bfloat16 [1536, 1024], P(('groups', 'seq')), parts along dimension 0, may hold values from -24 to 24
- residual: bfloat16 [1536, 16384], P(('groups', 'seq'), 'tensor'), parts along dimension 0, may hold values from -112 to 112
- out_weight: bfloat16 [16384, 16384], P('tensor'), may hold values from -0.125 to 0.125
- norm_gain: bfloat16 [16384], P('tensor'), may hold values from 0.099609375 to 1.8984375
- kv_weight: bfloat16 [16384, 2048], P(None, 'tensor'), may hold values from -0.046875 to 0.046875
Outputs:
- stream: bfloat16 [1536, 16384], P(('groups', 'seq'), 'tensor'), parts along dimension 0
- kv_next: bfloat16 [1536, 2048], P(('groups', 'seq'), 'tensor'), parts along dimension 0
There are 2 independent parts, one for each index of `groups`. A program takes and returns all parts, laid end to end along the dimension named above; an argument that names none is the same for every part. Nothing has to cross between parts.
All inputs are finite; a program needn't handle non-finite values. Where the computation divides by a largest or mean magnitude, that divisor is 1e-20 or more.
Results may differ from a plain program's by a relative error of at most 0.012.
Values may be sent and summed in bfloat16 or wider, within the bound.
No kernel may reach another device: no remote copies, remote signals or barrier semaphores. Data moves between devices by JAX's collectives and lax.ppermute only.
A program may use at most 320 MiB of HBM per device.

v0:
```python
import jax
import jax.numpy as jnp
from jax import lax
from jax.sharding import PartitionSpec as P

D = 16384
Q_HEADS = 128
KV_HEADS = 8
HEAD = 128
BLOCK = 128


def from_behind(block, axis, distance):
    devices = range(lax.axis_size(axis))
    route = [(i - distance, i) for i in devices if i - distance in devices]
    return lax.ppermute(block, axis, route)


def block_pack(matrix, block_size):
    row_count = matrix.shape[0]
    blocks = matrix.reshape(row_count, matrix.shape[1] // block_size, block_size)
    scales = jnp.max(jnp.abs(blocks), axis=2) + 1e-06
    packed = (blocks / scales[:, :, None]).astype(jnp.bfloat16)
    return (packed, scales)


def on_device(queries, keys, values, residual, out_weight, norm_gain, kv_weight):
    tok_rows = queries.shape[0]
    heads_here = queries.shape[1] // HEAD
    tensor_rank = lax.axis_index("tensor")
    seq_index = lax.axis_index("seq")
    kv_group = tensor_rank * heads_here // (Q_HEADS // KV_HEADS)
    own_keys = lax.dynamic_slice_in_dim(keys, kv_group * HEAD, HEAD, 1)
    own_values = lax.dynamic_slice_in_dim(values, kv_group * HEAD, HEAD, 1)
    earlier_keys, earlier_values = from_behind((own_keys, own_values), "seq", 1)
    all_keys = jnp.concatenate([earlier_keys, own_keys], axis=0)
    all_values = jnp.concatenate([earlier_values, own_values], axis=0)
    query_pos = jnp.arange(tok_rows)[:, None]
    key_pos = jnp.arange(2 * tok_rows)[None, :] - tok_rows
    visible = (key_pos <= query_pos) & ((key_pos >= 0) | (seq_index > 0))
    head_queries = queries.reshape(tok_rows, heads_here, HEAD)
    scores = jnp.einsum(
        "thd,kd->htk", head_queries, all_keys, preferred_element_type=jnp.float32
    ) * HEAD ** (-0.5)
    scores = jnp.where(visible[None], scores, -1e30)
    row_peak = jnp.max(scores, axis=2, keepdims=True)
    weights = jnp.exp(scores - row_peak)
    shares = (weights / jnp.sum(weights, axis=2, keepdims=True)).astype(jnp.bfloat16)
    context = jnp.einsum("htk,kd->thd", shares, all_values, preferred_element_type=jnp.float32)
    context = context.astype(jnp.bfloat16).reshape(tok_rows, heads_here * HEAD)
    partial_out = jnp.dot(context, out_weight, preferred_element_type=jnp.float32)
    packed, scales = block_pack(partial_out, BLOCK)
    recv_packed, recv_scales = (
        lax.all_to_all(
            packed.reshape(tok_rows, D), "tensor", split_axis=1, concat_axis=0, tiled=True
        ),
        lax.all_to_all(
            scales.astype(jnp.bfloat16), "tensor", split_axis=1, concat_axis=0, tiled=True
        ).astype(scales.dtype),
    )
    devices = lax.axis_size("tensor")
    local_blocks = scales.shape[1] // devices
    dequant_terms = recv_packed.reshape(devices, tok_rows, local_blocks, BLOCK).astype(
        jnp.float32
    ) * recv_scales.reshape(devices, tok_rows, local_blocks, 1)
    attended = jnp.sum(dequant_terms, axis=0).reshape(tok_rows, local_blocks * BLOCK)
    stream = (residual.astype(jnp.float32) + attended).astype(jnp.bfloat16)
    widened = stream.astype(jnp.float32)
    square_total = lax.psum(jnp.sum(widened * widened, axis=1), "tensor")
    inverse = lax.rsqrt(square_total / D + 1e-05)
    normed = widened * inverse[:, None] * norm_gain.astype(jnp.float32)[None, :]
    norm_packed, norm_scales = block_pack(normed, BLOCK)
    columns = kv_weight.shape[1]
    weight_blocks = kv_weight.reshape(D // BLOCK, BLOCK, columns)
    initial = jnp.zeros((tok_rows, columns), jnp.float32)
    piece_packed = lax.all_gather(norm_packed, "tensor", axis=1, tiled=True)
    piece_scales = lax.all_gather(
        norm_scales.astype(jnp.bfloat16), "tensor", axis=1, tiled=True
    ).astype(jnp.float32)
    product = jnp.einsum(
        "tmb,mbc->tmc", piece_packed, weight_blocks, preferred_element_type=jnp.float32
    )
    projected = initial + jnp.sum(product * piece_scales[:, :, None], axis=1)
    return (stream, projected.astype(jnp.bfloat16))


def solution(mesh):
    return jax.shard_map(
        on_device,
        mesh=mesh,
        in_specs=(
            P(("groups", "seq"), "tensor"),
            P(("groups", "seq"), None),
            P(("groups", "seq"), None),
            P(("groups", "seq"), "tensor"),
            P("tensor", None),
            P("tensor"),
            P(None, "tensor"),
        ),
        out_specs=(P(("groups", "seq"), "tensor"), P(("groups", "seq"), "tensor")),
        check_vma=False,
    )
```

profile of v0, /device:TPU:0, one launch (start us, length us, event | category | flops | bytes accessed | tf_op | source)
XLA Modules:
  0.0 691.1 jit_solution(12370233961717706102)
XLA Ops:
  7.2 0.0 copy-start
  7.2 1.0 constant_dynamic-slice_fusion
  8.2 2.4 collective-permute-start.1
  10.6 0.9 constant_dynamic-slice_fusion.1
  11.5 0.1 copy.34
  11.6 1.3 collective-permute-start
  12.9 0.3 fusion.24
  13.2 86.6 %copy.33 = bf16[16384,2048]{1,0:T(8,128)(2,1)} copy(bf16[16384,2048]{0,1:T(8,128)(2,1)} %bitcast.6) | data formatting | bytes 134217728 | tf_op jit(solution)/shard_map/dot_general | solution.py:51
  99.9 0.0 collective-permute-done.1
  99.9 10.2 %fusion.36 = (f32[16,384]{1,0:T(8,128)S(1)}, f32[16,384,768]{1,2,0:T(8,128)}) fusion(pred[384,768]{0,1:T(8,128)(4,1)S(1)} %fusion.24, bf16[384,128]{1,0:T(8,128)(2,1)S(1)} %constant_dynamic-slice_fusion, bf16[384,128]{1,0:T(8,128)(2,1)S(1)} %collective-permute-done.1, bf16[384,2048]{1,0:T(8,128)(2,1)S(1)} %copy-done), kind=kOutput, calls=%fused_computation.50 | convolution fusion | flops 1227227904 | bytes 20963328 | tf_op jit(solution)/shard_map/sub | solution.py:47
  110.1 0.0 collective-permute-done
  110.1 9.0 %fusion.12 = bf16[128,16,384]{2,0,1:T(8,128)(2,1)} fusion(f32[16,384,768]{1,2,0:T(8,128)} %get-tuple-element.13, f32[16,384]{1,0:T(8,128)S(1)} %get-tuple-element.12, bf16[384,128]{0,1:T(8,128)(2,1)S(1)} %copy.34, bf16[384,128]{0,1:T(8,128)(2,1)S(1)} %collective-permute-done), kind=kOutput, calls=%fused_computation.23 | convolution fusion | flops 1218576384 | bytes 20668416 | tf_op jit(solution)/shard_map/htk,kd->thd/dot_general | solution.py:49
  119.1 45.7 %abs_reduce_fusion = (f32[384,128]{0,1:T(8,128)S(1)}, f32[384,128,128]{0,2,1:T(8,128)}) fusion(bf16[384,2048,1]{0,1,2:T(8,128)(2,1)} %bitcast.76, bf16[128,128,2048]{2,1,0:T(8,128)(2,1)} %bitcast.7), kind=kOutput, calls=%fused_computation.6 | convolution fusion | flops 25782337536 | bytes 94044160 | tf_op jit(solution)/shard_map/dot_general | solution.py:51
  164.8 0.7 fusion.35
  165.5 6.6 all-to-all-start.1
  172.1 14.2 %divide_convert_fusion = bf16[384,128,128]{0,2,1:T(8,128)(2,1)} fusion(f32[384,128,128]{0,2,1:T(8,128)} %get-tuple-element.15, f32[384,128]{0,1:T(8,128)S(1)} %get-tuple-element.9), kind=kLoop, calls=%fused_computation.5 | loop fusion | flops 12582912 | bytes 37945344 | tf_op jit(solution)/shard_map/convert_element_type | solution.py:23
  186.4 0.0 all-to-all-done.1
  186.4 6.1 all-to-all-start
  192.5 0.0 all-gather.2.cloned.1.call-start
  192.6 0.9 copy.22
  193.5 271.1 %all-to-all-done = bf16[384,8,2048]{0,2,1:T(8,128)(2,1)} async-done(((bf16[384,8,2048]{0,2,1:T(8,128)(2,1)}), bf16[384,8,2048]{0,2,1:T(8,128)(2,1)}, u32[]{:S(2)}, u32[]{:S(2)}) %all-to-all-start) | async-done | bytes 12582944 | tf_op jit(solution)/shard_map/all_to_all | solution.py:54
  464.6 9.1 %fusion.2 = f32[384,2048]{0,1:T(8,128)} fusion(bf16[384,8,2048]{0,2,1:T(8,128)(2,1)} %all-to-all-done, f32[8,384,16]{1,2,0:T(8,128)S(1)} %convert_bitcast_fusion), kind=kLoop, calls=%fused_computation.4 | loop fusion | flops 18087936 | bytes 15925248 | tf_op jit(solution)/shard_map/reduce_sum | solution.py:66
  473.6 2.5 fusion.8
  476.1 19.5 %psum.7 = f32[384]{0:T(512)S(1)} all-reduce(f32[384]{0:T(512)S(1)} %get-tuple-element.6), channel_id=1, replica_groups=mesh['groups'=2,'seq'=2,'tensor'=8] {'tensor'}, use_global_device_ids=true, to_apply=%region_5.6 | all-reduce | flops 384 | bytes 3072 | tf_op jit(solution)/shard_map/psum | solution.py:69
  495.6 0.6 abs_reduce_fusion.1
  496.2 0.6 divide_convert_fusion.3
  496.8 1.7 copy.28
  498.5 0.0 all-gather.2.cloned.1.call-update
  498.5 1.6 copy.29
  500.1 31.4 %all_gather.7 = bf16[384,128]{0,1:T(8,128)(2,1)S(1)} all-gather(bf16[384,16]{0,1:T(8,128)(2,1)S(1)} %get-tuple-element.11), channel_id=1, replica_groups=mesh['groups'=2,'seq'=2,'tensor'=8] {'tensor'}, dimensions={1}, use_global_device_ids=true | all-gather | bytes 110592 | tf_op jit(solution)/shard_map/all_gather | solution.py:77
  531.6 141.3 %all-gather.2.cloned.1.call-done = bf16[384,128,128]{2,0,1:T(8,128)(2,1)} async-done(((bf16[384,16,128]{2,0,1:T(8,128)(2,1)}), bf16[384,128,128]{2,0,1:T(8,128)(2,1)}) %all-gather.2.cloned.1.call-update) | async-done | bytes 12582928 | tf_op jit(solution)/shard_map/all_gather | solution.py:76
  672.8 11.5 %fusion.1 = bf16[384,256]{1,0:T(8,128)(2,1)} fusion(f32[384,128]{0,1:T(8,128)S(1)} %convert_element_type.74, bf16[384,128,128]{2,0,1:T(8,128)(2,1)} %all-gather.2.cloned.1.call-done, bf16[128,128,256]{2,1,0:T(8,128)(2,1)} %bitcast.75), kind=kOutput, calls=%fused_computation.2 | convolution fusion | flops 3246292992 | bytes 21364736 | tf_op jit(solution)/shard_map/tmb,mbc->tmc/dot_general | solution.py:80
  (14 shorter events, 0.1 us)
Async XLA Ops:
  7.2 92.7 %copy-start = (bf16[384,2048]{1,0:T(8,128)(2,1)S(1)}, bf16[384,2048]{1,0:T(8,128)(2,1)}, u32[]{:S(2)}) copy-start(bf16[384,2048]{1,0:T(8,128)(2,1)} %param.7) | copy-start | bytes 4718596
  8.2 91.7 %collective-permute-start.1 = (bf16[384,128]{1,0:T(8,128)(2,1)S(1)}, bf16[384,128]{1,0:T(8,128)(2,1)S(1)}, u32[]{:S(2)}, u32[]{:S(2)}) collective-permute-start(bf16[384,128]{1,0:T(8,128)(2,1)S(1)} %constant_dynamic-slice_fusion), channel_id=1, source_target_pairs={{0,8},{1,9},{2,10},{3,11},{4,12},{5,13},{6,14},{7,15},{16,24},{17,... | collective-permute-start | bytes 294920 | tf_op jit(solution)/shard_map/ppermute | solution.py:16
  11.6 98.5 %collective-permute-start = (bf16[384,128]{0,1:T(8,128)(2,1)S(1)}, bf16[384,128]{0,1:T(8,128)(2,1)S(1)}, u32[]{:S(2)}, u32[]{:S(2)}) collective-permute-start(bf16[384,128]{0,1:T(8,128)(2,1)S(1)} %copy.34), channel_id=1, source_target_pairs={{0,8},{1,9},{2,10},{3,11},{4,12},{5,13},{6,14},{7,15},{16,24},{17,... | collective-permute-start | bytes 294920 | tf_op jit(solution)/shard_map/ppermute | solution.py:16
  165.5 20.9 %all-to-all-start.1 = ((bf16[384,8,16]{0,2,1:T(8,128)(2,1)}), bf16[384,8,16]{0,2,1:T(8,128)(2,1)S(1)}, u32[]{:S(2)}, u32[]{:S(2)}) async-start(bf16[384,8,16]{0,2,1:T(8,128)(2,1)} %bitcast.10), calls=%async_computation.1 | async-start | bytes 196608 | tf_op jit(solution)/shard_map/all_to_all | solution.py:57
  186.4 6.2 copy-start.2
  186.4 278.2 %all-to-all-start = ((bf16[384,8,2048]{0,2,1:T(8,128)(2,1)}), bf16[384,8,2048]{0,2,1:T(8,128)(2,1)}, u32[]{:S(2)}, u32[]{:S(2)}) async-start(bf16[384,8,2048]{0,2,1:T(8,128)(2,1)} %bitcast.74), calls=%async_computation | async-start | bytes 25165824 | tf_op jit(solution)/shard_map/all_to_all | solution.py:54
  192.5 0.9 copy-start.3
  192.5 480.3 %all-gather.2.cloned.1.call-start = ((), (), s32[]{:S(2)}) async-start(), calls=%async_computation.2 | async-start | bytes 14155776 | tf_op jit(solution)/shard_map/all_gather | solution.py:76
  672.8 11.5 %copy-start.1 = (bf16[384,2048]{1,0:T(8,128)(2,1)S(1)}, bf16[384,2048]{1,0:T(8,128)(2,1)}, u32[]{:S(2)}) copy-start(bf16[384,2048]{1,0:T(8,128)(2,1)} %param.7) | copy-start | bytes 4718596
Sparse Core Ops, SparseCore 0:
  498.6 174.1 all-gather.1
where the time goes:
time: 694 us; the launch traced here: 691 us
  waiting for transfers between devices  412 us (59%)
  local copies, waits for them, and re-layouts  92.9 us (13%)
  matrix products  76.4 us (11%)
  blocking collectives  50.9 us (7%)
  other arithmetic  28 us (4%)
  starting transfers between devices  16.5 us (2%)
  between operations  14.2 us (2%)
    all_to_all x1, waiting for transfers between devices, on_device(): lax.all_to_all(packed.reshape(tok_rows, D), 'tensor', split_axis=1, conca...  271 us
    all_gather x1, waiting for transfers between devices, on_device(): piece_packed = lax.all_gather(norm_packed, 'tensor', axis=1, tiled=True)  141 us
    dot_general x1, local copies, waits for them, and re-layouts, on_device(): jnp.dot(context, out_weight, preferred_element_type=jnp.float32)  86.6 us
    dot_general x1, matrix products, on_device(): jnp.dot(context, out_weight, preferred_element_type=jnp.float32)  45.7 us
    all_gather x1, blocking collectives, on_device(): lax.all_gather(norm_scales.astype(jnp.bfloat16), 'tensor', axis=1, tiled=...  31.4 us
    psum x1, blocking collectives, on_device(): square_total = lax.psum(jnp.sum(widened * widened, axis=1), 'tensor')  19.5 us
    convert_element_type x2, other arithmetic, block_pack(): packed = (blocks / scales[:, :, None]).astype(jnp.bfloat16)  14.8 us
  transfers between devices with their start and end apart: 5, of which 2 were waited for; matrix products, arithmetic and copies ran while one was open for 17% of the time, Pallas kernels for 0%

commit v1 on v0

v1 whole, which is shorter than its diff:
```python
import functools
import math

import jax
import jax.numpy as jnp
from jax import lax
from jax.experimental import pallas as pl
from jax.experimental.pallas import tpu as pltpu
from jax.sharding import PartitionSpec as P

D = 16384
Q_HEADS = 128
KV_HEADS = 8
HEAD = 128
ROW_CHUNKS = 2
F32 = jnp.float32
BF16 = jnp.bfloat16
LOGIT = HEAD ** (-0.5) * math.log2(math.e)


def attend_kernel(first, seq_ref, q_ref, ek_ref, ev_ref, k_ref, v_ref, out_ref):
    rows = q_ref.shape[0]
    contract = (((1,), (1,)), ((), ()))
    q = q_ref[...]
    early = lax.dot_general(q, ek_ref[...], contract, preferred_element_type=F32)
    early = jnp.where(seq_ref[0] > 0, early, -1e30)
    own = lax.dot_general(q, k_ref[...], contract, preferred_element_type=F32)
    key_pos = lax.broadcasted_iota(jnp.int32, own.shape, 1)
    row_pos = lax.broadcasted_iota(jnp.int32, own.shape, 0) + first
    own = jnp.where(key_pos <= row_pos, own, -1e30)
    peak = jnp.maximum(
        jnp.max(early, axis=1, keepdims=True), jnp.max(own, axis=1, keepdims=True)
    )
    early = jnp.exp2((early - peak) * LOGIT)
    own = jnp.exp2((own - peak) * LOGIT)
    total = jnp.sum(early, axis=1, keepdims=True) + jnp.sum(own, axis=1, keepdims=True)
    context = jnp.dot(early.astype(BF16), ev_ref[...], preferred_element_type=F32)
    context += jnp.dot(own.astype(BF16), v_ref[...], preferred_element_type=F32)
    out_ref[...] = (context / total).astype(BF16)


def attend(queries, early_keys, early_values, own_keys, own_values, seq_index, chunk, rows):
    heads = queries.shape[1] // HEAD
    early = early_keys.shape[0]
    seen = (chunk + 1) * rows
    flops = 4 * heads * rows * (early + seen) * HEAD
    return pl.pallas_call(
        functools.partial(attend_kernel, chunk * rows),
        grid_spec=pltpu.PrefetchScalarGridSpec(
            num_scalar_prefetch=1,
            grid=(heads,),
            in_specs=[
                pl.BlockSpec((rows, HEAD), lambda h, s: (chunk, h)),
                pl.BlockSpec((early, HEAD), lambda h, s: (0, 0)),
                pl.BlockSpec((early, HEAD), lambda h, s: (0, 0)),
                pl.BlockSpec((seen, HEAD), lambda h, s: (0, 0)),
                pl.BlockSpec((seen, HEAD), lambda h, s: (0, 0)),
            ],
            out_specs=pl.BlockSpec((rows, HEAD), lambda h, s: (0, h)),
        ),
        out_shape=jax.ShapeDtypeStruct((rows, heads * HEAD), BF16),
        compiler_params=pltpu.CompilerParams(vmem_limit_bytes=32 * 2**20),
        cost_estimate=pl.CostEstimate(
            flops=flops,
            bytes_accessed=4 * rows * heads * HEAD,
            transcendentals=heads * rows * (early + seen),
        ),
    )(seq_index, queries, early_keys, early_values, own_keys, own_values)


class Chain:
    def __init__(self):
        t = lax.axis_index("tensor")
        self.z, self.y = t // 2, t % 2
        low = self.z < 2
        far = jnp.where(low, 3, 0)
        near = jnp.where(low, 2, 1)
        self.order = (far, near, 6 - far - near - self.z, self.z)

    @staticmethod
    def over(block, pairs):
        return lax.ppermute(block, "tensor", pairs)

    def to_y(self, block):
        return self.over(block, [(i, i ^ 1) for i in range(8)])

    def to_middle(self, block):
        return self.over(block, [(0, 2), (1, 3), (6, 4), (7, 5)])

    def across(self, block):
        return self.over(block, [(2, 4), (3, 5), (4, 2), (5, 3)])

    def to_z1(self, block):
        return self.over(block, [(i, i ^ 2) for i in range(8)])

    def reduce_scatter(self, term):
        got = [
            self.to_y(term(2 * place + 1 - self.y).astype(BF16)) for place in self.order
        ]
        own = [
            term(2 * place + self.y) + got[j].astype(F32)
            for j, place in enumerate(self.order)
        ]
        far = self.to_middle(own[0].astype(BF16))
        near = self.to_middle(own[1].astype(BF16))
        far = self.across((own[0] + far.astype(F32)).astype(BF16))
        near = self.across((own[1] + near.astype(F32)).astype(BF16))
        last = self.to_z1((own[2] + far.astype(F32)).astype(BF16))
        return own[3] + near.astype(F32) + last.astype(F32)

    def total(self, block):
        for step in (1, 2, 4):
            block = block + self.over(block, [(i, i ^ step) for i in range(8)])
        return block

    def relay_weight(self, weight):
        depth, columns = weight.shape
        slab = depth // 8
        part = slab // 4
        group, seq = lax.axis_index("groups"), lax.axis_index("seq")
        quarter = group * 2 + seq
        blocks = weight.reshape(4, 2, 4, part, columns)
        blocks = lax.dynamic_index_in_dim(blocks, quarter, 2, keepdims=False)
        kept = lax.dynamic_index_in_dim(blocks, self.y, 1, keepdims=False)
        sent = lax.dynamic_index_in_dim(blocks, 1 - self.y, 1, keepdims=False)
        got = self.to_y(sent)
        first = self.y == 0
        pair = jnp.stack([jnp.where(first, kept, got), jnp.where(first, got, kept)], axis=1)
        mine = jnp.zeros((4, 2, part, columns), weight.dtype)
        for step in range(4):
            place = self.z ^ step
            piece = lax.dynamic_index_in_dim(pair, place, 0, keepdims=True)
            if step:
                piece = self.over(piece, [(i, i ^ (2 * step)) for i in range(8)])
            mine = lax.dynamic_update_slice_in_dim(mine, piece, place, 0)
        mine = mine.reshape(8, part, columns)
        swap = [(0, 1), (1, 0)]
        other = lax.ppermute(mine, "groups", swap)
        whole = jnp.zeros((8, slab, columns), weight.dtype)
        beside = lax.ppermute((mine, other), "seq", swap)
        for block, g, s in (
            (mine, group, seq),
            (other, 1 - group, seq),
            (beside[0], group, 1 - seq),
            (beside[1], 1 - group, 1 - seq),
        ):
            whole = lax.dynamic_update_slice_in_dim(whole, block, (g * 2 + s) * part, 1)
        return whole


def on_device(queries, keys, values, residual, out_weight, norm_gain, kv_weight):
    tokens = queries.shape[0]
    heads_here = queries.shape[1] // HEAD
    devices = lax.axis_size("tensor")
    width = D // devices
    columns = kv_weight.shape[1]
    tensor_rank = lax.axis_index("tensor")
    seq_index = lax.axis_index("seq")
    kv_group = tensor_rank * heads_here // (Q_HEADS // KV_HEADS)
    own_keys = lax.dynamic_slice_in_dim(keys, kv_group * HEAD, HEAD, 1)
    own_values = lax.dynamic_slice_in_dim(values, kv_group * HEAD, HEAD, 1)
    early_keys, early_values = lax.ppermute((own_keys, own_values), "seq", [(0, 1)])
    gain = norm_gain.astype(F32)[None, :]
    chained = devices == 8
    chunks = ROW_CHUNKS if chained else 1
    rows = tokens // chunks
    if chained:
        chain = Chain()
        slab_weight = chain.relay_weight(kv_weight)
    streams, projections = [], []
    for chunk in range(chunks):
        context = attend(
            queries, early_keys, early_values, own_keys, own_values,
            seq_index.reshape(1), chunk, rows,
        )

        def out_term(t):
            weight = lax.dynamic_slice_in_dim(out_weight, t * width, width, 1)
            return jnp.dot(context, weight, preferred_element_type=F32)

        if chained:
            attended = chain.reduce_scatter(out_term)
        else:
            partial = jnp.dot(context, out_weight, preferred_element_type=F32).astype(BF16)
            attended = lax.psum_scatter(
                partial, "tensor", scatter_dimension=1, tiled=True
            ).astype(F32)
        start = residual[chunk * rows : (chunk + 1) * rows]
        stream = (start.astype(F32) + attended).astype(BF16)
        widened = stream.astype(F32)
        squares = jnp.sum(widened * widened, axis=1)
        scaled = (widened * gain).astype(BF16)
        if chained:
            total = chain.total(squares)

            def kv_term(t):
                weight = lax.dynamic_index_in_dim(slab_weight, t, 0, keepdims=False)
                return jnp.dot(scaled, weight, preferred_element_type=F32)

            projected = chain.reduce_scatter(kv_term)
        else:
            total = lax.psum(squares, "tensor")
            everything = lax.all_gather(scaled, "tensor", axis=1, tiled=True)
            projected = jnp.dot(everything, kv_weight, preferred_element_type=F32)
        inverse = lax.rsqrt(total / D + 1e-05)
        streams.append(stream)
        projections.append((projected * inverse[:, None]).astype(BF16))
    return jnp.concatenate(streams, axis=0), jnp.concatenate(projections, axis=0)


def solution(mesh):
    return jax.shard_map(
        on_device,
        mesh=mesh,
        in_specs=(
            P(("groups", "seq"), "tensor"),
            P(("groups", "seq"), None),
            P(("groups", "seq"), None),
            P(("groups", "seq"), "tensor"),
            P("tensor", None),
            P("tensor"),
            P(None, "tensor"),
        ),
        out_specs=(P(("groups", "seq"), "tensor"), P(("groups", "seq"), "tensor")),
        check_vma=False,
    )
```

time: 694 us -> 372 us (0.54)
  waiting for transfers between devices: 412 us -> 121 us
  starting transfers between devices: 16.5 us -> 113 us
  local copies, waits for them, and re-layouts: 92.9 us -> 13 us
  blocking collectives: 50.9 us -> 0 us
  other arithmetic: 28 us -> 5.43 us
  matrix products: 76.4 us -> 94.8 us
  Pallas kernels: 0 us -> 18.2 us
  between operations: 14.2 us -> 1.84 us
    all_to_all x2 -> x0, waiting for transfers between devices: 271 us -> none  [the longest x1 271 us: on_device(): lax.all_to_all(packed.reshape(tok_rows, D), 'tensor', split_axis=1, conca...]
    all_gather x1 -> x0, waiting for transfers between devices: 141 us -> none  [on_device(): piece_packed = lax.all_gather(norm_packed, 'tensor', axis=1, tiled=True)]
    ppermute x2 -> x51, waiting for transfers between devices: 0.01 us -> 121 us  [the longest x46 119 us: over(): return lax.ppermute(block, 'tensor', pairs)]
    ppermute x2 -> x51, starting transfers between devices: 3.65 us -> 113 us  [the longest x46 108 us: over(): return lax.ppermute(block, 'tensor', pairs)]
    dot_general x1 -> x0, local copies, waits for them, and re-layouts: 86.6 us -> none  [on_device(): jnp.dot(context, out_weight, preferred_element_type=jnp.float32)]
    all_gather x1 -> x0, blocking collectives: 31.4 us -> none  [on_device(): lax.all_gather(norm_scales.astype(jnp.bfloat16), 'tensor', axis=1, tiled=...]
    dot_general x3 -> x32, matrix products: 66.2 us -> 94.8 us  [the longest x16 88.6 us: out_term(): return jnp.dot(context, weight, preferred_element_type=F32)]
    psum x1 -> x0, blocking collectives: 19.5 us -> none  [on_device(): square_total = lax.psum(jnp.sum(widened * widened, axis=1), 'tensor')]
  transfers between devices with their start and end apart: 5 -> 51, of which waited for: 2 -> 18; matrix products, arithmetic and copies ran while one was open for 17% -> 30% of each run, Pallas kernels for 0% -> 5%
where the time goes in v1:
time: 372 us; the launch traced here: 367 us
  waiting for transfers between devices  121 us (33%)
  starting transfers between devices  113 us (30%)
  matrix products  94.8 us (25%)
  Pallas kernels  18.2 us (5%)
  local copies, waits for them, and re-layouts  13 us (3%)
  other arithmetic  5.43 us (1%)
    ppermute x46, waiting for transfers between devices, over(): return lax.ppermute(block, 'tensor', pairs)  119 us
    ppermute x46, starting transfers between devices, over(): return lax.ppermute(block, 'tensor', pairs)  108 us
    dot_general x16, matrix products, out_term(): return jnp.dot(context, weight, preferred_element_type=F32)  88.6 us
    pallas_call x2, Pallas kernels, attend(): pl.pallas_call(functools.partial(attend_kernel, chunk * rows), grid_spec=...  18.2 us
  transfers between devices with their start and end apart: 51, of which 18 were waited for; matrix products, arithmetic and copies ran while one was open for 30% of the time, Pallas kernels for 5%

profile of v1, /device:TPU:0, one launch (start us, length us, event | category | flops | bytes accessed | tf_op | source)
XLA Modules:
  0.0 367.2 jit_solution(15243906908124087672)
XLA Ops:
  11.0 9.2 %shard_map.86 = bf16[192,2048]{1,0:T(8,128)(2,1)S(1)} custom-call(s32[1]{0:T(128)} %bitcast.seq_ref, bf16[384,2048]{1,0:T(8,128)(2,1)S(1)} %copy-done.2, bf16[384,128]{1,0:T(8,128)(2,1)S(1)} %collective-permute-done.ek_ref, bf16[384,128]{1,0:T(8,128)(2,1)S(1)} %collective-permute-done.1.ev_ref, bf16[384,128]{1,0:T(8,128)(2,1)S(1)} %constant_dynamic-slice_fusion.1.k_ref, ...), custom_call_target="tpu_custom_call" | custom-call | flops 905969664 | bytes 1572864 | tf_op jit(solution)/shard_map/pallas_call | solution.py:47
  20.2 5.2 %fusion.98 = bf16[192,2048]{1,0:T(8,128)(2,1)S(1)} fusion(bf16[192,2048]{1,0:T(8,128)(2,1)S(1)} %shard_map.86, bf16[2048,16384]{1,0:T(8,128)(2,1)} %param.11, s32[]{:T(128)S(6)} %select_n.161), kind=kOutput, calls=%fused_computation.62 | convolution fusion | flops 1611005952 | bytes 9961476 | tf_op jit(solution)/shard_map/dot_general | solution.py:179
  25.4 5.2 %fusion.86 = bf16[192,2048]{1,0:T(8,128)(2,1)S(1)} fusion(bf16[192,2048]{1,0:T(8,128)(2,1)S(1)} %shard_map.86, bf16[2048,16384]{1,0:T(8,128)(2,1)} %param.11, s32[]{:T(128)S(6)} %select_n.156), kind=kOutput, calls=%fused_computation.58 | convolution fusion | flops 1611005952 | bytes 9961476 | tf_op jit(solution)/shard_map/dot_general | solution.py:179
  30.6 9.0 %shard_map.87 = bf16[192,2048]{1,0:T(8,128)(2,1)S(1)} custom-call(s32[1]{0:T(128)} %bitcast.seq_ref, bf16[384,2048]{1,0:T(8,128)(2,1)S(1)} %copy-done.2, bf16[384,128]{1,0:T(8,128)(2,1)S(1)} %collective-permute-done.ek_ref, bf16[384,128]{1,0:T(8,128)(2,1)S(1)} %collective-permute-done.1.ev_ref, bf16[384,128]{1,0:T(8,128)(2,1)S(1)} %constant_dynamic-slice_fusion.1.k_ref, ...), custom_call_target="tpu_custom_call" | custom-call | flops 1207959552 | bytes 1572864 | tf_op jit(solution)/shard_map/pallas_call | solution.py:47
  39.6 5.2 %fusion.89 = bf16[192,2048]{1,0:T(8,128)(2,1)S(1)} fusion(bf16[192,2048]{1,0:T(8,128)(2,1)S(1)} %shard_map.87, bf16[2048,16384]{1,0:T(8,128)(2,1)} %param.11, s32[]{:T(128)S(6)} %select_n.156), kind=kOutput, calls=%fused_computation.59 | convolution fusion | flops 1611005952 | bytes 9961476 | tf_op jit(solution)/shard_map/dot_general | solution.py:179
  44.8 5.2 %fusion.101 = bf16[192,2048]{1,0:T(8,128)(2,1)S(1)} fusion(bf16[192,2048]{1,0:T(8,128)(2,1)S(1)} %shard_map.87, bf16[2048,16384]{1,0:T(8,128)(2,1)} %param.11, s32[]{:T(128)S(6)} %select_n.161), kind=kOutput, calls=%fused_computation.63 | convolution fusion | flops 1611005952 | bytes 9961476 | tf_op jit(solution)/shard_map/dot_general | solution.py:179
  50.0 5.2 %fusion.92 = bf16[192,2048]{1,0:T(8,128)(2,1)S(1)} fusion(bf16[192,2048]{1,0:T(8,128)(2,1)S(1)} %shard_map.86, bf16[2048,16384]{1,0:T(8,128)(2,1)} %param.11, s32[]{:T(128)S(6)} %select_n.159), kind=kOutput, calls=%fused_computation.60 | convolution fusion | flops 1611005952 | bytes 9961476 | tf_op jit(solution)/shard_map/dot_general | solution.py:179
  55.2 5.2 %fusion.95 = bf16[192,2048]{1,0:T(8,128)(2,1)S(1)} fusion(bf16[192,2048]{1,0:T(8,128)(2,1)S(1)} %shard_map.87, bf16[2048,16384]{1,0:T(8,128)(2,1)} %param.11, s32[]{:T(128)S(6)} %select_n.159), kind=kOutput, calls=%fused_computation.61 | convolution fusion | flops 1611005952 | bytes 9961476 | tf_op jit(solution)/shard_map/dot_general | solution.py:179
  62.5 5.2 %fusion.80 = bf16[192,2048]{1,0:T(8,128)(2,1)S(1)} fusion(bf16[192,2048]{1,0:T(8,128)(2,1)S(1)} %shard_map.86, bf16[2048,16384]{1,0:T(8,128)(2,1)} %param.11, s32[]{:T(128)S(6)} %select_n.153), kind=kOutput, calls=%fused_computation.56 | convolution fusion | flops 1611005952 | bytes 9961476 | tf_op jit(solution)/shard_map/dot_general | solution.py:179
  67.7 6.1 %fusion.83 = bf16[192,2048]{1,0:T(8,128)(2,1)} fusion(bf16[192,2048]{1,0:T(8,128)(2,1)S(1)} %shard_map.87, bf16[2048,16384]{1,0:T(8,128)(2,1)} %param.11, s32[]{:T(128)S(6)} %select_n.153), kind=kOutput, calls=%fused_computation.57 | convolution fusion | flops 1611005952 | bytes 9961476 | tf_op jit(solution)/shard_map/dot_general | solution.py:179
  75.8 5.1 %collective-permute-done.7 = bf16[192,2048]{1,0:T(8,128)(2,1)S(1)} collective-permute-done((bf16[192,2048]{1,0:T(8,128)(2,1)S(1)}, bf16[192,2048]{1,0:T(8,128)(2,1)S(1)}, u32[]{:S(2)}, u32[]{:S(2)}) %collective-permute-start.7) | collective-permute-done | bytes 786464 | tf_op jit(solution)/shard_map/ppermute | solution.py:82
  80.9 5.2 %fusion.221 = (bf16[192,2048]{1,0:T(8,128)(2,1)S(1)}, f32[192,2048]{1,0:T(8,128)S(1)}) fusion(bf16[192,2048]{1,0:T(8,128)(2,1)S(1)} %collective-permute-done.7, bf16[192,2048]{1,0:T(8,128)(2,1)S(1)} %shard_map.86, bf16[2048,16384]{1,0:T(8,128)(2,1)} %param.11, s32[]{:T(128)S(6)} %select_n.160), kind=kOutput, calls=%fused_computation.201 | convolution fusion | flops 1611792384 | bytes 12320772 | tf_op jit(solution)/shard_map/dot_general | solution.py:179
  86.2 11.6 %collective-permute-done.3 = bf16[192,2048]{1,0:T(8,128)(2,1)S(1)} collective-permute-done((bf16[192,2048]{1,0:T(8,128)(2,1)S(1)}, bf16[192,2048]{1,0:T(8,128)(2,1)S(1)}, u32[]{:S(2)}, u32[]{:S(2)}) %collective-permute-start.3) | collective-permute-done | bytes 786464 | tf_op jit(solution)/shard_map/ppermute | solution.py:82
  101.5 5.2 %fusion.222 = (bf16[192,2048]{1,0:T(8,128)(2,1)S(1)}, f32[192,2048]{1,0:T(8,128)S(1)}) fusion(bf16[192,2048]{1,0:T(8,128)(2,1)S(1)} %collective-permute-done.3, bf16[192,2048]{1,0:T(8,128)(2,1)S(1)} %shard_map.86, bf16[2048,16384]{1,0:T(8,128)(2,1)} %param.11, s32[]{:T(128)S(6)} %select_n.155), kind=kOutput, calls=%fused_computation.202 | convolution fusion | flops 1611792384 | bytes 12320772 | tf_op jit(solution)/shard_map/dot_general | solution.py:179
  110.9 20.6 %collective-permute-done.12 = bf16[192,2048]{1,0:T(8,128)(2,1)S(1)} collective-permute-done((bf16[192,2048]{1,0:T(8,128)(2,1)S(1)}, bf16[192,2048]{1,0:T(8,128)(2,1)S(1)}, u32[]{:S(2)}, u32[]{:S(2)}) %collective-permute-start.12) | collective-permute-done | bytes 786464 | tf_op jit(solution)/shard_map/ppermute | solution.py:82
  131.5 5.2 %fusion.220 = (bf16[192,2048]{1,0:T(8,128)(2,1)S(1)}, f32[192,2048]{1,0:T(8,128)S(1)}) fusion(bf16[192,2048]{1,0:T(8,128)(2,1)S(1)} %collective-permute-done.12, bf16[192,2048]{1,0:T(8,128)(2,1)S(1)} %shard_map.87, bf16[2048,16384]{1,0:T(8,128)(2,1)} %param.11, s32[]{:T(128)S(6)} %select_n.155), kind=kOutput, calls=%fused_computation.200 | convolution fusion | flops 1611792384 | bytes 12320772 | tf_op jit(solution)/shard_map/dot_general | solution.py:179
  139.4 7.1 %collective-permute-done.16 = bf16[192,2048]{1,0:T(8,128)(2,1)S(1)} collective-permute-done((bf16[192,2048]{1,0:T(8,128)(2,1)S(1)}, bf16[192,2048]{1,0:T(8,128)(2,1)S(1)}, u32[]{:S(2)}, u32[]{:S(2)}) %collective-permute-start.16) | collective-permute-done | bytes 786464 | tf_op jit(solution)/shard_map/ppermute | solution.py:82
  150.0 5.2 %fusion.219 = (bf16[192,2048]{1,0:T(8,128)(2,1)S(1)}, f32[192,2048]{1,0:T(8,128)S(1)}) fusion(bf16[192,2048]{1,0:T(8,128)(2,1)S(1)} %collective-permute-done.16, bf16[192,2048]{1,0:T(8,128)(2,1)S(1)} %shard_map.87, bf16[2048,16384]{1,0:T(8,128)(2,1)} %param.11, s32[]{:T(128)S(6)} %select_n.160), kind=kOutput, calls=%fused_computation.199 | convolution fusion | flops 1611792384 | bytes 12320772 | tf_op jit(solution)/shard_map/dot_general | solution.py:179
  157.6 13.8 %collective-permute-done.22 = bf16[1,2,512,256]{3,2,1,0:T(8,128)(2,1)S(1)} collective-permute-done((bf16[1,2,512,256]{3,2,1,0:T(8,128)(2,1)S(1)}, bf16[1,2,512,256]{3,2,1,0:T(8,128)(2,1)S(1)}, u32[]{:S(2)}, u32[]{:S(2)}) %collective-permute-start.22) | collective-permute-done | bytes 524320 | tf_op jit(solution)/shard_map/ppermute | solution.py:82
  172.7 11.3 %collective-permute-start.13 = (bf16[192,2048]{1,0:T(8,128)(2,1)S(1)}, bf16[192,2048]{1,0:T(8,128)(2,1)S(1)}, u32[]{:S(2)}, u32[]{:S(2)}) collective-permute-start(bf16[192,2048]{1,0:T(8,128)(2,1)S(1)} %get-tuple-element.10), channel_id=1, source_target_pairs={{0,2},{1,3},{6,4},{7,5},{8,10},{9,11},{14,12},{15,13},{16,18},{17,... | collective-permute-start | bytes 2359304 | tf_op jit(solution)/shard_map/ppermute | solution.py:82
  187.4 30.5 %collective-permute-done.17 = bf16[192,2048]{1,0:T(8,128)(2,1)S(1)} collective-permute-done((bf16[192,2048]{1,0:T(8,128)(2,1)S(1)}, bf16[192,2048]{1,0:T(8,128)(2,1)S(1)}, u32[]{:S(2)}, u32[]{:S(2)}) %collective-permute-start.17) | collective-permute-done | bytes 786464 | tf_op jit(solution)/shard_map/ppermute | solution.py:82
  220.8 6.2 %fusion.107 = bf16[192,2048]{1,0:T(8,128)(2,1)} fusion(bf16[192,2048]{1,0:T(8,128)(2,1)S(1)} %shard_map.86, bf16[2048,16384]{1,0:T(8,128)(2,1)} %param.11, s32[]{:T(128)S(6)} %select_n.158, bf16[192,2048]{1,0:T(8,128)(2,1)S(1)} %collective-permute-done.9, bf16[192,2048]{1,0:T(8,128)(2,1)S(1)} %collective-permute-done.6), kind=kOutput, calls=%fused_computation.65 | convolution fusion | flops 1612578816 | bytes 11534340 | tf_op jit(solution)/shard_map/dot_general | solution.py:179
  228.5 6.6 %collective-permute-start.10 = (bf16[192,2048]{1,0:T(8,128)(2,1)}, bf16[192,2048]{1,0:T(8,128)(2,1)}, u32[]{:S(2)}, u32[]{:S(2)}) collective-permute-start(bf16[192,2048]{1,0:T(8,128)(2,1)} %fusion.107), channel_id=1, source_target_pairs={{0,2},{1,3},{2,0},{3,1},{4,6},{5,7},{6,4},{7,5},{8,10},{9,11},{10,... | collective-permute-start | bytes 2359304 | tf_op jit(solution)/shard_map/ppermute | solution.py:82
  237.0 6.2 %fusion.104 = bf16[192,2048]{1,0:T(8,128)(2,1)} fusion(bf16[192,2048]{1,0:T(8,128)(2,1)S(1)} %shard_map.87, bf16[2048,16384]{1,0:T(8,128)(2,1)} %param.11, s32[]{:T(128)S(6)} %select_n.158, bf16[192,2048]{1,0:T(8,128)(2,1)S(1)} %collective-permute-done.18, bf16[192,2048]{1,0:T(8,128)(2,1)S(1)} %collective-permute-done.15), kind=kOutput, calls=%fused_computation.64 | convolution fusion | flops 1612578816 | bytes 11534340 | tf_op jit(solution)/shard_map/dot_general | solution.py:179
  244.9 17.4 %collective-permute-start.19 = (bf16[192,2048]{1,0:T(8,128)(2,1)}, bf16[192,2048]{1,0:T(8,128)(2,1)}, u32[]{:S(2)}, u32[]{:S(2)}) collective-permute-start(bf16[192,2048]{1,0:T(8,128)(2,1)} %fusion.104), channel_id=1, source_target_pairs={{0,2},{1,3},{2,0},{3,1},{4,6},{5,7},{6,4},{7,5},{8,10},{9,11},{10,... | collective-permute-start | bytes 2359304 | tf_op jit(solution)/shard_map/ppermute | solution.py:82
  264.9 6.6 %fusion.117 = (f32[192]{0:T(256)S(1)}, bf16[192,2048]{1,0:T(8,128)(2,1)S(1)}) fusion(bf16[192,2048]{1,0:T(8,128)(2,1)} %collective-permute-done.10, bf16[192,2048]{1,0:T(8,128)(2,1)} %collective-permute-done.5, bf16[192,2048]{1,0:T(8,128)(2,1)} %collective-permute-done.2, bf16[192,2048]{1,0:T(8,128)(2,1)S(1)} %shard_map.86, bf16[2048,16384]{1,0:T(8,128)(2,1)} %param.11, ...), kind=kOutput, calls=%fused_computation.73 | convolution fusion | flops 1615331072 | bytes 13107972 | tf_op jit(solution)/shard_map/dot_general | solution.py:179
  276.2 6.4 %fusion.119 = (f32[192]{0:T(256)S(1)}, bf16[192,2048]{1,0:T(8,128)(2,1)S(1)}) fusion(bf16[192,2048]{1,0:T(8,128)(2,1)} %collective-permute-done.19, bf16[192,2048]{1,0:T(8,128)(2,1)} %collective-permute-done.14, bf16[192,2048]{1,0:T(8,128)(2,1)} %collective-permute-done.11, bf16[192,2048]{1,0:T(8,128)(2,1)S(1)} %shard_map.87, ...), kind=kOutput, calls=%fused_computation.75 | convolution fusion | flops 1615331072 | bytes 13107972 | tf_op jit(solution)/shard_map/dot_general | solution.py:179
  309.2 5.8 %collective-permute-done.40 = bf16[192,256]{1,0:T(8,128)(2,1)S(1)} collective-permute-done((bf16[192,256]{1,0:T(8,128)(2,1)S(1)}, bf16[192,256]{1,0:T(8,128)(2,1)S(1)}, u32[]{:S(2)}, u32[]{:S(2)}) %collective-permute-start.40) | collective-permute-done | bytes 98336 | tf_op jit(solution)/shard_map/ppermute | solution.py:82
  325.6 4.3 %collective-permute-start.33 = (bf16[192,256]{1,0:T(8,128)(2,1)S(1)}, bf16[192,256]{1,0:T(8,128)(2,1)S(1)}, u32[]{:S(2)}, u32[]{:S(2)}) collective-permute-start(bf16[192,256]{1,0:T(8,128)(2,1)S(1)} %get-tuple-element.22), channel_id=1, source_target_pairs={{0,2},{1,3},{6,4},{7,5},{8,10},{9,11},{14,12},{15,13},{16,18},{17,... | collective-permute-start | bytes 294920 | tf_op jit(solution)/shard_map/ppermute | solution.py:82
  332.1 4.3 %collective-permute-start.41 = (bf16[192,256]{1,0:T(8,128)(2,1)S(1)}, bf16[192,256]{1,0:T(8,128)(2,1)S(1)}, u32[]{:S(2)}, u32[]{:S(2)}) collective-permute-start(bf16[192,256]{1,0:T(8,128)(2,1)S(1)} %get-tuple-element.18), channel_id=1, source_target_pairs={{0,2},{1,3},{6,4},{7,5},{8,10},{9,11},{14,12},{15,13},{16,18},{17,... | collective-permute-start | bytes 294920 | tf_op jit(solution)/shard_map/ppermute | solution.py:82
  338.6 4.3 %collective-permute-start.45 = (bf16[192,256]{1,0:T(8,128)(2,1)S(1)}, bf16[192,256]{1,0:T(8,128)(2,1)S(1)}, u32[]{:S(2)}, u32[]{:S(2)}) collective-permute-start(bf16[192,256]{1,0:T(8,128)(2,1)S(1)} %get-tuple-element.16), channel_id=1, source_target_pairs={{0,2},{1,3},{6,4},{7,5},{8,10},{9,11},{14,12},{15,13},{16,18},{17,... | collective-permute-start | bytes 294920 | tf_op jit(solution)/shard_map/ppermute | solution.py:82
  348.3 12.2 %collective-permute-start.35 = (bf16[192,256]{1,0:T(8,128)(2,1)S(1)}, bf16[192,256]{1,0:T(8,128)(2,1)S(1)}, u32[]{:S(2)}, u32[]{:S(2)}) collective-permute-start(bf16[192,256]{1,0:T(8,128)(2,1)S(1)} %fusion.131), channel_id=1, source_target_pairs={{0,2},{1,3},{2,0},{3,1},{4,6},{5,7},{6,4},{7,5},{8,10},{9,11},{10,... | collective-permute-start | bytes 294920 | tf_op jit(solution)/shard_map/ppermute | solution.py:82
  (145 shorter events, 103.6 us)
Async XLA Ops:
  8.7 98.1 %collective-permute-start.20 = (bf16[4,512,256]{2,1,0:T(8,128)(2,1)}, bf16[4,512,256]{2,1,0:T(8,128)(2,1)}, u32[]{:S(2)}, u32[]{:S(2)}) collective-permute-start(bf16[4,512,256]{2,1,0:T(8,128)(2,1)} %dynamic-slice_bitcast_fusion), channel_id=1, source_target_pairs={{0,1},{1,0},{2,3},{3,2},{4,5},{5,4},{6,7},{7,6},{8,9},{9,8},{10,11... | collective-permute-start | bytes 3145736 | tf_op jit(solution)/shard_map/ppermute | solution.py:82
  60.4 20.5 %collective-permute-start.7 = (bf16[192,2048]{1,0:T(8,128)(2,1)S(1)}, bf16[192,2048]{1,0:T(8,128)(2,1)S(1)}, u32[]{:S(2)}, u32[]{:S(2)}) collective-permute-start(bf16[192,2048]{1,0:T(8,128)(2,1)S(1)} %fusion.98), channel_id=1, source_target_pairs={{0,1},{1,0},{2,3},{3,2},{4,5},{5,4},{6,7},{7,6},{8,9},{9,8},{10,11... | collective-permute-start | bytes 2359304 | tf_op jit(solution)/shard_map/ppermute | solution.py:82
  60.5 37.3 %collective-permute-start.3 = (bf16[192,2048]{1,0:T(8,128)(2,1)S(1)}, bf16[192,2048]{1,0:T(8,128)(2,1)S(1)}, u32[]{:S(2)}, u32[]{:S(2)}) collective-permute-start(bf16[192,2048]{1,0:T(8,128)(2,1)S(1)} %fusion.86), channel_id=1, source_target_pairs={{0,1},{1,0},{2,3},{3,2},{4,5},{5,4},{6,7},{7,6},{8,9},{9,8},{10,11... | collective-permute-start | bytes 2359304 | tf_op jit(solution)/shard_map/ppermute | solution.py:82
  73.8 145.7 %collective-permute-start.6 = (bf16[192,2048]{1,0:T(8,128)(2,1)S(1)}, bf16[192,2048]{1,0:T(8,128)(2,1)S(1)}, u32[]{:S(2)}, u32[]{:S(2)}) collective-permute-start(bf16[192,2048]{1,0:T(8,128)(2,1)S(1)} %fusion.92), channel_id=1, source_target_pairs={{0,1},{1,0},{2,3},{3,2},{4,5},{5,4},{6,7},{7,6},{8,9},{9,8},{10,11... | collective-permute-start | bytes 2359304 | tf_op jit(solution)/shard_map/ppermute | solution.py:82
  73.8 57.6 %collective-permute-start.12 = (bf16[192,2048]{1,0:T(8,128)(2,1)S(1)}, bf16[192,2048]{1,0:T(8,128)(2,1)S(1)}, u32[]{:S(2)}, u32[]{:S(2)}) collective-permute-start(bf16[192,2048]{1,0:T(8,128)(2,1)S(1)} %fusion.89), channel_id=1, source_target_pairs={{0,1},{1,0},{2,3},{3,2},{4,5},{5,4},{6,7},{7,6},{8,9},{9,8},{10,11... | collective-permute-start | bytes 2359304 | tf_op jit(solution)/shard_map/ppermute | solution.py:82
  80.9 65.5 %collective-permute-start.16 = (bf16[192,2048]{1,0:T(8,128)(2,1)S(1)}, bf16[192,2048]{1,0:T(8,128)(2,1)S(1)}, u32[]{:S(2)}, u32[]{:S(2)}) collective-permute-start(bf16[192,2048]{1,0:T(8,128)(2,1)S(1)} %fusion.101), channel_id=1, source_target_pairs={{0,1},{1,0},{2,3},{3,2},{4,5},{5,4},{6,7},{7,6},{8,9},{9,8},{10,11... | collective-permute-start | bytes 2359304 | tf_op jit(solution)/shard_map/ppermute | solution.py:82
  97.8 87.1 %collective-permute-start.8 = (bf16[192,2048]{1,0:T(8,128)(2,1)S(1)}, bf16[192,2048]{1,0:T(8,128)(2,1)S(1)}, u32[]{:S(2)}, u32[]{:S(2)}) collective-permute-start(bf16[192,2048]{1,0:T(8,128)(2,1)S(1)} %get-tuple-element.12), channel_id=1, source_target_pairs={{0,2},{1,3},{6,4},{7,5},{8,10},{9,11},{14,12},{15,13},{16,18},{17,... | collective-permute-start | bytes 2359304 | tf_op jit(solution)/shard_map/ppermute | solution.py:82
  110.9 44.3 %collective-permute-start.21 = (bf16[1,2,512,256]{3,2,1,0:T(8,128)(2,1)S(1)}, bf16[1,2,512,256]{3,2,1,0:T(8,128)(2,1)S(1)}, u32[]{:S(2)}, u32[]{:S(2)}) collective-permute-start(bf16[1,2,512,256]{3,2,1,0:T(8,128)(2,1)S(1)} %get-tuple-element.6), channel_id=1, source_target_pairs={{0,2},{1,3},{2,0},{3,1},{4,6},{5,7},{6,4},{7,5},{8,10},{9,11},{10,... | collective-permute-start | bytes 1572872 | tf_op jit(solution)/shard_map/ppermute | solution.py:82
  136.7 34.7 %collective-permute-start.22 = (bf16[1,2,512,256]{3,2,1,0:T(8,128)(2,1)S(1)}, bf16[1,2,512,256]{3,2,1,0:T(8,128)(2,1)S(1)}, u32[]{:S(2)}, u32[]{:S(2)}) collective-permute-start(bf16[1,2,512,256]{3,2,1,0:T(8,128)(2,1)S(1)} %get-tuple-element.7), channel_id=1, source_target_pairs={{0,4},{1,5},{2,6},{3,7},{4,0},{5,1},{6,2},{7,3},{8,12},{9,13},{10,... | collective-permute-start | bytes 1572872 | tf_op jit(solution)/shard_map/ppermute | solution.py:82
  146.4 26.3 %collective-permute-start.23 = (bf16[1,2,512,256]{3,2,1,0:T(8,128)(2,1)S(1)}, bf16[1,2,512,256]{3,2,1,0:T(8,128)(2,1)S(1)}, u32[]{:S(2)}, u32[]{:S(2)}) collective-permute-start(bf16[1,2,512,256]{3,2,1,0:T(8,128)(2,1)S(1)} %get-tuple-element.4), channel_id=1, source_target_pairs={{0,6},{1,7},{2,4},{3,5},{4,2},{5,3},{6,0},{7,1},{8,14},{9,15},{10,... | collective-permute-start | bytes 1572872 | tf_op jit(solution)/shard_map/ppermute | solution.py:82
  155.2 31.2 %collective-permute-start.4 = (bf16[192,2048]{1,0:T(8,128)(2,1)S(1)}, bf16[192,2048]{1,0:T(8,128)(2,1)S(1)}, u32[]{:S(2)}, u32[]{:S(2)}) collective-permute-start(bf16[192,2048]{1,0:T(8,128)(2,1)S(1)} %get-tuple-element.14), channel_id=1, source_target_pairs={{0,2},{1,3},{6,4},{7,5},{8,10},{9,11},{14,12},{15,13},{16,18},{17,... | collective-permute-start | bytes 2359304 | tf_op jit(solution)/shard_map/ppermute | solution.py:82
  171.4 55.6 %collective-permute-start.15 = (bf16[192,2048]{1,0:T(8,128)(2,1)S(1)}, bf16[192,2048]{1,0:T(8,128)(2,1)S(1)}, u32[]{:S(2)}, u32[]{:S(2)}) collective-permute-start(bf16[192,2048]{1,0:T(8,128)(2,1)S(1)} %fusion.95), channel_id=1, source_target_pairs={{0,1},{1,0},{2,3},{3,2},{4,5},{5,4},{6,7},{7,6},{8,9},{9,8},{10,11... | collective-permute-start | bytes 2359304 | tf_op jit(solution)/shard_map/ppermute | solution.py:82
  172.7 55.8 %collective-permute-start.13 = (bf16[192,2048]{1,0:T(8,128)(2,1)S(1)}, bf16[192,2048]{1,0:T(8,128)(2,1)S(1)}, u32[]{:S(2)}, u32[]{:S(2)}) collective-permute-start(bf16[192,2048]{1,0:T(8,128)(2,1)S(1)} %get-tuple-element.10), channel_id=1, source_target_pairs={{0,2},{1,3},{6,4},{7,5},{8,10},{9,11},{14,12},{15,13},{16,18},{17,... | collective-permute-start | bytes 2359304 | tf_op jit(solution)/shard_map/ppermute | solution.py:82
  184.9 32.9 %collective-permute-start.17 = (bf16[192,2048]{1,0:T(8,128)(2,1)S(1)}, bf16[192,2048]{1,0:T(8,128)(2,1)S(1)}, u32[]{:S(2)}, u32[]{:S(2)}) collective-permute-start(bf16[192,2048]{1,0:T(8,128)(2,1)S(1)} %get-tuple-element.8), channel_id=1, source_target_pairs={{0,2},{1,3},{6,4},{7,5},{8,10},{9,11},{14,12},{15,13},{16,18},{17,... | collective-permute-start | bytes 2359304 | tf_op jit(solution)/shard_map/ppermute | solution.py:82
  186.5 33.6 %collective-permute-start.9 = (bf16[192,2048]{1,0:T(8,128)(2,1)S(1)}, bf16[192,2048]{1,0:T(8,128)(2,1)S(1)}, u32[]{:S(2)}, u32[]{:S(2)}) collective-permute-start(bf16[192,2048]{1,0:T(8,128)(2,1)S(1)} %add_convert_fusion.2), channel_id=1, source_target_pairs={{2,4},{3,5},{4,2},{5,3},{10,12},{11,13},{12,10},{13,11},{18,20},{1... | collective-permute-start | bytes 2359304 | tf_op jit(solution)/shard_map/ppermute | solution.py:82
  217.8 47.0 %collective-permute-start.24 = (bf16[8,512,256]{2,1,0:T(8,128)(2,1)}, bf16[8,512,256]{2,1,0:T(8,128)(2,1)}, u32[]{:S(2)}, u32[]{:S(2)}) collective-permute-start(bf16[8,512,256]{2,1,0:T(8,128)(2,1)} %bitcast.7), channel_id=1, source_target_pairs={{0,16},{16,0},{1,17},{17,1},{2,18},{18,2},{3,19},{19,3},{4,20},{20... | collective-permute-start | bytes 6291464 | tf_op jit(solution)/shard_map/ppermute | solution.py:138
  219.5 23.6 %collective-permute-start.2 = (bf16[192,2048]{1,0:T(8,128)(2,1)S(1)}, bf16[192,2048]{1,0:T(8,128)(2,1)}, u32[]{:S(2)}, u32[]{:S(2)}) collective-permute-start(bf16[192,2048]{1,0:T(8,128)(2,1)S(1)} %fusion.80), channel_id=1, source_target_pairs={{0,1},{1,0},{2,3},{3,2},{4,5},{5,4},{6,7},{7,6},{8,9},{9,8},{10,11... | collective-permute-start | bytes 2359304 | tf_op jit(solution)/shard_map/ppermute | solution.py:82
  220.1 15.3 %collective-permute-start.18 = (bf16[192,2048]{1,0:T(8,128)(2,1)S(1)}, bf16[192,2048]{1,0:T(8,128)(2,1)S(1)}, u32[]{:S(2)}, u32[]{:S(2)}) collective-permute-start(bf16[192,2048]{1,0:T(8,128)(2,1)S(1)} %add_convert_fusion), channel_id=1, source_target_pairs={{2,4},{3,5},{4,2},{5,3},{10,12},{11,13},{12,10},{13,11},{18,20},{1... | collective-permute-start | bytes 2359304 | tf_op jit(solution)/shard_map/ppermute | solution.py:82
  227.0 17.9 %collective-permute-start.5 = (bf16[192,2048]{1,0:T(8,128)(2,1)S(1)}, bf16[192,2048]{1,0:T(8,128)(2,1)}, u32[]{:S(2)}, u32[]{:S(2)}) collective-permute-start(bf16[192,2048]{1,0:T(8,128)(2,1)S(1)} %add_convert_fusion.3), channel_id=1, source_target_pairs={{2,4},{3,5},{4,2},{5,3},{10,12},{11,13},{12,10},{13,11},{18,20},{1... | collective-permute-start | bytes 2359304 | tf_op jit(solution)/shard_map/ppermute | solution.py:82
  228.5 33.8 %collective-permute-start.10 = (bf16[192,2048]{1,0:T(8,128)(2,1)}, bf16[192,2048]{1,0:T(8,128)(2,1)}, u32[]{:S(2)}, u32[]{:S(2)}) collective-permute-start(bf16[192,2048]{1,0:T(8,128)(2,1)} %fusion.107), channel_id=1, source_target_pairs={{0,2},{1,3},{2,0},{3,1},{4,6},{5,7},{6,4},{7,5},{8,10},{9,11},{10,... | collective-permute-start | bytes 2359304 | tf_op jit(solution)/shard_map/ppermute | solution.py:82
  235.4 36.1 %collective-permute-start.11 = (bf16[192,2048]{1,0:T(8,128)(2,1)}, bf16[192,2048]{1,0:T(8,128)(2,1)}, u32[]{:S(2)}, u32[]{:S(2)}) collective-permute-start(bf16[192,2048]{1,0:T(8,128)(2,1)} %fusion.83), channel_id=1, source_target_pairs={{0,1},{1,0},{2,3},{3,2},{4,5},{5,4},{6,7},{7,6},{8,9},{9,8},{10,11... | collective-permute-start | bytes 2359304 | tf_op jit(solution)/shard_map/ppermute | solution.py:82
  243.1 28.9 %collective-permute-start.14 = (bf16[192,2048]{1,0:T(8,128)(2,1)S(1)}, bf16[192,2048]{1,0:T(8,128)(2,1)}, u32[]{:S(2)}, u32[]{:S(2)}) collective-permute-start(bf16[192,2048]{1,0:T(8,128)(2,1)S(1)} %add_convert_fusion.1), channel_id=1, source_target_pairs={{2,4},{3,5},{4,2},{5,3},{10,12},{11,13},{12,10},{13,11},{18,20},{1... | collective-permute-start | bytes 2359304 | tf_op jit(solution)/shard_map/ppermute | solution.py:82
  244.9 31.3 %collective-permute-start.19 = (bf16[192,2048]{1,0:T(8,128)(2,1)}, bf16[192,2048]{1,0:T(8,128)(2,1)}, u32[]{:S(2)}, u32[]{:S(2)}) collective-permute-start(bf16[192,2048]{1,0:T(8,128)(2,1)} %fusion.104), channel_id=1, source_target_pairs={{0,2},{1,3},{2,0},{3,1},{4,6},{5,7},{6,4},{7,5},{8,10},{9,11},{10,... | collective-permute-start | bytes 2359304 | tf_op jit(solution)/shard_map/ppermute | solution.py:82
  262.4 36.5 %collective-permute-start.25 = (bf16[8,512,256]{2,1,0:T(8,128)(2,1)}, bf16[8,512,256]{2,1,0:T(8,128)(2,1)S(1)}, u32[]{:S(2)}, u32[]{:S(2)}) collective-permute-start(bf16[8,512,256]{2,1,0:T(8,128)(2,1)} %bitcast.7), channel_id=1, source_target_pairs={{0,8},{8,0},{1,9},{9,1},{2,10},{10,2},{3,11},{11,3},{4,12},{12,4},... | collective-permute-start | bytes 6291464 | tf_op jit(solution)/shard_map/ppermute | solution.py:140
  264.8 34.3 %collective-permute-start.26 = (bf16[8,512,256]{2,1,0:T(8,128)(2,1)}, bf16[8,512,256]{2,1,0:T(8,128)(2,1)S(1)}, u32[]{:S(2)}, u32[]{:S(2)}) collective-permute-start(bf16[8,512,256]{2,1,0:T(8,128)(2,1)} %collective-permute-done.24), channel_id=1, source_target_pairs={{0,8},{8,0},{1,9},{9,1},{2,10},{10,2},{3,11},{11,3},{4,12},{12,4},... | collective-permute-start | bytes 6291464 | tf_op jit(solution)/shard_map/ppermute | solution.py:140
  303.1 57.8 %collective-permute-start.27 = (bf16[192,256]{1,0:T(8,128)(2,1)S(1)}, bf16[192,256]{1,0:T(8,128)(2,1)S(1)}, u32[]{:S(2)}, u32[]{:S(2)}) collective-permute-start(bf16[192,256]{1,0:T(8,128)(2,1)S(1)} %convolution_convert_fusion.7), channel_id=1, source_target_pairs={{0,1},{1,0},{2,3},{3,2},{4,5},{5,4},{6,7},{7,6},{8,9},{9,8},{10,11... | collective-permute-start | bytes 294920 | tf_op jit(solution)/shard_map/ppermute | solution.py:82
  304.7 41.1 %collective-permute-start.31 = (bf16[192,256]{1,0:T(8,128)(2,1)S(1)}, bf16[192,256]{1,0:T(8,128)(2,1)S(1)}, u32[]{:S(2)}, u32[]{:S(2)}) collective-permute-start(bf16[192,256]{1,0:T(8,128)(2,1)S(1)} %convolution_convert_fusion.5), channel_id=1, source_target_pairs={{0,1},{1,0},{2,3},{3,2},{4,5},{5,4},{6,7},{7,6},{8,9},{9,8},{10,11... | collective-permute-start | bytes 294920 | tf_op jit(solution)/shard_map/ppermute | solution.py:82
  306.7 56.8 %collective-permute-start.39 = (bf16[192,256]{1,0:T(8,128)(2,1)S(1)}, bf16[192,256]{1,0:T(8,128)(2,1)S(1)}, u32[]{:S(2)}, u32[]{:S(2)}) collective-permute-start(bf16[192,256]{1,0:T(8,128)(2,1)S(1)} %convolution_convert_fusion.3), channel_id=1, source_target_pairs={{0,1},{1,0},{2,3},{3,2},{4,5},{5,4},{6,7},{7,6},{8,9},{9,8},{10,11... | collective-permute-start | bytes 294920 | tf_op jit(solution)/shard_map/ppermute | solution.py:82
  314.9 32.7 %collective-permute-start.43 = (bf16[192,256]{1,0:T(8,128)(2,1)S(1)}, bf16[192,256]{1,0:T(8,128)(2,1)S(1)}, u32[]{:S(2)}, u32[]{:S(2)}) collective-permute-start(bf16[192,256]{1,0:T(8,128)(2,1)S(1)} %convolution_convert_fusion.1), channel_id=1, source_target_pairs={{0,1},{1,0},{2,3},{3,2},{4,5},{5,4},{6,7},{7,6},{8,9},{9,8},{10,11... | collective-permute-start | bytes 294920 | tf_op jit(solution)/shard_map/ppermute | solution.py:82
  345.8 15.2 %collective-permute-start.30 = (bf16[192,256]{1,0:T(8,128)(2,1)S(1)}, bf16[192,256]{1,0:T(8,128)(2,1)S(1)}, u32[]{:S(2)}, u32[]{:S(2)}) collective-permute-start(bf16[192,256]{1,0:T(8,128)(2,1)S(1)} %add_convert_fusion.7), channel_id=1, source_target_pairs={{2,4},{3,5},{4,2},{5,3},{10,12},{11,13},{12,10},{13,11},{18,20},{1... | collective-permute-start | bytes 294920 | tf_op jit(solution)/shard_map/ppermute | solution.py:82
  347.6 15.9 %collective-permute-start.42 = (bf16[192,256]{1,0:T(8,128)(2,1)S(1)}, bf16[192,256]{1,0:T(8,128)(2,1)S(1)}, u32[]{:S(2)}, u32[]{:S(2)}) collective-permute-start(bf16[192,256]{1,0:T(8,128)(2,1)S(1)} %add_convert_fusion.5), channel_id=1, source_target_pairs={{2,4},{3,5},{4,2},{5,3},{10,12},{11,13},{12,10},{13,11},{18,20},{1... | collective-permute-start | bytes 294920 | tf_op jit(solution)/shard_map/ppermute | solution.py:82
  348.3 14.8 %collective-permute-start.35 = (bf16[192,256]{1,0:T(8,128)(2,1)S(1)}, bf16[192,256]{1,0:T(8,128)(2,1)S(1)}, u32[]{:S(2)}, u32[]{:S(2)}) collective-permute-start(bf16[192,256]{1,0:T(8,128)(2,1)S(1)} %fusion.131), channel_id=1, source_target_pairs={{0,2},{1,3},{2,0},{3,1},{4,6},{5,7},{6,4},{7,5},{8,10},{9,11},{10,... | collective-permute-start | bytes 294920 | tf_op jit(solution)/shard_map/ppermute | solution.py:82
  (24 other events, 170.8 us)

commit v2 on v0

v2 whole, which is shorter than its diff:
```python
import functools
import math

import jax
import jax.numpy as jnp
from jax import lax
from jax.experimental import pallas as pl
from jax.experimental.pallas import tpu as pltpu
from jax.sharding import PartitionSpec as P

D = 16384
Q_HEADS = 128
KV_HEADS = 8
HEAD = 128
ATTEND_PARTS = 2
F32 = jnp.float32
BF16 = jnp.bfloat16
LOGIT = HEAD ** (-0.5) * math.log2(math.e)


def attend_kernel(parts, seq_ref, q_ref, ek_ref, ev_ref, k_ref, v_ref, out_ref):
    rows = q_ref.shape[0] // parts
    contract = (((1,), (1,)), ((), ()))
    shape = (rows, rows)
    hidden = lax.broadcasted_iota(jnp.int32, shape, 1) > lax.broadcasted_iota(
        jnp.int32, shape, 0
    )
    for part in range(parts):
        here = pl.ds(part * rows, rows)
        q = q_ref[here]
        early = lax.dot_general(q, ek_ref[...], contract, preferred_element_type=F32)
        early = jnp.where(seq_ref[0] > 0, early, -1e30)
        edge = lax.dot_general(q, k_ref[here], contract, preferred_element_type=F32)
        edge = jnp.where(hidden, -1e30, edge)
        pieces = [(early, ev_ref[...]), (edge, v_ref[here])]
        if part:
            before = pl.ds(0, part * rows)
            own = lax.dot_general(q, k_ref[before], contract, preferred_element_type=F32)
            pieces.append((own, v_ref[before]))
        peak = functools.reduce(
            jnp.maximum, [jnp.max(p, axis=1, keepdims=True) for p, _ in pieces]
        )
        total, context = 0.0, 0.0
        for scores, value in pieces:
            weights = jnp.exp2((scores - peak) * LOGIT)
            total += jnp.sum(weights, axis=1, keepdims=True)
            context += jnp.dot(weights.astype(BF16), value, preferred_element_type=F32)
        out_ref[here] = (context / total).astype(BF16)


def attend(queries, early_keys, early_values, own_keys, own_values, seq_index):
    rows = queries.shape[0]
    heads = queries.shape[1] // HEAD
    whole = pl.BlockSpec((rows, HEAD), lambda h, s: (0, 0))
    return pl.pallas_call(
        functools.partial(attend_kernel, ATTEND_PARTS),
        grid_spec=pltpu.PrefetchScalarGridSpec(
            num_scalar_prefetch=1,
            grid=(heads,),
            in_specs=[pl.BlockSpec((rows, HEAD), lambda h, s: (0, h))] + [whole] * 4,
            out_specs=pl.BlockSpec((rows, HEAD), lambda h, s: (0, h)),
        ),
        out_shape=jax.ShapeDtypeStruct((rows, heads * HEAD), BF16),
        compiler_params=pltpu.CompilerParams(vmem_limit_bytes=32 * 2**20),
        cost_estimate=pl.CostEstimate(flops=1000, bytes_accessed=1000, transcendentals=0),
    )(seq_index, queries, early_keys, early_values, own_keys, own_values)


def slab_kernel(at_ref, left_ref, right_ref, out_ref):
    out_ref[...] = jnp.dot(
        left_ref[...], right_ref[...], preferred_element_type=F32
    ).astype(out_ref.dtype)


def slab_dot(left, weight, at, width, dtype):
    rows, depth = left.shape
    tile = min(width, 512)
    tiles = width // tile
    return pl.pallas_call(
        slab_kernel,
        grid_spec=pltpu.PrefetchScalarGridSpec(
            num_scalar_prefetch=1,
            grid=(tiles,),
            in_specs=[
                pl.BlockSpec((rows, depth), lambda i, at: (0, 0)),
                pl.BlockSpec((depth, tile), lambda i, at: (0, at[0] * tiles + i)),
            ],
            out_specs=pl.BlockSpec((rows, tile), lambda i, at: (0, i)),
        ),
        out_shape=jax.ShapeDtypeStruct((rows, width), dtype),
        compiler_params=pltpu.CompilerParams(vmem_limit_bytes=32 * 2**20),
        cost_estimate=pl.CostEstimate(flops=1000, bytes_accessed=1000, transcendentals=0),
    )(jnp.reshape(at, (1,)), left, weight)


def together(*values):
    return lax.optimization_barrier(values)


def over(block, pairs):
    return lax.ppermute(block, "tensor", pairs)


def by_xor(block, step):
    return over(block, [(i, i ^ step) for i in range(8)])


def to_middle(block):
    return over(block, [(0, 2), (1, 3), (6, 4), (7, 5)])


def across(block):
    return over(block, [(2, 4), (3, 5), (4, 2), (5, 3)])


def place():
    t = lax.axis_index("tensor")
    z, y = t // 2, t % 2
    low = z < 2
    far = jnp.where(low, 3, 0)
    near = jnp.where(low, 2, 1)
    return z, y, (far, near, 6 - far - near - z, z)


def weight_over_y(weight):
    z, y, _ = place()
    depth, columns = weight.shape
    part = depth // 32
    quarter = lax.axis_index("groups") * 2 + lax.axis_index("seq")
    blocks = weight.reshape(4, 2, 4, part, columns)
    blocks = lax.dynamic_index_in_dim(blocks, quarter, 2, keepdims=False)
    kept = lax.dynamic_index_in_dim(blocks, y, 1, keepdims=False)
    sent = lax.dynamic_index_in_dim(blocks, 1 - y, 1, keepdims=False)
    return kept, by_xor(sent, 1)


def weight_over_z(kept, got):
    z, y, _ = place()
    first = y == 0
    pair = jnp.stack([jnp.where(first, kept, got), jnp.where(first, got, kept)], axis=1)
    pieces = []
    for step in range(4):
        piece = lax.dynamic_index_in_dim(pair, z ^ step, 0, keepdims=True)
        pieces.append(by_xor(piece, 2 * step) if step else piece)
    return pieces


def weight_in_order(pieces):
    z, _, _ = place()
    mine = jnp.zeros((4,) + pieces[0].shape[1:], pieces[0].dtype)
    for step, piece in enumerate(pieces):
        mine = lax.dynamic_update_slice_in_dim(mine, piece, z ^ step, 0)
    return mine.reshape((8,) + mine.shape[2:])


SWAP = [(0, 1), (1, 0)]


def weight_over_seq(mine, other):
    group, seq = lax.axis_index("groups"), lax.axis_index("seq")
    part = mine.shape[1]
    whole = jnp.zeros((8, 4 * part, mine.shape[2]), mine.dtype)
    beside = lax.ppermute((mine, other), "seq", SWAP)
    for block, g, s in (
        (mine, group, seq),
        (other, 1 - group, seq),
        (beside[0], group, 1 - seq),
        (beside[1], 1 - group, 1 - seq),
    ):
        whole = lax.dynamic_update_slice_in_dim(whole, block, (g * 2 + s) * part, 1)
    return whole


def kv_sum(scaled, weight):
    z, y, _ = place()
    high, low = z // 2, z % 2
    rows, depth = scaled.shape
    columns = weight.shape[2]
    blocks = weight.reshape(2, 2, 2, depth, columns)

    def terms(half):
        block = lax.dynamic_index_in_dim(blocks, half, 2, keepdims=False)
        return jnp.einsum("rk,hlkc->hlrc", scaled, block, preferred_element_type=F32)

    got = by_xor(terms(1 - y).astype(BF16), 1)
    block = terms(y) + got.astype(F32)
    for half, step in ((high, 4), (low, 2)):
        leaving = lax.dynamic_index_in_dim(block, 1 - half, 0, keepdims=False)
        staying = lax.dynamic_index_in_dim(block, half, 0, keepdims=False)
        block = staying + by_xor(leaving.astype(BF16), step).astype(F32)
    return block


def row_total(squares):
    for step in (1, 4, 2):
        squares = squares + by_xor(squares, step)
    return squares


def chained(residual, out_weight, gain, kv_weight, attend_all):
    z, y, order = place()
    width = residual.shape[1]
    wide = lambda block: block.astype(F32)
    kept, got = weight_over_y(kv_weight)
    context = attend_all()

    def sent_term(j):
        return slab_dot(context, out_weight, 2 * order[j] + 1 - y, width, BF16)

    def own_term(j):
        return slab_dot(context, out_weight, 2 * order[j] + y, width, F32)

    context, kept, got = together(context, kept, got)
    relay = weight_over_z(kept, got)
    leaving = sent_term(0)
    leaving, context = together(leaving, context)
    y_got = by_xor(leaving, 1)
    term, leaving = own_term(0), sent_term(1)
    y_got, term, leaving, context, *relay = together(y_got, term, leaving, context, *relay)
    relay = weight_in_order(relay)
    far = term + wide(y_got)
    y_got = by_xor(leaving, 1)
    far_got = to_middle(far.astype(BF16))
    term, leaving = own_term(1), sent_term(2)
    y_got, far_got, term, leaving, context, relay = together(
        y_got, far_got, term, leaving, context, relay
    )
    near = term + wide(y_got)
    y_got = by_xor(leaving, 1)
    far_got = across((far + wide(far_got)).astype(BF16))
    near_got = to_middle(near.astype(BF16))
    other = lax.ppermute(relay, "groups", SWAP)
    term, leaving, own = own_term(2), sent_term(3), own_term(3)
    y_got, far_got, near_got, term, leaving, own = together(
        y_got, far_got, near_got, term, leaving, own
    )
    last = term + wide(y_got) + wide(far_got)
    y_got = by_xor(leaving, 1)
    last_got = by_xor(last.astype(BF16), 2)
    near_got = across((near + wide(near_got)).astype(BF16))
    slab_weight = weight_over_seq(relay, other)
    y_got, last_got, near_got, own, slab_weight = together(
        y_got, last_got, near_got, own, slab_weight
    )
    attended = own + wide(y_got) + wide(near_got) + wide(last_got)
    stream = (wide(residual) + attended).astype(BF16)
    widened = wide(stream)
    total = row_total(jnp.sum(widened * widened, axis=1))
    inverse = lax.rsqrt(total / D + 1e-05)
    projected = kv_sum((widened * gain).astype(BF16), slab_weight)
    return stream, (projected * inverse[:, None]).astype(BF16)


def gathered(residual, out_weight, gain, kv_weight, attend_all):
    partial = jnp.dot(attend_all(), out_weight, preferred_element_type=F32)
    attended = lax.psum_scatter(
        partial.astype(BF16), "tensor", scatter_dimension=1, tiled=True
    ).astype(F32)
    stream = (residual.astype(F32) + attended).astype(BF16)
    widened = stream.astype(F32)
    total = lax.psum(jnp.sum(widened * widened, axis=1), "tensor")
    inverse = lax.rsqrt(total / D + 1e-05)
    scaled = (widened * gain).astype(BF16)
    everything = lax.all_gather(scaled, "tensor", axis=1, tiled=True)
    projected = jnp.dot(everything, kv_weight, preferred_element_type=F32)
    return stream, (projected * inverse[:, None]).astype(BF16)


def on_device(queries, keys, values, residual, out_weight, norm_gain, kv_weight):
    heads_here = queries.shape[1] // HEAD
    devices = lax.axis_size("tensor")
    tensor_rank = lax.axis_index("tensor")
    seq_index = lax.axis_index("seq")
    kv_group = tensor_rank * heads_here // (Q_HEADS // KV_HEADS)
    own_keys = lax.dynamic_slice_in_dim(keys, kv_group * HEAD, HEAD, 1)
    own_values = lax.dynamic_slice_in_dim(values, kv_group * HEAD, HEAD, 1)
    early_keys, early_values = lax.ppermute((own_keys, own_values), "seq", [(0, 1)])
    gain = norm_gain.astype(F32)[None, :]

    def attend_all():
        return attend(
            queries, early_keys, early_values, own_keys, own_values, seq_index.reshape(1)
        )

    summed = chained if devices == 8 else gathered
    return summed(residual, out_weight, gain, kv_weight, attend_all)


def solution(mesh):
    return jax.shard_map(
        on_device,
        mesh=mesh,
        in_specs=(
            P(("groups", "seq"), "tensor"),
            P(("groups", "seq"), None),
            P(("groups", "seq"), None),
            P(("groups", "seq"), "tensor"),
            P("tensor", None),
            P("tensor"),
            P(None, "tensor"),
        ),
        out_specs=(P(("groups", "seq"), "tensor"), P(("groups", "seq"), "tensor")),
        check_vma=False,
    )
```

time: 694 us -> 285 us (0.41)
  waiting for transfers between devices: 412 us -> 106 us
  Pallas kernels: 0 us -> 70.7 us
  local copies, waits for them, and re-layouts: 92.9 us -> 22.5 us
  matrix products: 76.4 us -> 7.27 us
  blocking collectives: 50.9 us -> 0 us
  starting transfers between devices: 16.5 us -> 53.3 us
  between operations: 14.2 us -> 1.05 us
    all_to_all x2 -> x0, waiting for transfers between devices: 271 us -> none  [the longest x1 271 us: on_device(): lax.all_to_all(packed.reshape(tok_rows, D), 'tensor', split_axis=1, conca...]
    all_gather x1 -> x0, waiting for transfers between devices: 141 us -> none  [on_device(): piece_packed = lax.all_gather(norm_packed, 'tensor', axis=1, tiled=True)]
    ppermute x2 -> x24, waiting for transfers between devices: 0.01 us -> 106 us  [the longest x19 101 us: over(): return lax.ppermute(block, 'tensor', pairs)]
    dot_general x1 -> x0, local copies, waits for them, and re-layouts: 86.6 us -> none  [on_device(): jnp.dot(context, out_weight, preferred_element_type=jnp.float32)]
    pallas_call x0 -> x9, Pallas kernels: none -> 70.7 us  [the longest x8 55 us: slab_dot(): pl.pallas_call(slab_kernel, grid_spec=pltpu.PrefetchScalarGridSpec(num_sc...]
    dot_general x3 -> x2, matrix products: 66.2 us -> 7.27 us  [terms(): jnp.einsum('rk,hlkc->hlrc', scaled, block, preferred_element_type=F32)]
    ppermute x2 -> x24, starting transfers between devices: 3.65 us -> 53.3 us  [the longest x19 49.1 us: over(): return lax.ppermute(block, 'tensor', pairs)]
    all_gather x1 -> x0, blocking collectives: 31.4 us -> none  [on_device(): lax.all_gather(norm_scales.astype(jnp.bfloat16), 'tensor', axis=1, tiled=...]
  transfers between devices with their start and end apart: 5 -> 24, of which waited for: 2 -> 14; matrix products, arithmetic and copies ran while one was open for 17% -> 13% of each run, Pallas kernels for 0% -> 23%
where the time goes in v2:
time: 285 us; the launch traced here: 284 us
  waiting for transfers between devices  106 us (37%)
  Pallas kernels  70.7 us (25%)
  starting transfers between devices  53.3 us (19%)
  other arithmetic  22.7 us (8%)
  local copies, waits for them, and re-layouts  22.5 us (8%)
  matrix products  7.27 us (3%)
    ppermute x19, waiting for transfers between devices, over(): return lax.ppermute(block, 'tensor', pairs)  101 us
    pallas_call x8, Pallas kernels, slab_dot(): pl.pallas_call(slab_kernel, grid_spec=pltpu.PrefetchScalarGridSpec(num_sc...  55 us
    ppermute x19, starting transfers between devices, over(): return lax.ppermute(block, 'tensor', pairs)  49.1 us
    pallas_call x1, Pallas kernels, attend(): pl.pallas_call(functools.partial(attend_kernel, ATTEND_PARTS), grid_spec=...  15.7 us
    dynamic_update_slice x4, local copies, waits for them, and re-layouts, weight_over_seq(): whole = lax.dynamic_update_slice_in_dim(whole, block, (g * 2 + s) * part, 1)  7.51 us
    dot_general x2, matrix products, terms(): jnp.einsum('rk,hlkc->hlrc', scaled, block, preferred_element_type=F32)  7.27 us
    dynamic_update_slice x4, local copies, waits for them, and re-layouts, weight_in_order(): mine = lax.dynamic_update_slice_in_dim(mine, piece, z ^ step, 0)  6.77 us
  transfers between devices with their start and end apart: 24, of which 14 were waited for; matrix products, arithmetic and copies ran while one was open for 13% of the time, Pallas kernels for 23%

profile of v2, /device:TPU:0, one launch (start us, length us, event | category | flops | bytes accessed | tf_op | source)
XLA Modules:
  0.0 283.9 jit_solution(6539546055636979342)
XLA Ops:
  0.7 3.2 %dynamic-slice_bitcast_fusion = (bf16[4,512,256]{2,1,0:T(8,128)(2,1)}, bf16[4,512,256]{2,1,0:T(8,128)(2,1)}) fusion(bf16[4,2,4,512,256]{4,3,2,1,0:T(8,128)(2,1)} %bitcast.64, s32[]{:T(128)S(6)} %select_n.126, s32[]{:T(128)S(6)} %select_n.124, s32[]{:T(128)S(6)} %select_n.122), kind=kLoop, calls=%fused_computation.32 | loop fusion | bytes 4194316 | tf_op jit(solution)/shard_map/jit(dynamic_index_in_dim)/squeeze | solution.py:133
  3.9 3.0 %collective-permute-start.2 = (bf16[4,512,256]{2,1,0:T(8,128)(2,1)}, bf16[4,512,256]{2,1,0:T(8,128)(2,1)}, u32[]{:S(2)}, u32[]{:S(2)}) collective-permute-start(bf16[4,512,256]{2,1,0:T(8,128)(2,1)} %get-tuple-element.68), channel_id=1, source_target_pairs={{0,1},{1,0},{2,3},{3,2},{4,5},{5,4},{6,7},{7,6},{8,9},{9,8},{10,11... | collective-permute-start | bytes 3145736 | tf_op jit(solution)/shard_map/ppermute | solution.py:101
  11.5 15.7 %shard_map.86.left_ref = bf16[384,2048]{1,0:T(8,128)(2,1)S(1)} custom-call(s32[1]{0:T(128)} %bitcast.1.seq_ref, bf16[384,2048]{1,0:T(8,128)(2,1)S(1)} %copy-done.8, bf16[384,128]{1,0:T(8,128)(2,1)S(1)} %collective-permute-done.ek_ref, bf16[384,128]{1,0:T(8,128)(2,1)S(1)} %collective-permute-done.1.ev_ref, ...), custom_call_target="tpu_custom_call" | custom-call | flops 1000 | bytes 1000 | tf_op jit(solution)/shard_map/pallas_call | solution.py:55
  27.1 3.2 %collective-permute-done.2 = bf16[4,512,256]{2,1,0:T(8,128)(2,1)} collective-permute-done((bf16[4,512,256]{2,1,0:T(8,128)(2,1)}, bf16[4,512,256]{2,1,0:T(8,128)(2,1)}, u32[]{:S(2)}, u32[]{:S(2)}) %collective-permute-start.2) | collective-permute-done | bytes 1048608 | tf_op jit(solution)/shard_map/ppermute | solution.py:101
  30.3 6.3 %shard_map.87 = bf16[384,2048]{1,0:T(8,128)(2,1)S(1)} custom-call(s32[1]{0:T(128)} %bitcast.at_ref, bf16[384,2048]{1,0:T(8,128)(2,1)S(1)} %shard_map.86.left_ref, bf16[2048,16384]{1,0:T(8,128)(2,1)} %right_ref.15), custom_call_target="tpu_custom_call" | custom-call | flops 1000 | bytes 1000 | tf_op jit(solution)/shard_map/pallas_call | solution.py:79
  46.0 6.4 %shard_map.88 = f32[384,2048]{1,0:T(8,128)S(1)} custom-call(s32[1]{0:T(128)} %bitcast.5.at_ref, bf16[384,2048]{1,0:T(8,128)(2,1)S(1)} %shard_map.86.left_ref, bf16[2048,16384]{1,0:T(8,128)(2,1)} %right_ref.15), custom_call_target="tpu_custom_call" | custom-call | flops 1000 | bytes 1000 | tf_op jit(solution)/shard_map/pallas_call | solution.py:79
  52.4 8.4 %shard_map.89 = bf16[384,2048]{1,0:T(8,128)(2,1)} custom-call(s32[1]{0:T(128)} %bitcast.6.at_ref, bf16[384,2048]{1,0:T(8,128)(2,1)S(1)} %shard_map.86.left_ref, bf16[2048,16384]{1,0:T(8,128)(2,1)} %right_ref.15), custom_call_target="tpu_custom_call" | custom-call | flops 1000 | bytes 1000 | tf_op jit(solution)/shard_map/pallas_call | solution.py:79
  60.8 3.5 %collective-permute-done.4 = bf16[1,2,512,256]{3,2,1,0:T(8,128)(2,1)} collective-permute-done((bf16[1,2,512,256]{3,2,1,0:T(8,128)(2,1)}, bf16[1,2,512,256]{3,2,1,0:T(8,128)(2,1)}, u32[]{:S(2)}, u32[]{:S(2)}) %collective-permute-start.4) | collective-permute-done | bytes 524320 | tf_op jit(solution)/shard_map/ppermute | solution.py:101
  64.3 17.4 %collective-permute-done.5 = bf16[1,2,512,256]{3,2,1,0:T(8,128)(2,1)} collective-permute-done((bf16[1,2,512,256]{3,2,1,0:T(8,128)(2,1)}, bf16[1,2,512,256]{3,2,1,0:T(8,128)(2,1)}, u32[]{:S(2)}, u32[]{:S(2)}) %collective-permute-start.5) | collective-permute-done | bytes 524320 | tf_op jit(solution)/shard_map/ppermute | solution.py:101
  82.2 3.1 %fusion.8 = bf16[384,2048]{1,0:T(8,128)(2,1)} fusion(f32[384,2048]{1,0:T(8,128)S(1)} %shard_map.88, bf16[384,2048]{1,0:T(8,128)(2,1)} %collective-permute-done.3), kind=kLoop, calls=%fused_computation.24 | loop fusion | flops 2359296 | bytes 6291456 | tf_op jit(solution)/shard_map/convert_element_type | solution.py:223
  85.3 12.3 %collective-permute-start.8 = (bf16[384,2048]{1,0:T(8,128)(2,1)}, bf16[384,2048]{1,0:T(8,128)(2,1)}, u32[]{:S(2)}, u32[]{:S(2)}) collective-permute-start(bf16[384,2048]{1,0:T(8,128)(2,1)} %fusion.8), channel_id=1, source_target_pairs={{0,2},{1,3},{6,4},{7,5},{8,10},{9,11},{14,12},{15,13},{16,18},{17,... | collective-permute-start | bytes 4718600 | tf_op jit(solution)/shard_map/ppermute | solution.py:101
  97.6 6.4 %shard_map.90 = f32[384,2048]{1,0:T(8,128)S(1)} custom-call(s32[1]{0:T(128)} %bitcast.10.at_ref, bf16[384,2048]{1,0:T(8,128)(2,1)S(1)} %shard_map.86.left_ref, bf16[2048,16384]{1,0:T(8,128)(2,1)} %right_ref.15), custom_call_target="tpu_custom_call" | custom-call | flops 1000 | bytes 1000 | tf_op jit(solution)/shard_map/pallas_call | solution.py:79
  104.1 8.4 %shard_map.91 = bf16[384,2048]{1,0:T(8,128)(2,1)} custom-call(s32[1]{0:T(128)} %bitcast.11.at_ref, bf16[384,2048]{1,0:T(8,128)(2,1)S(1)} %shard_map.86.left_ref, bf16[2048,16384]{1,0:T(8,128)(2,1)} %right_ref.15), custom_call_target="tpu_custom_call" | custom-call | flops 1000 | bytes 1000 | tf_op jit(solution)/shard_map/pallas_call | solution.py:79
  120.7 7.1 %collective-permute-done.8 = bf16[384,2048]{1,0:T(8,128)(2,1)} collective-permute-done((bf16[384,2048]{1,0:T(8,128)(2,1)}, bf16[384,2048]{1,0:T(8,128)(2,1)}, u32[]{:S(2)}, u32[]{:S(2)}) %collective-permute-start.8) | collective-permute-done | bytes 1572896 | tf_op jit(solution)/shard_map/ppermute | solution.py:101
  129.3 3.8 %add_convert_fusion.3 = bf16[384,2048]{1,0:T(8,128)(2,1)} fusion(bf16[384,2048]{1,0:T(8,128)(2,1)} %collective-permute-done.8, f32[384,2048]{1,0:T(8,128)S(1)} %copy-done.5, bf16[384,2048]{1,0:T(8,128)(2,1)} %collective-permute-done.3), kind=kLoop, calls=%fused_computation.14 | loop fusion | flops 3932160 | bytes 7864320 | tf_op jit(solution)/shard_map/convert_element_type | solution.py:230
  138.2 7.3 %collective-permute-start.11 = (bf16[384,2048]{1,0:T(8,128)(2,1)}, bf16[384,2048]{1,0:T(8,128)(2,1)}, u32[]{:S(2)}, u32[]{:S(2)}) collective-permute-start(bf16[384,2048]{1,0:T(8,128)(2,1)} %fusion.9), channel_id=1, source_target_pairs={{0,2},{1,3},{6,4},{7,5},{8,10},{9,11},{14,12},{15,13},{16,18},{17,... | collective-permute-start | bytes 4718600 | tf_op jit(solution)/shard_map/ppermute | solution.py:101
  145.4 6.4 %shard_map.92 = f32[384,2048]{1,0:T(8,128)S(1)} custom-call(s32[1]{0:T(128)} %bitcast.13.at_ref, bf16[384,2048]{1,0:T(8,128)(2,1)S(1)} %shard_map.86.left_ref, bf16[2048,16384]{1,0:T(8,128)(2,1)} %right_ref.15), custom_call_target="tpu_custom_call" | custom-call | flops 1000 | bytes 1000 | tf_op jit(solution)/shard_map/pallas_call | solution.py:79
  151.9 6.4 %shard_map.93 = bf16[384,2048]{1,0:T(8,128)(2,1)S(1)} custom-call(s32[1]{0:T(128)} %bitcast.14.at_ref, bf16[384,2048]{1,0:T(8,128)(2,1)S(1)} %shard_map.86.left_ref, bf16[2048,16384]{1,0:T(8,128)(2,1)} %right_ref.15), custom_call_target="tpu_custom_call" | custom-call | flops 1000 | bytes 1000 | tf_op jit(solution)/shard_map/pallas_call | solution.py:79
  158.2 6.4 %shard_map.94 = f32[384,2048]{1,0:T(8,128)S(1)} custom-call(s32[1]{0:T(128)} %bitcast.15.at_ref, bf16[384,2048]{1,0:T(8,128)(2,1)S(1)} %shard_map.86.left_ref, bf16[2048,16384]{1,0:T(8,128)(2,1)} %right_ref.15), custom_call_target="tpu_custom_call" | custom-call | flops 1000 | bytes 1000 | tf_op jit(solution)/shard_map/pallas_call | solution.py:79
  164.7 9.2 %collective-permute-done.11 = bf16[384,2048]{1,0:T(8,128)(2,1)} collective-permute-done((bf16[384,2048]{1,0:T(8,128)(2,1)}, bf16[384,2048]{1,0:T(8,128)(2,1)}, u32[]{:S(2)}, u32[]{:S(2)}) %collective-permute-start.11) | collective-permute-done | bytes 1572896 | tf_op jit(solution)/shard_map/ppermute | solution.py:101
  174.4 4.5 %collective-permute-done.15 = bf16[8,512,256]{2,1,0:T(8,128)(2,1)} collective-permute-done((bf16[8,512,256]{2,1,0:T(8,128)(2,1)}, bf16[8,512,256]{2,1,0:T(8,128)(2,1)}, u32[]{:S(2)}, u32[]{:S(2)}) %collective-permute-start.15) | collective-permute-done | bytes 2097184 | tf_op jit(solution)/shard_map/ppermute | solution.py:232
  181.5 4.0 %collective-permute-start.13 = (bf16[384,2048]{1,0:T(8,128)(2,1)S(1)}, bf16[384,2048]{1,0:T(8,128)(2,1)}, u32[]{:S(2)}, u32[]{:S(2)}) collective-permute-start(bf16[384,2048]{1,0:T(8,128)(2,1)S(1)} %add_convert_fusion.2), channel_id=1, source_target_pairs={{0,2},{1,3},{2,0},{3,1},{4,6},{5,7},{6,4},{7,5},{8,10},{9,11},{10,... | collective-permute-start | bytes 4718600 | tf_op jit(solution)/shard_map/ppermute | solution.py:101
  185.5 3.3 %add_convert_fusion.1 = bf16[384,2048]{1,0:T(8,128)(2,1)} fusion(bf16[384,2048]{1,0:T(8,128)(2,1)} %collective-permute-done.11, f32[384,2048]{1,0:T(8,128)S(1)} %copy-done.3, bf16[384,2048]{1,0:T(8,128)(2,1)S(1)} %copy-done.11), kind=kLoop, calls=%fused_computation.11 | loop fusion | flops 3932160 | bytes 7864320 | tf_op jit(solution)/shard_map/convert_element_type | solution.py:240
  198.8 6.0 %collective-permute-done.12 = bf16[384,2048]{1,0:T(8,128)(2,1)} collective-permute-done((bf16[384,2048]{1,0:T(8,128)(2,1)S(1)}, bf16[384,2048]{1,0:T(8,128)(2,1)}, u32[]{:S(2)}, u32[]{:S(2)}) %collective-permute-start.12) | collective-permute-done | bytes 1572896 | tf_op jit(solution)/shard_map/ppermute | solution.py:101
  204.8 15.9 %collective-permute-done.13 = bf16[384,2048]{1,0:T(8,128)(2,1)} collective-permute-done((bf16[384,2048]{1,0:T(8,128)(2,1)S(1)}, bf16[384,2048]{1,0:T(8,128)(2,1)}, u32[]{:S(2)}, u32[]{:S(2)}) %collective-permute-start.13) | collective-permute-done | bytes 1572896 | tf_op jit(solution)/shard_map/ppermute | solution.py:101
  220.7 3.7 %fusion.7 = (f32[384]{0:T(512)S(1)}, bf16[384,2048]{1,0:T(8,128)(2,1)S(1)}) fusion(bf16[384,2048]{1,0:T(8,128)(2,1)} %collective-permute-done.13, bf16[384,2048]{1,0:T(8,128)(2,1)} %collective-permute-done.14, f32[384,2048]{1,0:T(8,128)S(1)} %copy-done.7, bf16[384,2048]{1,0:T(8,128)(2,1)} %collective-permute-done.12, bf16[384,2048]{1,0:T(8,128)(2,1)S(1)} %copy-done.13), kind=kLoop, calls=%fused_computation.9 | loop fusion | flops 9436800 | bytes 11011584 | tf_op jit(solution)/shard_map/reduce_sum | solution.py:248
  227.4 19.0 %collective-permute-done.18 = bf16[2,2,384,256]{2,3,1,0:T(8,128)(2,1)} collective-permute-done((bf16[2,2,384,256]{2,3,1,0:T(8,128)(2,1)S(1)}, bf16[2,2,384,256]{2,3,1,0:T(8,128)(2,1)}, u32[]{:S(2)}, u32[]{:S(2)}) %collective-permute-start.18) | collective-permute-done | bytes 786464 | tf_op jit(solution)/shard_map/ppermute | solution.py:101
  246.4 4.9 %bitcast_add_fusion = f32[2,2,384,256]{2,3,1,0:T(8,128)S(1)} fusion(bf16[2,2,384,256]{2,3,1,0:T(8,128)(2,1)} %collective-permute-done.18, bf16[2,2,2,2048,256]{4,3,2,1,0:T(8,128)(2,1)} %bitcast.63, s32[]{:T(128)S(6)} %select_n.121, bf16[384,2048]{1,0:T(8,128)(2,1)S(1)} %get-tuple-element.67, f32[2048]{0:T(1024)S(1)} %convert_element_type.104), kind=kOutput, calls=%fused_computation.27 | convolution fusion | flops 1613758464 | bytes 8134660 | tf_op jit(solution)/shard_map/rk,hlkc->hlrc/dot_general | solution.py:183
  252.5 6.9 %collective-permute-start.19 = (bf16[2,384,256]{1,2,0:T(8,128)(2,1)S(1)}, bf16[2,384,256]{1,2,0:T(8,128)(2,1)S(1)}, u32[]{:S(2)}, u32[]{:S(2)}) collective-permute-start(bf16[2,384,256]{1,2,0:T(8,128)(2,1)S(1)} %fusion.25), channel_id=1, source_target_pairs={{0,4},{1,5},{2,6},{3,7},{4,0},{5,1},{6,2},{7,3},{8,12},{9,13},{10,... | collective-permute-start | bytes 1179656 | tf_op jit(solution)/shard_map/ppermute | solution.py:101
  259.9 3.1 %collective-permute-done.21 = f32[384]{0:T(512)S(1)} collective-permute-done((f32[384]{0:T(512)S(1)}, f32[384]{0:T(512)S(1)}, u32[]{:S(2)}, u32[]{:S(2)}) %collective-permute-start.21) | collective-permute-done | bytes 1568 | tf_op jit(solution)/shard_map/ppermute | solution.py:101
  263.1 13.0 %collective-permute-done.22 = f32[384]{0:T(512)S(1)} collective-permute-done((f32[384]{0:T(512)S(1)}, f32[384]{0:T(512)S(1)}, u32[]{:S(2)}, u32[]{:S(2)}) %collective-permute-start.22) | collective-permute-done | bytes 1568 | tf_op jit(solution)/shard_map/ppermute | solution.py:101
  279.7 3.3 %collective-permute-done.20 = bf16[384,256]{0,1:T(8,128)(2,1)S(1)} collective-permute-done((bf16[384,256]{0,1:T(8,128)(2,1)S(1)}, bf16[384,256]{0,1:T(8,128)(2,1)S(1)}, u32[]{:S(2)}, u32[]{:S(2)}) %collective-permute-start.20) | collective-permute-done | bytes 196640 | tf_op jit(solution)/shard_map/ppermute | solution.py:101
  (91 shorter events, 51.6 us)
Async XLA Ops:
  3.9 26.4 %collective-permute-start.2 = (bf16[4,512,256]{2,1,0:T(8,128)(2,1)}, bf16[4,512,256]{2,1,0:T(8,128)(2,1)}, u32[]{:S(2)}, u32[]{:S(2)}) collective-permute-start(bf16[4,512,256]{2,1,0:T(8,128)(2,1)} %get-tuple-element.68), channel_id=1, source_target_pairs={{0,1},{1,0},{2,3},{3,2},{4,5},{5,4},{6,7},{7,6},{8,9},{9,8},{10,11... | collective-permute-start | bytes 3145736 | tf_op jit(solution)/shard_map/ppermute | solution.py:101
  6.9 3.7 %collective-permute-start = (bf16[384,128]{1,0:T(8,128)(2,1)S(1)}, bf16[384,128]{1,0:T(8,128)(2,1)S(1)}, u32[]{:S(2)}, u32[]{:S(2)}) collective-permute-start(bf16[384,128]{1,0:T(8,128)(2,1)S(1)} %constant_dynamic-slice_fusion.1.k_ref), channel_id=1, source_target_pairs={{0,8},{1,9},{2,10},{3,11},{4,12},{5,13},{6,14},{7,15},{16,24},{17,... | collective-permute-start | bytes 294920 | tf_op jit(solution)/shard_map/ppermute | solution.py:277
  9.3 2.2 collective-permute-start.1
  36.7 45.1 %collective-permute-start.3 = (bf16[384,2048]{1,0:T(8,128)(2,1)S(1)}, bf16[384,2048]{1,0:T(8,128)(2,1)}, u32[]{:S(2)}, u32[]{:S(2)}) collective-permute-start(bf16[384,2048]{1,0:T(8,128)(2,1)S(1)} %shard_map.87), channel_id=1, source_target_pairs={{0,1},{1,0},{2,3},{3,2},{4,5},{5,4},{6,7},{7,6},{8,9},{9,8},{10,11... | collective-permute-start | bytes 4718600 | tf_op jit(solution)/shard_map/ppermute | solution.py:101
  41.6 22.7 %collective-permute-start.4 = (bf16[1,2,512,256]{3,2,1,0:T(8,128)(2,1)}, bf16[1,2,512,256]{3,2,1,0:T(8,128)(2,1)}, u32[]{:S(2)}, u32[]{:S(2)}) collective-permute-start(bf16[1,2,512,256]{3,2,1,0:T(8,128)(2,1)} %get-tuple-element.72), channel_id=1, source_target_pairs={{0,2},{1,3},{2,0},{3,1},{4,6},{5,7},{6,4},{7,5},{8,10},{9,11},{10,... | collective-permute-start | bytes 1572872 | tf_op jit(solution)/shard_map/ppermute | solution.py:101
  43.1 38.5 %collective-permute-start.5 = (bf16[1,2,512,256]{3,2,1,0:T(8,128)(2,1)}, bf16[1,2,512,256]{3,2,1,0:T(8,128)(2,1)}, u32[]{:S(2)}, u32[]{:S(2)}) collective-permute-start(bf16[1,2,512,256]{3,2,1,0:T(8,128)(2,1)} %get-tuple-element.73), channel_id=1, source_target_pairs={{0,4},{1,5},{2,6},{3,7},{4,0},{5,1},{6,2},{7,3},{8,12},{9,13},{10,... | collective-permute-start | bytes 1572872 | tf_op jit(solution)/shard_map/ppermute | solution.py:101
  45.7 36.0 %collective-permute-start.6 = (bf16[1,2,512,256]{3,2,1,0:T(8,128)(2,1)}, bf16[1,2,512,256]{3,2,1,0:T(8,128)(2,1)}, u32[]{:S(2)}, u32[]{:S(2)}) collective-permute-start(bf16[1,2,512,256]{3,2,1,0:T(8,128)(2,1)} %get-tuple-element.70), channel_id=1, source_target_pairs={{0,6},{1,7},{2,4},{3,5},{4,2},{5,3},{6,0},{7,1},{8,14},{9,15},{10,... | collective-permute-start | bytes 1572872 | tf_op jit(solution)/shard_map/ppermute | solution.py:101
  52.4 29.8 %copy-start.4 = (f32[384,2048]{1,0:T(8,128)}, f32[384,2048]{1,0:T(8,128)S(1)}, u32[]{:S(2)}) copy-start(f32[384,2048]{1,0:T(8,128)S(1)} %shard_map.88) | copy-start | bytes 9437188
  81.7 39.0 %collective-permute-start.7 = (bf16[384,2048]{1,0:T(8,128)(2,1)}, bf16[384,2048]{1,0:T(8,128)(2,1)S(1)}, u32[]{:S(2)}, u32[]{:S(2)}) collective-permute-start(bf16[384,2048]{1,0:T(8,128)(2,1)} %shard_map.89), channel_id=1, source_target_pairs={{0,1},{1,0},{2,3},{3,2},{4,5},{5,4},{6,7},{7,6},{8,9},{9,8},{10,11... | collective-permute-start | bytes 4718600 | tf_op jit(solution)/shard_map/ppermute | solution.py:101
  85.3 42.5 %collective-permute-start.8 = (bf16[384,2048]{1,0:T(8,128)(2,1)}, bf16[384,2048]{1,0:T(8,128)(2,1)}, u32[]{:S(2)}, u32[]{:S(2)}) collective-permute-start(bf16[384,2048]{1,0:T(8,128)(2,1)} %fusion.8), channel_id=1, source_target_pairs={{0,2},{1,3},{6,4},{7,5},{8,10},{9,11},{14,12},{15,13},{16,18},{17,... | collective-permute-start | bytes 4718600 | tf_op jit(solution)/shard_map/ppermute | solution.py:101
  104.1 32.4 %copy-start.2 = (f32[384,2048]{1,0:T(8,128)}, f32[384,2048]{1,0:T(8,128)S(1)}, u32[]{:S(2)}) copy-start(f32[384,2048]{1,0:T(8,128)S(1)} %shard_map.90) | copy-start | bytes 9437188
  127.8 36.9 %collective-permute-start.9 = (bf16[384,2048]{1,0:T(8,128)(2,1)}, bf16[384,2048]{1,0:T(8,128)(2,1)}, u32[]{:S(2)}, u32[]{:S(2)}) collective-permute-start(bf16[384,2048]{1,0:T(8,128)(2,1)} %shard_map.91), channel_id=1, source_target_pairs={{0,1},{1,0},{2,3},{3,2},{4,5},{5,4},{6,7},{7,6},{8,9},{9,8},{10,11... | collective-permute-start | bytes 4718600 | tf_op jit(solution)/shard_map/ppermute | solution.py:101
  133.1 31.6 %collective-permute-start.10 = (bf16[384,2048]{1,0:T(8,128)(2,1)}, bf16[384,2048]{1,0:T(8,128)(2,1)}, u32[]{:S(2)}, u32[]{:S(2)}) collective-permute-start(bf16[384,2048]{1,0:T(8,128)(2,1)} %add_convert_fusion.3), channel_id=1, source_target_pairs={{2,4},{3,5},{4,2},{5,3},{10,12},{11,13},{12,10},{13,11},{18,20},{1... | collective-permute-start | bytes 4718600 | tf_op jit(solution)/shard_map/ppermute | solution.py:101
  134.9 43.9 %collective-permute-start.15 = (bf16[8,512,256]{2,1,0:T(8,128)(2,1)}, bf16[8,512,256]{2,1,0:T(8,128)(2,1)}, u32[]{:S(2)}, u32[]{:S(2)}) collective-permute-start(bf16[8,512,256]{2,1,0:T(8,128)(2,1)} %bitcast.12), channel_id=1, source_target_pairs={{0,16},{16,0},{1,17},{17,1},{2,18},{18,2},{3,19},{19,3},{4,20},{20... | collective-permute-start | bytes 6291464 | tf_op jit(solution)/shard_map/ppermute | solution.py:232
  138.2 35.7 %collective-permute-start.11 = (bf16[384,2048]{1,0:T(8,128)(2,1)}, bf16[384,2048]{1,0:T(8,128)(2,1)}, u32[]{:S(2)}, u32[]{:S(2)}) collective-permute-start(bf16[384,2048]{1,0:T(8,128)(2,1)} %fusion.9), channel_id=1, source_target_pairs={{0,2},{1,3},{6,4},{7,5},{8,10},{9,11},{14,12},{15,13},{16,18},{17,... | collective-permute-start | bytes 4718600 | tf_op jit(solution)/shard_map/ppermute | solution.py:101
  145.4 49.4 %collective-permute-start.16 = (bf16[8,512,256]{2,1,0:T(8,128)(2,1)}, bf16[8,512,256]{2,1,0:T(8,128)(2,1)}, u32[]{:S(2)}, u32[]{:S(2)}) collective-permute-start(bf16[8,512,256]{2,1,0:T(8,128)(2,1)} %bitcast.12), channel_id=1, source_target_pairs={{0,8},{8,0},{1,9},{9,1},{2,10},{10,2},{3,11},{11,3},{4,12},{12,4},... | collective-permute-start | bytes 6291464 | tf_op jit(solution)/shard_map/ppermute | solution.py:163
  164.6 20.9 %copy-start.3 = (f32[384,2048]{1,0:T(8,128)S(1)}, f32[384,2048]{1,0:T(8,128)}, u32[]{:S(2)}) copy-start(f32[384,2048]{1,0:T(8,128)} %copy-done.2) | copy-start | bytes 9437188
  173.9 31.0 %collective-permute-start.12 = (bf16[384,2048]{1,0:T(8,128)(2,1)S(1)}, bf16[384,2048]{1,0:T(8,128)(2,1)}, u32[]{:S(2)}, u32[]{:S(2)}) collective-permute-start(bf16[384,2048]{1,0:T(8,128)(2,1)S(1)} %shard_map.93), channel_id=1, source_target_pairs={{0,1},{1,0},{2,3},{3,2},{4,5},{5,4},{6,7},{7,6},{8,9},{9,8},{10,11... | collective-permute-start | bytes 4718600 | tf_op jit(solution)/shard_map/ppermute | solution.py:101
  178.8 18.0 %collective-permute-start.17 = (bf16[8,512,256]{2,1,0:T(8,128)(2,1)}, bf16[8,512,256]{2,1,0:T(8,128)(2,1)}, u32[]{:S(2)}, u32[]{:S(2)}) collective-permute-start(bf16[8,512,256]{2,1,0:T(8,128)(2,1)} %collective-permute-done.15), channel_id=1, source_target_pairs={{0,8},{8,0},{1,9},{9,1},{2,10},{10,2},{3,11},{11,3},{4,12},{12,4},... | collective-permute-start | bytes 6291464 | tf_op jit(solution)/shard_map/ppermute | solution.py:163
  181.5 39.2 %collective-permute-start.13 = (bf16[384,2048]{1,0:T(8,128)(2,1)S(1)}, bf16[384,2048]{1,0:T(8,128)(2,1)}, u32[]{:S(2)}, u32[]{:S(2)}) collective-permute-start(bf16[384,2048]{1,0:T(8,128)(2,1)S(1)} %add_convert_fusion.2), channel_id=1, source_target_pairs={{0,2},{1,3},{2,0},{3,1},{4,6},{5,7},{6,4},{7,5},{8,10},{9,11},{10,... | collective-permute-start | bytes 4718600 | tf_op jit(solution)/shard_map/ppermute | solution.py:101
  188.9 31.9 %collective-permute-start.14 = (bf16[384,2048]{1,0:T(8,128)(2,1)}, bf16[384,2048]{1,0:T(8,128)(2,1)}, u32[]{:S(2)}, u32[]{:S(2)}) collective-permute-start(bf16[384,2048]{1,0:T(8,128)(2,1)} %add_convert_fusion.1), channel_id=1, source_target_pairs={{2,4},{3,5},{4,2},{5,3},{10,12},{11,13},{12,10},{13,11},{18,20},{1... | collective-permute-start | bytes 4718600 | tf_op jit(solution)/shard_map/ppermute | solution.py:101
  194.9 25.8 %copy-start.13 = (bf16[384,2048]{1,0:T(8,128)(2,1)S(1)}, bf16[384,2048]{1,0:T(8,128)(2,1)}, u32[]{:S(2)}) copy-start(bf16[384,2048]{1,0:T(8,128)(2,1)} %param.10) | copy-start | bytes 4718596
  196.8 23.9 %copy-start.7 = (f32[384,2048]{1,0:T(8,128)S(1)}, f32[384,2048]{1,0:T(8,128)}, u32[]{:S(2)}) copy-start(f32[384,2048]{1,0:T(8,128)} %copy-done.6) | copy-start | bytes 9437188
  198.8 28.0 %copy-start.9 = (bf16[8,2048,256]{2,1,0:T(8,128)(2,1)}, bf16[8,2048,256]{2,1,0:T(8,128)(2,1)S(1)}, u32[]{:S(2)}) copy-start(bf16[8,2048,256]{2,1,0:T(8,128)(2,1)S(1)} %constant_dynamic-update-slice_fusion) | copy-start | bytes 25165828
  224.4 22.0 %copy-start.14 = (bf16[384,2048]{1,0:T(8,128)(2,1)}, bf16[384,2048]{1,0:T(8,128)(2,1)S(1)}, u32[]{:S(2)}) copy-start(bf16[384,2048]{1,0:T(8,128)(2,1)S(1)} %get-tuple-element.67) | copy-start | bytes 4718596
  226.8 19.5 %collective-permute-start.18 = (bf16[2,2,384,256]{2,3,1,0:T(8,128)(2,1)S(1)}, bf16[2,2,384,256]{2,3,1,0:T(8,128)(2,1)}, u32[]{:S(2)}, u32[]{:S(2)}) collective-permute-start(bf16[2,2,384,256]{2,3,1,0:T(8,128)(2,1)S(1)} %fusion.16), channel_id=1, source_target_pairs={{0,1},{1,0},{2,3},{3,2},{4,5},{5,4},{6,7},{7,6},{8,9},{9,8},{10,11... | collective-permute-start | bytes 2359304 | tf_op jit(solution)/shard_map/ppermute | solution.py:101
  246.4 37.6 %copy-start.1 = (bf16[384,1024]{1,0:T(8,128)(2,1)S(1)}, bf16[384,1024]{1,0:T(8,128)(2,1)}, u32[]{:S(2)}) copy-start(bf16[384,1024]{1,0:T(8,128)(2,1)} %param.8) | copy-start | bytes 2359300
  252.5 23.6 %collective-permute-start.19 = (bf16[2,384,256]{1,2,0:T(8,128)(2,1)S(1)}, bf16[2,384,256]{1,2,0:T(8,128)(2,1)S(1)}, u32[]{:S(2)}, u32[]{:S(2)}) collective-permute-start(bf16[2,384,256]{1,2,0:T(8,128)(2,1)S(1)} %fusion.25), channel_id=1, source_target_pairs={{0,4},{1,5},{2,6},{3,7},{4,0},{5,1},{6,2},{7,3},{8,12},{9,13},{10,... | collective-permute-start | bytes 1179656 | tf_op jit(solution)/shard_map/ppermute | solution.py:101
  259.4 3.6 %collective-permute-start.21 = (f32[384]{0:T(512)S(1)}, f32[384]{0:T(512)S(1)}, u32[]{:S(2)}, u32[]{:S(2)}) collective-permute-start(f32[384]{0:T(512)S(1)} %get-tuple-element.66), channel_id=1, source_target_pairs={{0,1},{1,0},{2,3},{3,2},{4,5},{5,4},{6,7},{7,6},{8,9},{9,8},{10,11... | collective-permute-start | bytes 4616 | tf_op jit(solution)/shard_map/ppermute | solution.py:101
  263.0 13.1 %collective-permute-start.22 = (f32[384]{0:T(512)S(1)}, f32[384]{0:T(512)S(1)}, u32[]{:S(2)}, u32[]{:S(2)}) collective-permute-start(f32[384]{0:T(512)S(1)} %add.221), channel_id=1, source_target_pairs={{0,4},{1,5},{2,6},{3,7},{4,0},{5,1},{6,2},{7,3},{8,12},{9,13},{10,... | collective-permute-start | bytes 4616 | tf_op jit(solution)/shard_map/ppermute | solution.py:101
  276.1 3.7 %collective-permute-start.23 = (f32[384]{0:T(512)S(1)}, f32[384]{0:T(512)S(1)}, u32[]{:S(2)}, u32[]{:S(2)}) collective-permute-start(f32[384]{0:T(512)S(1)} %add.222), channel_id=1, source_target_pairs={{0,2},{1,3},{2,0},{3,1},{4,6},{5,7},{6,4},{7,5},{8,10},{9,11},{10,... | collective-permute-start | bytes 4616 | tf_op jit(solution)/shard_map/ppermute | solution.py:101
  277.3 5.7 %collective-permute-start.20 = (bf16[384,256]{0,1:T(8,128)(2,1)S(1)}, bf16[384,256]{0,1:T(8,128)(2,1)S(1)}, u32[]{:S(2)}, u32[]{:S(2)}) collective-permute-start(bf16[384,256]{0,1:T(8,128)(2,1)S(1)} %fusion.28), channel_id=1, source_target_pairs={{0,2},{1,3},{2,0},{3,1},{4,6},{5,7},{6,4},{7,5},{8,10},{9,11},{10,... | collective-permute-start | bytes 589832 | tf_op jit(solution)/shard_map/ppermute | solution.py:101
  (9 other events, 97.8 us)

commit v3 on v0

v3 whole, which is shorter than its diff:
```python
import functools
import math

import jax
import jax.numpy as jnp
from jax import lax
from jax.experimental import pallas as pl
from jax.experimental.pallas import tpu as pltpu
from jax.sharding import PartitionSpec as P

D = 16384
Q_HEADS = 128
KV_HEADS = 8
HEAD = 128
F32 = jnp.float32
BF16 = jnp.bfloat16
LOGIT = HEAD ** (-0.5) * math.log2(math.e)
SWAP = [(0, 1), (1, 0)]
EXTRA = 16
PARAMS = pltpu.CompilerParams(vmem_limit_bytes=40 * 2**20)
BRIEF = pl.CostEstimate(flops=1000, bytes_accessed=1000, transcendentals=0)


def wide(block):
    return block.astype(F32)


def attend_kernel(seq_ref, q_ref, ek_ref, ev_ref, k_ref, v_ref, out_ref):
    contract = (((1,), (1,)), ((), ()))
    shape = (q_ref.shape[0], k_ref.shape[0])
    hidden = lax.broadcasted_iota(jnp.int32, shape, 1) > lax.broadcasted_iota(
        jnp.int32, shape, 0
    )

    def heads(with_earlier):
        for head in range(q_ref.shape[1] // HEAD):
            here = pl.ds(head * HEAD, HEAD)
            q = q_ref[:, here]
            scores = lambda keys: lax.dot_general(q, keys, contract, preferred_element_type=F32)
            pieces = [(jnp.where(hidden, -1e30, scores(k_ref[...])), v_ref)]
            if with_earlier:
                pieces.append((scores(ek_ref[...]), ev_ref))
            peak = functools.reduce(
                jnp.maximum, [jnp.max(p, axis=1, keepdims=True) for p, _ in pieces]
            )
            both = 0.0
            for piece, value_ref in pieces:
                weights = jnp.exp2((piece - peak) * LOGIT).astype(BF16)
                value = value_ref[...]
                beside = jnp.concatenate([value, jnp.ones_like(value)], axis=1)
                both += jnp.dot(weights, beside, preferred_element_type=F32)
            out_ref[:, here] = (both[:, :HEAD] / both[:, HEAD:]).astype(BF16)

    pl.when(seq_ref[0] > 0)(lambda: heads(True))
    pl.when(seq_ref[0] == 0)(lambda: heads(False))


def attend(seq_index, queries, earlier, own):
    rows, columns = queries.shape
    some = min(8, columns // HEAD) * HEAD
    block = pl.BlockSpec((rows, some), lambda h, s: (0, h))
    head = lambda i: pl.BlockSpec((rows, HEAD), lambda h, s: (0, i))
    return pl.pallas_call(
        attend_kernel,
        grid_spec=pltpu.PrefetchScalarGridSpec(
            num_scalar_prefetch=1,
            grid=(columns // some,),
            in_specs=[block, head(0), head(1), head(0), head(1)],
            out_specs=block,
        ),
        out_shape=jax.ShapeDtypeStruct((rows, columns), BF16),
        compiler_params=PARAMS,
        cost_estimate=BRIEF,
    )(seq_index, queries, earlier, earlier, own, own)


def slab_kernel(cuts, at_ref, left_ref, right_ref, *out_refs):
    product = jnp.dot(left_ref[...], right_ref[...], preferred_element_type=F32)
    first = 0
    for rows, out_ref in zip(cuts, out_refs, strict=True):
        out_ref[...] = product[first : first + rows].astype(out_ref.dtype)
        first += rows


def slab_dot(left, weight, at, width, dtype, span=None, cuts=None):
    depth = left.shape[1]
    first, last = span or (0, left.shape[0])
    rows = last - first
    cuts = cuts or (rows,)
    tile = min(width, 1024)
    tiles = width // tile
    return pl.pallas_call(
        functools.partial(slab_kernel, cuts),
        grid_spec=pltpu.PrefetchScalarGridSpec(
            num_scalar_prefetch=1,
            grid=(tiles,),
            in_specs=[
                pl.BlockSpec((rows, depth), lambda i, at: (first // rows, 0)),
                pl.BlockSpec((depth, tile), lambda i, at: (0, at[0] * tiles + i)),
            ],
            out_specs=[pl.BlockSpec((n, tile), lambda i, at: (0, i)) for n in cuts],
        ),
        out_shape=[jax.ShapeDtypeStruct((n, width), dtype) for n in cuts],
        compiler_params=PARAMS,
        cost_estimate=BRIEF,
    )(jnp.reshape(at, (1,)), left, weight)


def put_squares(out_ref, squares):
    rows = out_ref.shape[0] - EXTRA
    high = squares.astype(BF16)
    low = (squares - wide(high)).astype(BF16)
    line = lax.broadcasted_iota(jnp.int32, (EXTRA, squares.shape[1]), 0)
    both = jnp.where(line == 0, wide(high), jnp.where(line == 1, wide(low), 0.0))
    out_ref[rows:] = both.astype(BF16)


def kv_kernel(at_ref, *refs):
    lefts, rights, rest = refs[:4], refs[4:8], refs[8:]
    out_ref = rest[-1]
    rows = lefts[0].shape[0]
    for i in range(out_ref.shape[0]):
        total = 0.0
        for left, right in zip(lefts, rights, strict=True):
            total += jnp.dot(left[...], right[0, i], preferred_element_type=F32)
        out_ref[i, :rows] = total.astype(out_ref.dtype)
        if len(rest) == 2:
            put_squares(out_ref.at[i], rest[0][...])


def kv_dot(scaled, quarters, parts, side, squares=None):
    rows = scaled.shape[0]
    _, _, part, columns = parts[0].shape
    step = 2
    left = lambda q: pl.BlockSpec((rows, part), lambda i, at: (0, at[q]))
    right = pl.BlockSpec((1, step, part, columns), lambda i, at: (side, i, 0, 0))
    beside = [] if squares is None else [squares]
    total, dtype = (rows, F32) if squares is None else (rows + EXTRA, BF16)
    return pl.pallas_call(
        kv_kernel,
        grid_spec=pltpu.PrefetchScalarGridSpec(
            num_scalar_prefetch=1,
            grid=(4 // step,),
            in_specs=[left(q) for q in range(4)]
            + [right] * 4
            + [pl.BlockSpec((1, columns), lambda i, at: (0, 0))] * len(beside),
            out_specs=pl.BlockSpec((step, total, columns), lambda i, at: (i, 0, 0)),
        ),
        out_shape=jax.ShapeDtypeStruct((4, total, columns), dtype),
        compiler_params=PARAMS,
        cost_estimate=BRIEF,
    )(quarters, *[scaled] * 4, *parts, *beside)


def kv_pair_kernel(kept_ref, got_ref, squares_ref, own_ref, total_ref, *sent_refs):
    rows = kept_ref.shape[1]
    given = wide(got_ref[0, rows:])
    squares = squares_ref[...] + given[0:1] + given[1:2]
    total_ref[...] = squares
    own_ref[...] = kept_ref[0] + wide(got_ref[0, :rows])
    for i, sent_ref in enumerate(sent_refs, 1):
        sent_ref[:rows] = (kept_ref[i] + wide(got_ref[i, :rows])).astype(BF16)
        put_squares(sent_ref, squares)


def kv_sum(kept, got, squares):
    rows, columns = kept.shape[1:]
    own, total, *sent = pl.pallas_call(
        kv_pair_kernel,
        out_shape=[
            jax.ShapeDtypeStruct((rows, columns), F32),
            jax.ShapeDtypeStruct((1, columns), F32),
        ]
        + [jax.ShapeDtypeStruct((rows + EXTRA, columns), BF16)] * 3,
        compiler_params=PARAMS,
        cost_estimate=BRIEF,
    )(kept, got, squares)
    return own, total, [by_xor(sent[i - 1], 2 * i) for i in (3, 2, 1)]


def kv_finish(own, total, arrived):
    rows = own.shape[0]
    for block in arrived:
        own = own + wide(block[:rows])
        total = total + wide(block[rows : rows + 1]) + wide(block[rows + 1 : rows + 2])
    inverse = lax.rsqrt(total[0, :rows] / D + 1e-05)
    return (own * inverse[:, None]).astype(BF16)


def together(*values):
    return lax.optimization_barrier(values)


def over(block, pairs):
    return lax.ppermute(block, "tensor", pairs)


def by_xor(block, step):
    return over(block, [(i, i ^ step) for i in range(8)])


def to_middle(block):
    return over(block, [(0, 2), (1, 3), (6, 4), (7, 5)])


def across(block):
    return over(block, [(2, 4), (3, 5), (4, 2), (5, 3)])


def place():
    t = lax.axis_index("tensor")
    z, y = t // 2, t % 2
    low = z < 2
    far = jnp.where(low, 3, 0)
    near = jnp.where(low, 2, 1)
    return z, y, (far, near, 6 - far - near - z, z)


def weight_blocks(weight, quarter, side):
    depth, columns = weight.shape
    blocks = weight.reshape(4, 2, 4, depth // 32, columns)
    blocks = lax.dynamic_index_in_dim(blocks, side, 1, keepdims=False)
    return lax.dynamic_index_in_dim(blocks, quarter, 1, keepdims=False)


def weight_over_z(blocks, steps):
    z = place()[0]
    pieces = [lax.dynamic_index_in_dim(blocks, z ^ i, 0, keepdims=False) for i in steps]
    return [by_xor(piece, 2 * i) if i else piece for i, piece in zip(steps, pieces)]


def chained(attend_all, residual, out_weight, gain, kv_weight):
    z, y, order = place()
    tokens, width = residual.shape
    columns = kv_weight.shape[1]
    quarter = lax.axis_index("groups") * 2 + lax.axis_index("seq")
    quarters = jnp.stack([quarter, quarter ^ 2, quarter ^ 1, quarter ^ 3])
    half = tokens // 2
    cuts = (half, half)

    def sent_term(j):
        return slab_dot(context, out_weight, 2 * order[j] + 1 - y, width, BF16, cuts=cuts)

    def own_term(j):
        return slab_dot(context, out_weight, 2 * order[j] + y, width, F32, cuts=cuts)

    got = by_xor(weight_blocks(kv_weight, quarter, 1 - y), 1)
    context = attend_all()
    kept = weight_blocks(kv_weight, quarter, y)
    pieces = weight_over_z(kept, (0, 1, 2, 3))
    *leaving, context, got, p1, p2, p3 = together(*sent_term(0), context, got, *pieces[1:])
    arriving = [by_xor(block, 1) for block in leaving]
    pieces = [pieces[0], p1, p2, p3]
    other_pieces = weight_over_z(got, (0, 1, 2, 3))
    own = own_term(0)
    arriving += [by_xor(block, 1) for block in sent_term(1)]
    started = []
    far, near, streams, sums = [], [], [], []
    for h in range(8):
        j, side = divmod(h, 2)
        moved = started[h - 2] if h > 1 else other_pieces[1:] if h == 0 else []
        here, context, *rest = together(arriving[h], context, *own, *moved)
        own, moved = rest[:2], rest[2:]
        term = own[side] + wide(here)
        if j == 0:
            far.append(term)
            started.append([to_middle(term.astype(BF16))])
        if j == 1:
            near.append(term)
            far_sent = (far[side] + wide(moved[0])).astype(BF16)
            started.append([across(far_sent), to_middle(term.astype(BF16))])
        if j == 2:
            last_sent = (term + wide(moved[0])).astype(BF16)
            near_sent = (near[side] + wide(moved[1])).astype(BF16)
            started.append([by_xor(last_sent, 2), across(near_sent)])
        if j == 3:
            attended = term + wide(moved[0]) + wide(moved[1])
            first = side * half
            stream = (wide(residual[first : first + half]) + attended).astype(BF16)
            widened = wide(stream)
            squares = jnp.sum(widened * widened, axis=1)
            squares = jnp.pad(squares, (0, columns - half)).reshape(1, columns)
            scaled = (widened * gain).astype(BF16)
            streams.append(stream)
            leaving = kv_dot(scaled, quarters, parts, 1, squares)
            staying = kv_dot(scaled, quarters, parts, 0)
            sums.append((staying, by_xor(leaving, 1), squares))
        if h == 0:
            mine = jnp.stack([*pieces, other_pieces[0], *moved]).reshape((2, *kept.shape))
            other = lax.ppermute(mine, "groups", SWAP)
        if h == 4:
            mine, other, context = together(mine, other, context)
            parts = [mine, other] + [lax.ppermute(p, "seq", SWAP) for p in (mine, other)]
        if h == 5:
            *parts, context = together(*parts, context)
        if side == 0 and j < 3:
            following = own_term(j + 1)
            if j < 2:
                arriving += [by_xor(block, 1) for block in sent_term(j + 2)]
        if side == 1 and j < 3:
            own = following
    projected = [kv_finish(*kv_sum(*terms)) for terms in sums]
    return jnp.concatenate(streams, axis=0), jnp.concatenate(projected, axis=0)


def gathered(attend_all, residual, out_weight, gain, kv_weight):
    context = attend_all()
    partial = jnp.dot(context, out_weight, preferred_element_type=F32)
    attended = lax.psum_scatter(partial.astype(BF16), "tensor", scatter_dimension=1, tiled=True)
    stream = (wide(residual) + wide(attended)).astype(BF16)
    widened = wide(stream)
    total = lax.psum(jnp.sum(widened * widened, axis=1), "tensor")
    inverse = lax.rsqrt(total / D + 1e-05)
    everything = lax.all_gather((widened * gain).astype(BF16), "tensor", axis=1, tiled=True)
    projected = jnp.dot(everything, kv_weight, preferred_element_type=F32)
    return stream, (projected * inverse[:, None]).astype(BF16)


def on_device(queries, keys, values, residual, out_weight, norm_gain, kv_weight):
    heads_here = queries.shape[1] // HEAD
    devices = lax.axis_size("tensor")
    tensor_rank = lax.axis_index("tensor")
    seq_index = lax.axis_index("seq").reshape(1)
    kv_group = tensor_rank * heads_here // (Q_HEADS // KV_HEADS)
    head = lambda heads: lax.dynamic_slice_in_dim(heads, kv_group * HEAD, HEAD, 1)
    own = jnp.concatenate([head(keys), head(values)], axis=1)
    earlier = lax.ppermute(own, "seq", [(0, 1)])
    attend_all = functools.partial(attend, seq_index, queries, earlier, own)
    summed = chained if devices == 8 else gathered
    gain = wide(norm_gain)[None, :]
    return summed(attend_all, residual, out_weight, gain, kv_weight)


def solution(mesh):
    return jax.shard_map(
        on_device,
        mesh=mesh,
        in_specs=(
            P(("groups", "seq"), "tensor"),
            P(("groups", "seq"), None),
            P(("groups", "seq"), None),
            P(("groups", "seq"), "tensor"),
            P("tensor", None),
            P("tensor"),
            P(None, "tensor"),
        ),
        out_specs=(P(("groups", "seq"), "tensor"), P(("groups", "seq"), "tensor")),
        check_vma=False,
    )
```

time: 694 us -> 214 us (0.31)
  waiting for transfers between devices: 412 us -> 60.2 us
  matrix products: 76.4 us -> 0 us
  local copies, waits for them, and re-layouts: 92.9 us -> 19.1 us
  Pallas kernels: 0 us -> 66.2 us
  blocking collectives: 50.9 us -> 0 us
  starting transfers between devices: 16.5 us -> 51.6 us
  between operations: 14.2 us -> 1.05 us
  other arithmetic: 28 us -> 15.1 us
    all_to_all x2 -> x0, waiting for transfers between devices: 271 us -> none  [the longest x1 271 us: on_device(): lax.all_to_all(packed.reshape(tok_rows, D), 'tensor', split_axis=1, conca...]
    all_gather x1 -> x0, waiting for transfers between devices: 141 us -> none  [on_device(): piece_packed = lax.all_gather(norm_packed, 'tensor', axis=1, tiled=True)]
    dot_general x1 -> x0, local copies, waits for them, and re-layouts: 86.6 us -> none  [on_device(): jnp.dot(context, out_weight, preferred_element_type=jnp.float32)]
    pallas_call x0 -> x15, Pallas kernels: none -> 66.2 us  [the longest x8 47.6 us: slab_dot(): pl.pallas_call(functools.partial(slab_kernel, cuts), grid_spec=pltpu.Pref...]
    dot_general x3 -> x0, matrix products: 66.2 us -> none  [the longest x1 45.7 us: on_device(): jnp.dot(context, out_weight, preferred_element_type=jnp.float32)]
    ppermute x2 -> x37, waiting for transfers between devices: 0.01 us -> 60.2 us  [the longest x33 49.6 us: over(): return lax.ppermute(block, 'tensor', pairs)]
    ppermute x2 -> x37, starting transfers between devices: 3.65 us -> 51.6 us  [the longest x33 48.3 us: over(): return lax.ppermute(block, 'tensor', pairs)]
    all_gather x1 -> x0, blocking collectives: 31.4 us -> none  [on_device(): lax.all_gather(norm_scales.astype(jnp.bfloat16), 'tensor', axis=1, tiled=...]
  transfers between devices with their start and end apart: 5 -> 37, of which waited for: 2 -> 14; matrix products, arithmetic and copies ran while one was open for 17% -> 15% of each run, Pallas kernels for 0% -> 29%
where the time goes in v3:
time: 214 us; the launch traced here: 213 us
  Pallas kernels  66.2 us (31%)
  waiting for transfers between devices  60.2 us (28%)
  starting transfers between devices  51.6 us (24%)
  local copies, waits for them, and re-layouts  19.1 us (9%)
  other arithmetic  15.1 us (7%)
    ppermute x33, waiting for transfers between devices, over(): return lax.ppermute(block, 'tensor', pairs)  49.6 us
    ppermute x33, starting transfers between devices, over(): return lax.ppermute(block, 'tensor', pairs)  48.3 us
    pallas_call x8, Pallas kernels, slab_dot(): pl.pallas_call(functools.partial(slab_kernel, cuts), grid_spec=pltpu.Pref...  47.6 us
    pallas_call x4, Pallas kernels, kv_dot(): pl.pallas_call(kv_kernel, grid_spec=pltpu.PrefetchScalarGridSpec(num_scal...  13.4 us
    unnamed x13, local copies, waits for them, and re-layouts  12.1 us
    ppermute x1, waiting for transfers between devices, chained(): other = lax.ppermute(mine, 'groups', SWAP)  10.5 us
    pallas_call x1, Pallas kernels, attend(): pl.pallas_call(attend_kernel, grid_spec=pltpu.PrefetchScalarGridSpec(num_...  5.04 us
  transfers between devices with their start and end apart: 37, of which 14 were waited for; matrix products, arithmetic and copies ran while one was open for 15% of the time, Pallas kernels for 29%

profile of v3, /device:TPU:0, one launch (start us, length us, event | category | flops | bytes accessed | tf_op | source)
XLA Modules:
  0.0 213.2 jit_solution(9564389811759544513)
XLA Ops:
  2.9 3.0 %collective-permute-start.1 = (bf16[4,512,256]{2,1,0:T(8,128)(2,1)}, bf16[4,512,256]{2,1,0:T(8,128)(2,1)}, u32[]{:S(2)}, u32[]{:S(2)}) collective-permute-start(bf16[4,512,256]{2,1,0:T(8,128)(2,1)} %dynamic-slice_bitcast_fusion), channel_id=1, source_target_pairs={{0,1},{1,0},{2,3},{3,2},{4,5},{5,4},{6,7},{7,6},{8,9},{9,8},{10,11... | collective-permute-start | bytes 3145736 | tf_op jit(solution)/shard_map/ppermute | solution.py:195
  7.9 3.6 %collective-permute-start.4 = (bf16[512,256]{1,0:T(8,128)(2,1)}, bf16[512,256]{1,0:T(8,128)(2,1)}, u32[]{:S(2)}, u32[]{:S(2)}) collective-permute-start(bf16[512,256]{1,0:T(8,128)(2,1)} %get-tuple-element.162), channel_id=1, source_target_pairs={{0,6},{1,7},{2,4},{3,5},{4,2},{5,3},{6,0},{7,1},{8,14},{9,15},{10,... | collective-permute-start | bytes 786440 | tf_op jit(solution)/shard_map/ppermute | solution.py:195
  16.3 5.0 %shard_map.86.left_ref = bf16[384,2048]{1,0:T(8,128)(2,1)S(1)} custom-call(s32[1]{0:T(128)} %bitcast.3.seq_ref, bf16[384,2048]{1,0:T(8,128)(2,1)S(1)} %copy-done, bf16[384,256]{1,0:T(8,128)(2,1)S(1)} %collective-permute-done.ek_ref.ev_ref, bf16[384,256]{1,0:T(8,128)(2,1)S(1)} %collective-permute-done.ek_ref.ev_ref, ...), custom_call_target="tpu_custom_call" | custom-call | flops 1000 | bytes 1000 | tf_op jit(solution)/shard_map/pallas_call | solution.py:63
  21.4 5.9 %shard_map.87 = (bf16[192,2048]{1,0:T(8,128)(2,1)S(1)}, bf16[192,2048]{1,0:T(8,128)(2,1)S(1)}) custom-call(s32[1]{0:T(128)} %bitcast.2.at_ref, bf16[384,2048]{1,0:T(8,128)(2,1)S(1)} %shard_map.86.left_ref, bf16[2048,16384]{1,0:T(8,128)(2,1)} %right_ref.15), custom_call_target="tpu_custom_call" | custom-call | flops 1000 | bytes 1000 | tf_op jit(solution)/shard_map/pallas_call | solution.py:92
  27.3 6.6 %collective-permute-done.3 = bf16[512,256]{1,0:T(8,128)(2,1)} collective-permute-done((bf16[512,256]{1,0:T(8,128)(2,1)}, bf16[512,256]{1,0:T(8,128)(2,1)}, u32[]{:S(2)}, u32[]{:S(2)}) %collective-permute-start.3) | collective-permute-done | bytes 262176 | tf_op jit(solution)/shard_map/ppermute | solution.py:195
  42.9 2.5 %collective-permute-start.10 = (bf16[512,256]{1,0:T(8,128)(2,1)}, bf16[512,256]{1,0:T(8,128)(2,1)}, u32[]{:S(2)}, u32[]{:S(2)}) collective-permute-start(bf16[512,256]{1,0:T(8,128)(2,1)} %get-tuple-element.168), channel_id=1, source_target_pairs={{0,6},{1,7},{2,4},{3,5},{4,2},{5,3},{6,0},{7,1},{8,14},{9,15},{10,... | collective-permute-start | bytes 786440 | tf_op jit(solution)/shard_map/ppermute | solution.py:195
  47.3 5.9 %shard_map.88 = (bf16[192,2048]{1,0:T(8,128)(2,1)S(1)}, bf16[192,2048]{1,0:T(8,128)(2,1)S(1)}) custom-call(s32[1]{0:T(128)} %bitcast.1.at_ref, bf16[384,2048]{1,0:T(8,128)(2,1)S(1)} %shard_map.86.left_ref, bf16[2048,16384]{1,0:T(8,128)(2,1)} %right_ref.15), custom_call_target="tpu_custom_call" | custom-call | flops 1000 | bytes 1000 | tf_op jit(solution)/shard_map/pallas_call | solution.py:92
  53.2 6.0 %shard_map.89 = (f32[192,2048]{1,0:T(8,128)S(1)}, f32[192,2048]{1,0:T(8,128)S(1)}) custom-call(s32[1]{0:T(128)} %bitcast.9.at_ref, bf16[384,2048]{1,0:T(8,128)(2,1)S(1)} %shard_map.86.left_ref, bf16[2048,16384]{1,0:T(8,128)(2,1)} %right_ref.15), custom_call_target="tpu_custom_call" | custom-call | flops 1000 | bytes 1000 | tf_op jit(solution)/shard_map/pallas_call | solution.py:92
  59.9 5.7 %collective-permute-done.9 = bf16[512,256]{1,0:T(8,128)(2,1)} collective-permute-done((bf16[512,256]{1,0:T(8,128)(2,1)}, bf16[512,256]{1,0:T(8,128)(2,1)}, u32[]{:S(2)}, u32[]{:S(2)}) %collective-permute-start.9) | collective-permute-done | bytes 262176 | tf_op jit(solution)/shard_map/ppermute | solution.py:195
  66.3 5.0 %collective-permute-done.7 = bf16[192,2048]{1,0:T(8,128)(2,1)} collective-permute-done((bf16[192,2048]{1,0:T(8,128)(2,1)S(1)}, bf16[192,2048]{1,0:T(8,128)(2,1)}, u32[]{:S(2)}, u32[]{:S(2)}) %collective-permute-start.7) | collective-permute-done | bytes 786464 | tf_op jit(solution)/shard_map/ppermute | solution.py:195
  77.1 5.9 %shard_map.92 = (bf16[192,2048]{1,0:T(8,128)(2,1)S(1)}, bf16[192,2048]{1,0:T(8,128)(2,1)S(1)}) custom-call(s32[1]{0:T(128)} %bitcast.23.at_ref, bf16[384,2048]{1,0:T(8,128)(2,1)S(1)} %shard_map.86.left_ref, bf16[2048,16384]{1,0:T(8,128)(2,1)} %right_ref.15), custom_call_target="tpu_custom_call" | custom-call | flops 1000 | bytes 1000 | tf_op jit(solution)/shard_map/pallas_call | solution.py:92
  87.1 6.0 %shard_map.90 = (f32[192,2048]{1,0:T(8,128)S(1)}, f32[192,2048]{1,0:T(8,128)S(1)}) custom-call(s32[1]{0:T(128)} %bitcast.13.at_ref, bf16[384,2048]{1,0:T(8,128)(2,1)S(1)} %shard_map.86.left_ref, bf16[2048,16384]{1,0:T(8,128)(2,1)} %right_ref.15), custom_call_target="tpu_custom_call" | custom-call | flops 1000 | bytes 1000 | tf_op jit(solution)/shard_map/pallas_call | solution.py:92
  99.1 5.8 %collective-permute-done.15 = bf16[192,2048]{1,0:T(8,128)(2,1)S(1)} collective-permute-done((bf16[192,2048]{1,0:T(8,128)(2,1)S(1)}, bf16[192,2048]{1,0:T(8,128)(2,1)S(1)}, u32[]{:S(2)}, u32[]{:S(2)}) %collective-permute-start.15) | collective-permute-done | bytes 786464 | tf_op jit(solution)/shard_map/ppermute | solution.py:195
  105.1 3.8 %collective-permute-start.18 = (bf16[192,2048]{1,0:T(8,128)(2,1)S(1)}, bf16[192,2048]{1,0:T(8,128)(2,1)S(1)}, u32[]{:S(2)}, u32[]{:S(2)}) collective-permute-start(bf16[192,2048]{1,0:T(8,128)(2,1)S(1)} %fusion.6), channel_id=1, source_target_pairs={{0,2},{1,3},{6,4},{7,5},{8,10},{9,11},{14,12},{15,13},{16,18},{17,... | collective-permute-start | bytes 2359304 | tf_op jit(solution)/shard_map/ppermute | solution.py:195
  109.8 5.9 %shard_map.91 = (bf16[192,2048]{1,0:T(8,128)(2,1)S(1)}, bf16[192,2048]{1,0:T(8,128)(2,1)S(1)}) custom-call(s32[1]{0:T(128)} %bitcast.at_ref, bf16[384,2048]{1,0:T(8,128)(2,1)S(1)} %shard_map.86.left_ref, bf16[2048,16384]{1,0:T(8,128)(2,1)} %right_ref.15), custom_call_target="tpu_custom_call" | custom-call | flops 1000 | bytes 1000 | tf_op jit(solution)/shard_map/pallas_call | solution.py:92
  115.7 6.0 %shard_map.93 = (f32[192,2048]{1,0:T(8,128)S(1)}, f32[192,2048]{1,0:T(8,128)S(1)}) custom-call(s32[1]{0:T(128)} %bitcast.24.at_ref, bf16[384,2048]{1,0:T(8,128)(2,1)S(1)} %shard_map.86.left_ref, bf16[2048,16384]{1,0:T(8,128)(2,1)} %right_ref.15), custom_call_target="tpu_custom_call" | custom-call | flops 1000 | bytes 1000 | tf_op jit(solution)/shard_map/pallas_call | solution.py:92
  123.2 3.9 %collective-permute-start.24 = (bf16[192,2048]{1,0:T(8,128)(2,1)S(1)}, bf16[192,2048]{1,0:T(8,128)(2,1)S(1)}, u32[]{:S(2)}, u32[]{:S(2)}) collective-permute-start(bf16[192,2048]{1,0:T(8,128)(2,1)S(1)} %fusion.7), channel_id=1, source_target_pairs={{0,2},{1,3},{6,4},{7,5},{8,10},{9,11},{14,12},{15,13},{16,18},{17,... | collective-permute-start | bytes 2359304 | tf_op jit(solution)/shard_map/ppermute | solution.py:195
  128.9 10.5 %collective-permute-done.13.refs_5_ = bf16[2,4,512,256]{3,2,1,0:T(8,128)(2,1)} collective-permute-done((bf16[2,4,512,256]{3,2,1,0:T(8,128)(2,1)}, bf16[2,4,512,256]{3,2,1,0:T(8,128)(2,1)}, u32[]{:S(2)}, u32[]{:S(2)}) %collective-permute-start.13) | collective-permute-done | bytes 2097184 | tf_op jit(solution)/shard_map/ppermute | solution.py:290
  141.0 3.1 %collective-permute-done.24 = bf16[192,2048]{1,0:T(8,128)(2,1)S(1)} collective-permute-done((bf16[192,2048]{1,0:T(8,128)(2,1)S(1)}, bf16[192,2048]{1,0:T(8,128)(2,1)S(1)}, u32[]{:S(2)}, u32[]{:S(2)}) %collective-permute-start.24) | collective-permute-done | bytes 786464 | tf_op jit(solution)/shard_map/ppermute | solution.py:195
  147.0 6.5 %collective-permute-done.12 = bf16[192,2048]{1,0:T(8,128)(2,1)S(1)} collective-permute-done((bf16[192,2048]{1,0:T(8,128)(2,1)S(1)}, bf16[192,2048]{1,0:T(8,128)(2,1)S(1)}, u32[]{:S(2)}, u32[]{:S(2)}) %collective-permute-start.12) | collective-permute-done | bytes 786464 | tf_op jit(solution)/shard_map/ppermute | solution.py:195
  154.2 3.6 %collective-permute-done.19 = bf16[192,2048]{1,0:T(8,128)(2,1)} collective-permute-done((bf16[192,2048]{1,0:T(8,128)(2,1)S(1)}, bf16[192,2048]{1,0:T(8,128)(2,1)}, u32[]{:S(2)}, u32[]{:S(2)}) %collective-permute-start.19) | collective-permute-done | bytes 786464 | tf_op jit(solution)/shard_map/ppermute | solution.py:195
  157.8 2.6 %collective-permute-start.25 = (bf16[192,2048]{1,0:T(8,128)(2,1)}, bf16[192,2048]{1,0:T(8,128)(2,1)}, u32[]{:S(2)}, u32[]{:S(2)}) collective-permute-start(bf16[192,2048]{1,0:T(8,128)(2,1)} %add_convert_fusion.2), channel_id=1, source_target_pairs={{0,2},{1,3},{2,0},{3,1},{4,6},{5,7},{6,4},{7,5},{8,10},{9,11},{10,... | collective-permute-start | bytes 2359304 | tf_op jit(solution)/shard_map/ppermute | solution.py:195
  162.1 6.1 %shard_map.94 = (f32[192,2048]{1,0:T(8,128)S(1)}, f32[192,2048]{1,0:T(8,128)S(1)}) custom-call(s32[1]{0:T(128)} %bitcast.14.at_ref, bf16[384,2048]{1,0:T(8,128)(2,1)S(1)} %shard_map.86.left_ref, bf16[2048,16384]{1,0:T(8,128)(2,1)} %right_ref.15), custom_call_target="tpu_custom_call" | custom-call | flops 1000 | bytes 1000 | tf_op jit(solution)/shard_map/pallas_call | solution.py:92
  168.2 3.2 %collective-permute-done.21 = bf16[192,2048]{1,0:T(8,128)(2,1)} collective-permute-done((bf16[192,2048]{1,0:T(8,128)(2,1)S(1)}, bf16[192,2048]{1,0:T(8,128)(2,1)}, u32[]{:S(2)}, u32[]{:S(2)}) %collective-permute-start.21) | collective-permute-done | bytes 786464 | tf_op jit(solution)/shard_map/ppermute | solution.py:195
  173.0 3.6 %fusion.1 = (f32[192]{0:T(256)S(1)}, bf16[192,2048]{1,0:T(8,128)(2,1)S(1)}, f32[192]{0:T(256)S(1)}, bf16[192,2048]{1,0:T(8,128)(2,1)S(1)}) fusion(bf16[192,2048]{1,0:T(8,128)(2,1)} %collective-permute-done.20, bf16[192,2048]{1,0:T(8,128)(2,1)} %collective-permute-done.19, f32[192,2048]{1,0:T(8,128)S(1)} %get-tuple-element.123, ...), kind=kLoop, calls=%fused_computation.5 | loop fusion | flops 9436800 | bytes 11011584 | tf_op jit(solution)/shard_map/reduce_sum | solution.py:281
  177.0 3.4 %shard_map.99 = bf16[4,208,256]{2,1,0:T(8,128)(2,1)S(1)} custom-call(s32[4]{0:T(128)S(1)} %pad_add_fusion.at_ref, bf16[192,2048]{1,0:T(8,128)(2,1)S(1)} %get-tuple-element.184.refs_0_.refs_1_.refs_2_.refs_3_, bf16[192,2048]{1,0:T(8,128)(2,1)S(1)} %get-tuple-element.184.refs_0_.refs_1_.refs_2_.refs_3_, ...), custom_call_target="tpu_custom_call" | custom-call | flops 1000 | bytes 1000 | tf_op jit(solution)/shard_map/pallas_call | solution.py:139
  180.7 3.3 %shard_map.96 = bf16[4,208,256]{2,1,0:T(8,128)(2,1)S(1)} custom-call(s32[4]{0:T(128)S(1)} %pad_add_fusion.at_ref, bf16[192,2048]{1,0:T(8,128)(2,1)S(1)} %get-tuple-element.183.refs_0_.refs_1_.refs_2_.refs_3_, bf16[192,2048]{1,0:T(8,128)(2,1)S(1)} %get-tuple-element.183.refs_0_.refs_1_.refs_2_.refs_3_, ...), custom_call_target="tpu_custom_call" | custom-call | flops 1000 | bytes 1000 | tf_op jit(solution)/shard_map/pallas_call | solution.py:139
  185.8 3.3 %shard_map.98.kept_ref = f32[4,192,256]{2,1,0:T(8,128)S(1)} custom-call(s32[4]{0:T(128)S(1)} %pad_add_fusion.at_ref, bf16[192,2048]{1,0:T(8,128)(2,1)S(1)} %get-tuple-element.184.refs_0_.refs_1_.refs_2_.refs_3_, bf16[192,2048]{1,0:T(8,128)(2,1)S(1)} %get-tuple-element.184.refs_0_.refs_1_.refs_2_.refs_3_, ...), custom_call_target="tpu_custom_call" | custom-call | flops 1000 | bytes 1000 | tf_op jit(solution)/shard_map/pallas_call | solution.py:139
  189.2 3.2 %collective-permute-done.33.got_ref = bf16[4,208,256]{2,1,0:T(8,128)(2,1)S(1)} collective-permute-done((bf16[4,208,256]{2,1,0:T(8,128)(2,1)S(1)}, bf16[4,208,256]{2,1,0:T(8,128)(2,1)S(1)}, u32[]{:S(2)}, u32[]{:S(2)}) %collective-permute-start.33) | collective-permute-done | bytes 426016 | tf_op jit(solution)/shard_map/ppermute | solution.py:195
  195.2 3.3 %shard_map.95.kept_ref = f32[4,192,256]{2,1,0:T(8,128)S(1)} custom-call(s32[4]{0:T(128)S(1)} %pad_add_fusion.at_ref, bf16[192,2048]{1,0:T(8,128)(2,1)S(1)} %get-tuple-element.183.refs_0_.refs_1_.refs_2_.refs_3_, bf16[192,2048]{1,0:T(8,128)(2,1)S(1)} %get-tuple-element.183.refs_0_.refs_1_.refs_2_.refs_3_, ...), custom_call_target="tpu_custom_call" | custom-call | flops 1000 | bytes 1000 | tf_op jit(solution)/shard_map/pallas_call | solution.py:139
  198.5 3.9 %collective-permute-start.35 = (bf16[208,256]{1,0:T(8,128)(2,1)S(1)}, bf16[208,256]{1,0:T(8,128)(2,1)S(1)}, u32[]{:S(2)}, u32[]{:S(2)}) collective-permute-start(bf16[208,256]{1,0:T(8,128)(2,1)S(1)} %get-tuple-element.155), channel_id=1, source_target_pairs={{0,4},{1,5},{2,6},{3,7},{4,0},{5,1},{6,2},{7,3},{8,12},{9,13},{10,... | collective-permute-start | bytes 319496 | tf_op jit(solution)/shard_map/ppermute | solution.py:195
  209.3 3.0 %collective-permute-done.31 = bf16[208,256]{1,0:T(8,128)(2,1)S(1)} collective-permute-done((bf16[208,256]{1,0:T(8,128)(2,1)S(1)}, bf16[208,256]{1,0:T(8,128)(2,1)S(1)}, u32[]{:S(2)}, u32[]{:S(2)}) %collective-permute-start.31) | collective-permute-done | bytes 106528 | tf_op jit(solution)/shard_map/ppermute | solution.py:195
  (103 shorter events, 63.0 us)
Async XLA Ops:
  2.9 30.9 %collective-permute-start.1 = (bf16[4,512,256]{2,1,0:T(8,128)(2,1)}, bf16[4,512,256]{2,1,0:T(8,128)(2,1)}, u32[]{:S(2)}, u32[]{:S(2)}) collective-permute-start(bf16[4,512,256]{2,1,0:T(8,128)(2,1)} %dynamic-slice_bitcast_fusion), channel_id=1, source_target_pairs={{0,1},{1,0},{2,3},{3,2},{4,5},{5,4},{6,7},{7,6},{8,9},{9,8},{10,11... | collective-permute-start | bytes 3145736 | tf_op jit(solution)/shard_map/ppermute | solution.py:195
  7.9 19.4 %collective-permute-start.4 = (bf16[512,256]{1,0:T(8,128)(2,1)}, bf16[512,256]{1,0:T(8,128)(2,1)}, u32[]{:S(2)}, u32[]{:S(2)}) collective-permute-start(bf16[512,256]{1,0:T(8,128)(2,1)} %get-tuple-element.162), channel_id=1, source_target_pairs={{0,6},{1,7},{2,4},{3,5},{4,2},{5,3},{6,0},{7,1},{8,14},{9,15},{10,... | collective-permute-start | bytes 786440 | tf_op jit(solution)/shard_map/ppermute | solution.py:195
  11.5 22.3 %collective-permute-start.3 = (bf16[512,256]{1,0:T(8,128)(2,1)}, bf16[512,256]{1,0:T(8,128)(2,1)}, u32[]{:S(2)}, u32[]{:S(2)}) collective-permute-start(bf16[512,256]{1,0:T(8,128)(2,1)} %get-tuple-element.163), channel_id=1, source_target_pairs={{0,4},{1,5},{2,6},{3,7},{4,0},{5,1},{6,2},{7,3},{8,12},{9,13},{10,... | collective-permute-start | bytes 786440 | tf_op jit(solution)/shard_map/ppermute | solution.py:195
  11.5 22.3 %collective-permute-start.2 = (bf16[512,256]{1,0:T(8,128)(2,1)}, bf16[512,256]{1,0:T(8,128)(2,1)}, u32[]{:S(2)}, u32[]{:S(2)}) collective-permute-start(bf16[512,256]{1,0:T(8,128)(2,1)} %get-tuple-element.164), channel_id=1, source_target_pairs={{0,2},{1,3},{2,0},{3,1},{4,6},{5,7},{6,4},{7,5},{8,10},{9,11},{10,... | collective-permute-start | bytes 786440 | tf_op jit(solution)/shard_map/ppermute | solution.py:195
  33.9 37.4 %collective-permute-start.6 = (bf16[192,2048]{1,0:T(8,128)(2,1)S(1)}, bf16[192,2048]{1,0:T(8,128)(2,1)}, u32[]{:S(2)}, u32[]{:S(2)}) collective-permute-start(bf16[192,2048]{1,0:T(8,128)(2,1)S(1)} %get-tuple-element.84), channel_id=1, source_target_pairs={{0,1},{1,0},{2,3},{3,2},{4,5},{5,4},{6,7},{7,6},{8,9},{9,8},{10,11... | collective-permute-start | bytes 2359304 | tf_op jit(solution)/shard_map/ppermute | solution.py:195
  34.5 36.8 %collective-permute-start.7 = (bf16[192,2048]{1,0:T(8,128)(2,1)S(1)}, bf16[192,2048]{1,0:T(8,128)(2,1)}, u32[]{:S(2)}, u32[]{:S(2)}) collective-permute-start(bf16[192,2048]{1,0:T(8,128)(2,1)S(1)} %get-tuple-element.85), channel_id=1, source_target_pairs={{0,1},{1,0},{2,3},{3,2},{4,5},{5,4},{6,7},{7,6},{8,9},{9,8},{10,11... | collective-permute-start | bytes 2359304 | tf_op jit(solution)/shard_map/ppermute | solution.py:195
  42.9 16.3 %collective-permute-start.10 = (bf16[512,256]{1,0:T(8,128)(2,1)}, bf16[512,256]{1,0:T(8,128)(2,1)}, u32[]{:S(2)}, u32[]{:S(2)}) collective-permute-start(bf16[512,256]{1,0:T(8,128)(2,1)} %get-tuple-element.168), channel_id=1, source_target_pairs={{0,6},{1,7},{2,4},{3,5},{4,2},{5,3},{6,0},{7,1},{8,14},{9,15},{10,... | collective-permute-start | bytes 786440 | tf_op jit(solution)/shard_map/ppermute | solution.py:195
  45.4 20.2 %collective-permute-start.9 = (bf16[512,256]{1,0:T(8,128)(2,1)}, bf16[512,256]{1,0:T(8,128)(2,1)}, u32[]{:S(2)}, u32[]{:S(2)}) collective-permute-start(bf16[512,256]{1,0:T(8,128)(2,1)} %get-tuple-element.169), channel_id=1, source_target_pairs={{0,4},{1,5},{2,6},{3,7},{4,0},{5,1},{6,2},{7,3},{8,12},{9,13},{10,... | collective-permute-start | bytes 786440 | tf_op jit(solution)/shard_map/ppermute | solution.py:195
  45.4 20.9 %collective-permute-start.8 = (bf16[512,256]{1,0:T(8,128)(2,1)S(1)}, bf16[512,256]{1,0:T(8,128)(2,1)}, u32[]{:S(2)}, u32[]{:S(2)}) collective-permute-start(bf16[512,256]{1,0:T(8,128)(2,1)S(1)} %get-tuple-element.170), channel_id=1, source_target_pairs={{0,2},{1,3},{2,0},{3,1},{4,6},{5,7},{6,4},{7,5},{8,10},{9,11},{10,... | collective-permute-start | bytes 786440 | tf_op jit(solution)/shard_map/ppermute | solution.py:195
  59.2 35.5 %collective-permute-start.5 = (bf16[192,2048]{1,0:T(8,128)(2,1)S(1)}, bf16[192,2048]{1,0:T(8,128)(2,1)S(1)}, u32[]{:S(2)}, u32[]{:S(2)}) collective-permute-start(bf16[192,2048]{1,0:T(8,128)(2,1)S(1)} %get-tuple-element.83), channel_id=1, source_target_pairs={{0,1},{1,0},{2,3},{3,2},{4,5},{5,4},{6,7},{7,6},{8,9},{9,8},{10,11... | collective-permute-start | bytes 2359304 | tf_op jit(solution)/shard_map/ppermute | solution.py:195
  65.6 39.3 %collective-permute-start.15 = (bf16[192,2048]{1,0:T(8,128)(2,1)S(1)}, bf16[192,2048]{1,0:T(8,128)(2,1)S(1)}, u32[]{:S(2)}, u32[]{:S(2)}) collective-permute-start(bf16[192,2048]{1,0:T(8,128)(2,1)S(1)} %get-tuple-element.105), channel_id=1, source_target_pairs={{0,1},{1,0},{2,3},{3,2},{4,5},{5,4},{6,7},{7,6},{8,9},{9,8},{10,11... | collective-permute-start | bytes 2359304 | tf_op jit(solution)/shard_map/ppermute | solution.py:195
  72.6 23.5 %collective-permute-start.11 = (bf16[192,2048]{1,0:T(8,128)(2,1)S(1)}, bf16[192,2048]{1,0:T(8,128)(2,1)S(1)}, u32[]{:S(2)}, u32[]{:S(2)}) collective-permute-start(bf16[192,2048]{1,0:T(8,128)(2,1)S(1)} %fusion.4), channel_id=1, source_target_pairs={{0,2},{1,3},{6,4},{7,5},{8,10},{9,11},{14,12},{15,13},{16,18},{17,... | collective-permute-start | bytes 2359304 | tf_op jit(solution)/shard_map/ppermute | solution.py:195
  75.6 29.3 %collective-permute-start.16 = (bf16[192,2048]{1,0:T(8,128)(2,1)S(1)}, bf16[192,2048]{1,0:T(8,128)(2,1)S(1)}, u32[]{:S(2)}, u32[]{:S(2)}) collective-permute-start(bf16[192,2048]{1,0:T(8,128)(2,1)S(1)} %fusion.5), channel_id=1, source_target_pairs={{0,2},{1,3},{6,4},{7,5},{8,10},{9,11},{14,12},{15,13},{16,18},{17,... | collective-permute-start | bytes 2359304 | tf_op jit(solution)/shard_map/ppermute | solution.py:195
  83.0 40.2 %collective-permute-start.14 = (bf16[192,2048]{1,0:T(8,128)(2,1)S(1)}, bf16[192,2048]{1,0:T(8,128)(2,1)S(1)}, u32[]{:S(2)}, u32[]{:S(2)}) collective-permute-start(bf16[192,2048]{1,0:T(8,128)(2,1)S(1)} %get-tuple-element.104), channel_id=1, source_target_pairs={{0,1},{1,0},{2,3},{3,2},{4,5},{5,4},{6,7},{7,6},{8,9},{9,8},{10,11... | collective-permute-start | bytes 2359304 | tf_op jit(solution)/shard_map/ppermute | solution.py:195
  94.7 44.7 %collective-permute-start.22 = (bf16[192,2048]{1,0:T(8,128)(2,1)S(1)}, bf16[192,2048]{1,0:T(8,128)(2,1)S(1)}, u32[]{:S(2)}, u32[]{:S(2)}) collective-permute-start(bf16[192,2048]{1,0:T(8,128)(2,1)S(1)} %get-tuple-element.129), channel_id=1, source_target_pairs={{0,1},{1,0},{2,3},{3,2},{4,5},{5,4},{6,7},{7,6},{8,9},{9,8},{10,11... | collective-permute-start | bytes 2359304 | tf_op jit(solution)/shard_map/ppermute | solution.py:195
  96.1 43.3 %collective-permute-start.13 = (bf16[2,4,512,256]{3,2,1,0:T(8,128)(2,1)}, bf16[2,4,512,256]{3,2,1,0:T(8,128)(2,1)}, u32[]{:S(2)}, u32[]{:S(2)}) collective-permute-start(bf16[2,4,512,256]{3,2,1,0:T(8,128)(2,1)} %bitcast.22.refs_4_), channel_id=1, source_target_pairs={{0,16},{16,0},{1,17},{17,1},{2,18},{18,2},{3,19},{19,3},{4,20},{20... | collective-permute-start | bytes 6291464 | tf_op jit(solution)/shard_map/ppermute | solution.py:290
  105.1 22.0 %collective-permute-start.18 = (bf16[192,2048]{1,0:T(8,128)(2,1)S(1)}, bf16[192,2048]{1,0:T(8,128)(2,1)S(1)}, u32[]{:S(2)}, u32[]{:S(2)}) collective-permute-start(bf16[192,2048]{1,0:T(8,128)(2,1)S(1)} %fusion.6), channel_id=1, source_target_pairs={{0,2},{1,3},{6,4},{7,5},{8,10},{9,11},{14,12},{15,13},{16,18},{17,... | collective-permute-start | bytes 2359304 | tf_op jit(solution)/shard_map/ppermute | solution.py:195
  108.9 18.9 %collective-permute-start.17 = (bf16[192,2048]{1,0:T(8,128)(2,1)S(1)}, bf16[192,2048]{1,0:T(8,128)(2,1)S(1)}, u32[]{:S(2)}, u32[]{:S(2)}) collective-permute-start(bf16[192,2048]{1,0:T(8,128)(2,1)S(1)} %add_convert_fusion.7), channel_id=1, source_target_pairs={{2,4},{3,5},{4,2},{5,3},{10,12},{11,13},{12,10},{13,11},{18,20},{1... | collective-permute-start | bytes 2359304 | tf_op jit(solution)/shard_map/ppermute | solution.py:195
  123.2 20.9 %collective-permute-start.24 = (bf16[192,2048]{1,0:T(8,128)(2,1)S(1)}, bf16[192,2048]{1,0:T(8,128)(2,1)S(1)}, u32[]{:S(2)}, u32[]{:S(2)}) collective-permute-start(bf16[192,2048]{1,0:T(8,128)(2,1)S(1)} %fusion.7), channel_id=1, source_target_pairs={{0,2},{1,3},{6,4},{7,5},{8,10},{9,11},{14,12},{15,13},{16,18},{17,... | collective-permute-start | bytes 2359304 | tf_op jit(solution)/shard_map/ppermute | solution.py:195
  127.1 17.0 %collective-permute-start.23 = (bf16[192,2048]{1,0:T(8,128)(2,1)S(1)}, bf16[192,2048]{1,0:T(8,128)(2,1)S(1)}, u32[]{:S(2)}, u32[]{:S(2)}) collective-permute-start(bf16[192,2048]{1,0:T(8,128)(2,1)S(1)} %add_convert_fusion.3), channel_id=1, source_target_pairs={{2,4},{3,5},{4,2},{5,3},{10,12},{11,13},{12,10},{13,11},{18,20},{1... | collective-permute-start | bytes 2359304 | tf_op jit(solution)/shard_map/ppermute | solution.py:195
  127.8 25.7 %collective-permute-start.12 = (bf16[192,2048]{1,0:T(8,128)(2,1)S(1)}, bf16[192,2048]{1,0:T(8,128)(2,1)S(1)}, u32[]{:S(2)}, u32[]{:S(2)}) collective-permute-start(bf16[192,2048]{1,0:T(8,128)(2,1)S(1)} %get-tuple-element.97), channel_id=1, source_target_pairs={{0,1},{1,0},{2,3},{3,2},{4,5},{5,4},{6,7},{7,6},{8,9},{9,8},{10,11... | collective-permute-start | bytes 2359304 | tf_op jit(solution)/shard_map/ppermute | solution.py:195
  139.4 18.4 %collective-permute-start.19 = (bf16[192,2048]{1,0:T(8,128)(2,1)S(1)}, bf16[192,2048]{1,0:T(8,128)(2,1)}, u32[]{:S(2)}, u32[]{:S(2)}) collective-permute-start(bf16[192,2048]{1,0:T(8,128)(2,1)S(1)} %add_convert_fusion.6), channel_id=1, source_target_pairs={{0,2},{1,3},{2,0},{3,1},{4,6},{5,7},{6,4},{7,5},{8,10},{9,11},{10,... | collective-permute-start | bytes 2359304 | tf_op jit(solution)/shard_map/ppermute | solution.py:195
  139.4 21.0 %collective-permute-start.20 = (bf16[192,2048]{1,0:T(8,128)(2,1)S(1)}, bf16[192,2048]{1,0:T(8,128)(2,1)}, u32[]{:S(2)}, u32[]{:S(2)}) collective-permute-start(bf16[192,2048]{1,0:T(8,128)(2,1)S(1)} %add_convert_fusion.5), channel_id=1, source_target_pairs={{2,4},{3,5},{4,2},{5,3},{10,12},{11,13},{12,10},{13,11},{18,20},{1... | collective-permute-start | bytes 2359304 | tf_op jit(solution)/shard_map/ppermute | solution.py:195
  145.3 31.7 %collective-permute-start.27 = (bf16[2,4,512,256]{3,2,1,0:T(8,128)(2,1)}, bf16[2,4,512,256]{3,2,1,0:T(8,128)(2,1)}, u32[]{:S(2)}, u32[]{:S(2)}) collective-permute-start(bf16[2,4,512,256]{3,2,1,0:T(8,128)(2,1)} %bitcast.22.refs_4_), channel_id=1, source_target_pairs={{0,8},{8,0},{1,9},{9,1},{2,10},{10,2},{3,11},{11,3},{4,12},{12,4},... | collective-permute-start | bytes 6291464 | tf_op jit(solution)/shard_map/ppermute | solution.py:293
  145.3 31.7 %collective-permute-start.28 = (bf16[2,4,512,256]{3,2,1,0:T(8,128)(2,1)}, bf16[2,4,512,256]{3,2,1,0:T(8,128)(2,1)}, u32[]{:S(2)}, u32[]{:S(2)}) collective-permute-start(bf16[2,4,512,256]{3,2,1,0:T(8,128)(2,1)} %collective-permute-done.13.refs_5_), channel_id=1, source_target_pairs={{0,8},{8,0},{1,9},{9,1},{2,10},{10,2},{3,11},{11,3},{4,12},{12,4},... | collective-permute-start | bytes 6291464 | tf_op jit(solution)/shard_map/ppermute | solution.py:293
  153.5 17.8 %collective-permute-start.21 = (bf16[192,2048]{1,0:T(8,128)(2,1)S(1)}, bf16[192,2048]{1,0:T(8,128)(2,1)}, u32[]{:S(2)}, u32[]{:S(2)}) collective-permute-start(bf16[192,2048]{1,0:T(8,128)(2,1)S(1)} %get-tuple-element.127), channel_id=1, source_target_pairs={{0,1},{1,0},{2,3},{3,2},{4,5},{5,4},{6,7},{7,6},{8,9},{9,8},{10,11... | collective-permute-start | bytes 2359304 | tf_op jit(solution)/shard_map/ppermute | solution.py:195
  157.8 15.2 %collective-permute-start.25 = (bf16[192,2048]{1,0:T(8,128)(2,1)}, bf16[192,2048]{1,0:T(8,128)(2,1)}, u32[]{:S(2)}, u32[]{:S(2)}) collective-permute-start(bf16[192,2048]{1,0:T(8,128)(2,1)} %add_convert_fusion.2), channel_id=1, source_target_pairs={{0,2},{1,3},{2,0},{3,1},{4,6},{5,7},{6,4},{7,5},{8,10},{9,11},{10,... | collective-permute-start | bytes 2359304 | tf_op jit(solution)/shard_map/ppermute | solution.py:195
  160.4 12.6 %collective-permute-start.26 = (bf16[192,2048]{1,0:T(8,128)(2,1)}, bf16[192,2048]{1,0:T(8,128)(2,1)}, u32[]{:S(2)}, u32[]{:S(2)}) collective-permute-start(bf16[192,2048]{1,0:T(8,128)(2,1)} %add_convert_fusion.1), channel_id=1, source_target_pairs={{2,4},{3,5},{4,2},{5,3},{10,12},{11,13},{12,10},{13,11},{18,20},{1... | collective-permute-start | bytes 2359304 | tf_op jit(solution)/shard_map/ppermute | solution.py:195
  180.3 12.1 %collective-permute-start.33 = (bf16[4,208,256]{2,1,0:T(8,128)(2,1)S(1)}, bf16[4,208,256]{2,1,0:T(8,128)(2,1)S(1)}, u32[]{:S(2)}, u32[]{:S(2)}) collective-permute-start(bf16[4,208,256]{2,1,0:T(8,128)(2,1)S(1)} %shard_map.99), channel_id=1, source_target_pairs={{0,1},{1,0},{2,3},{3,2},{4,5},{5,4},{6,7},{7,6},{8,9},{9,8},{10,11... | collective-permute-start | bytes 1277960 | tf_op jit(solution)/shard_map/ppermute | solution.py:195
  184.1 18.4 %collective-permute-start.29 = (bf16[4,208,256]{2,1,0:T(8,128)(2,1)S(1)}, bf16[4,208,256]{2,1,0:T(8,128)(2,1)S(1)}, u32[]{:S(2)}, u32[]{:S(2)}) collective-permute-start(bf16[4,208,256]{2,1,0:T(8,128)(2,1)S(1)} %shard_map.96), channel_id=1, source_target_pairs={{0,1},{1,0},{2,3},{3,2},{4,5},{5,4},{6,7},{7,6},{8,9},{9,8},{10,11... | collective-permute-start | bytes 1277960 | tf_op jit(solution)/shard_map/ppermute | solution.py:195
  192.5 13.6 %collective-permute-start.34 = (bf16[208,256]{1,0:T(8,128)(2,1)S(1)}, bf16[208,256]{1,0:T(8,128)(2,1)S(1)}, u32[]{:S(2)}, u32[]{:S(2)}) collective-permute-start(bf16[208,256]{1,0:T(8,128)(2,1)S(1)} %get-tuple-element.154), channel_id=1, source_target_pairs={{0,6},{1,7},{2,4},{3,5},{4,2},{5,3},{6,0},{7,1},{8,14},{9,15},{10,... | collective-permute-start | bytes 319496 | tf_op jit(solution)/shard_map/ppermute | solution.py:195
  198.5 8.5 %collective-permute-start.35 = (bf16[208,256]{1,0:T(8,128)(2,1)S(1)}, bf16[208,256]{1,0:T(8,128)(2,1)S(1)}, u32[]{:S(2)}, u32[]{:S(2)}) collective-permute-start(bf16[208,256]{1,0:T(8,128)(2,1)S(1)} %get-tuple-element.155), channel_id=1, source_target_pairs={{0,4},{1,5},{2,6},{3,7},{4,0},{5,1},{6,2},{7,3},{8,12},{9,13},{10,... | collective-permute-start | bytes 319496 | tf_op jit(solution)/shard_map/ppermute | solution.py:195
  (8 other events, 70.0 us)

commit v4 on v3

--- a/solution.py
+++ b/solution.py
@@ -102,7 +102,7 @@
         ),
         out_shape=[jax.ShapeDtypeStruct((n, width), dtype) for n in cuts],
         compiler_params=PARAMS,
-        cost_estimate=BRIEF,
+        cost_estimate=pl.CostEstimate(flops=1000000000, bytes_accessed=1000, transcendentals=0),
     )(jnp.reshape(at, (1,)), left, weight)
 
 
@@ -259,8 +259,13 @@
     for h in range(8):
         j, side = divmod(h, 2)
         moved = started[h - 2] if h > 1 else other_pieces[1:] if h == 0 else []
-        here, context, *rest = together(arriving[h], context, *own, *moved)
+        values = [arriving[h], context, *own, *moved]
+        if h == 7:
+            values += sums[0][:2]
+        here, context, *rest = together(*values)
         own, moved = rest[:2], rest[2:]
+        if h == 7:
+            sums[0][0], sums[0][1] = moved[2:]
         term = own[side] + wide(here)
         if j == 0:
             far.append(term)
@@ -284,7 +289,7 @@
             streams.append(stream)
             leaving = kv_dot(scaled, quarters, parts, 1, squares)
             staying = kv_dot(scaled, quarters, parts, 0)
-            sums.append((staying, by_xor(leaving, 1), squares))
+            sums.append([staying, leaving, squares])
         if h == 0:
             mine = jnp.stack([*pieces, other_pieces[0], *moved]).reshape((2, *kept.shape))
             other = lax.ppermute(mine, "groups", SWAP)
@@ -299,6 +304,7 @@
                 arriving += [by_xor(block, 1) for block in sent_term(j + 2)]
         if side == 1 and j < 3:
             own = following
+    sums = [(staying, by_xor(leaving, 1), squares) for staying, leaving, squares in sums]
     projected = [kv_finish(*kv_sum(*terms)) for terms in sums]
     return jnp.concatenate(streams, axis=0), jnp.concatenate(projected, axis=0)
 

time: 214 us -> 205 us (0.958)
  waiting for transfers between devices: 60.2 us -> 76.1 us
  local copies, waits for them, and re-layouts: 19.1 us -> 8.16 us
  Pallas kernels: 66.2 us -> 60.4 us
  other arithmetic: 15.1 us -> 9.31 us
    ppermute x33, waiting for transfers between devices: 49.6 us -> 72 us  [over(): return lax.ppermute(block, 'tensor', pairs)]
    unnamed x13 -> x23, local copies, waits for them, and re-layouts: 12.1 us -> 2.85 us
    ppermute x1, waiting for transfers between devices: 10.5 us -> 4.08 us  [chained(): other = lax.ppermute(mine, 'groups', SWAP)]
    pallas_call x4, Pallas kernels: 13.4 us -> 7.37 us  [kv_dot(): pl.pallas_call(kv_kernel, grid_spec=pltpu.PrefetchScalarGridSpec(num_scal...]
    reduce_sum x1 -> x2, other arithmetic: 3.55 us -> 1.29 us  [chained(): squares = jnp.sum(widened * widened, axis=1)]
    convert_element_type x2, other arithmetic: 2.62 us -> 0.36 us  [chained(): started.append([to_middle(term.astype(BF16))])]
    ppermute x33, starting transfers between devices: 48.3 us -> 46 us  [over(): return lax.ppermute(block, 'tensor', pairs)]
  transfers between devices with their start and end apart: 37 -> 37, of which waited for: 14 -> 17; matrix products, arithmetic and copies ran while one was open for 15% -> 6% of each run, Pallas kernels for 29% -> 30%
where the time goes in v4:
time: 205 us
  waiting for transfers between devices  76.1 us (37%)
  Pallas kernels  60.4 us (29%)
  starting transfers between devices  49.5 us (24%)
  other arithmetic  9.31 us (5%)
  local copies, waits for them, and re-layouts  8.16 us (4%)
    ppermute x33, waiting for transfers between devices, over(): return lax.ppermute(block, 'tensor', pairs)  72 us
    pallas_call x8, Pallas kernels, slab_dot(): pl.pallas_call(functools.partial(slab_kernel, cuts), grid_spec=pltpu.Pref...  47.9 us
    ppermute x33, starting transfers between devices, over(): return lax.ppermute(block, 'tensor', pairs)  46 us
    pallas_call x4, Pallas kernels, kv_dot(): pl.pallas_call(kv_kernel, grid_spec=pltpu.PrefetchScalarGridSpec(num_scal...  7.37 us
    pallas_call x1, Pallas kernels, attend(): pl.pallas_call(attend_kernel, grid_spec=pltpu.PrefetchScalarGridSpec(num_...  5.06 us
  transfers between devices with their start and end apart: 37, of which 17 were waited for; matrix products, arithmetic and copies ran while one was open for 6% of the time, Pallas kernels for 30%

profile of v4, /device:TPU:0, one launch (start us, length us, event | category | flops | bytes accessed | tf_op | source)
XLA Modules:
  0.0 204.7 jit_solution(14739575608665105981)
XLA Ops:
  0.7 2.3 %dynamic-slice_bitcast_fusion = bf16[4,512,256]{2,1,0:T(8,128)(2,1)} fusion(bf16[4,2,4,512,256]{4,3,2,1,0:T(8,128)(2,1)} %bitcast.57, s32[]{:T(128)S(6)} %select_n.77, s32[]{:T(128)S(6)} %select_n.79), kind=kLoop, calls=%fused_computation.25 | loop fusion | bytes 2097160 | tf_op jit(solution)/shard_map/jit(dynamic_index_in_dim)/squeeze | solution.py:223
  2.9 3.0 %collective-permute-start.1 = (bf16[4,512,256]{2,1,0:T(8,128)(2,1)}, bf16[4,512,256]{2,1,0:T(8,128)(2,1)S(1)}, u32[]{:S(2)}, u32[]{:S(2)}) collective-permute-start(bf16[4,512,256]{2,1,0:T(8,128)(2,1)} %dynamic-slice_bitcast_fusion), channel_id=1, source_target_pairs={{0,1},{1,0},{2,3},{3,2},{4,5},{5,4},{6,7},{7,6},{8,9},{9,8},{10,11... | collective-permute-start | bytes 3145736 | tf_op jit(solution)/shard_map/ppermute | solution.py:195
  8.4 2.0 dynamic-slice_bitcast_fusion.4
  10.4 3.6 %collective-permute-start.4 = (bf16[512,256]{1,0:T(8,128)(2,1)}, bf16[512,256]{1,0:T(8,128)(2,1)S(1)}, u32[]{:S(2)}, u32[]{:S(2)}) collective-permute-start(bf16[512,256]{1,0:T(8,128)(2,1)} %get-tuple-element.166), channel_id=1, source_target_pairs={{0,6},{1,7},{2,4},{3,5},{4,2},{5,3},{6,0},{7,1},{8,14},{9,15},{10,... | collective-permute-start | bytes 786440 | tf_op jit(solution)/shard_map/ppermute | solution.py:195
  16.4 5.1 %shard_map.86.left_ref = bf16[384,2048]{1,0:T(8,128)(2,1)S(1)} custom-call(s32[1]{0:T(128)} %bitcast.3.seq_ref, bf16[384,2048]{1,0:T(8,128)(2,1)S(1)} %copy-done, bf16[384,256]{1,0:T(8,128)(2,1)S(1)} %collective-permute-done.ek_ref.ev_ref, bf16[384,256]{1,0:T(8,128)(2,1)S(1)} %collective-permute-done.ek_ref.ev_ref, ...), custom_call_target="tpu_custom_call" | custom-call | flops 1000 | bytes 1000 | tf_op jit(solution)/shard_map/pallas_call | solution.py:63
  21.5 5.9 %shard_map.87 = (bf16[192,2048]{1,0:T(8,128)(2,1)S(1)}, bf16[192,2048]{1,0:T(8,128)(2,1)S(1)}) custom-call(s32[1]{0:T(128)} %bitcast.2.at_ref, bf16[384,2048]{1,0:T(8,128)(2,1)S(1)} %shard_map.86.left_ref, bf16[2048,16384]{1,0:T(8,128)(2,1)} %right_ref.15), custom_call_target="tpu_custom_call" | custom-call | flops 1000000000 | bytes 1000 | tf_op jit(solution)/shard_map/pallas_call | solution.py:92
  27.4 8.7 %collective-permute-done.3 = bf16[512,256]{1,0:T(8,128)(2,1)S(1)} collective-permute-done((bf16[512,256]{1,0:T(8,128)(2,1)}, bf16[512,256]{1,0:T(8,128)(2,1)S(1)}, u32[]{:S(2)}, u32[]{:S(2)}) %collective-permute-start.3) | collective-permute-done | bytes 262176 | tf_op jit(solution)/shard_map/ppermute | solution.py:195
  39.3 2.5 %collective-permute-start.10 = (bf16[512,256]{1,0:T(8,128)(2,1)S(1)}, bf16[512,256]{1,0:T(8,128)(2,1)S(1)}, u32[]{:S(2)}, u32[]{:S(2)}) collective-permute-start(bf16[512,256]{1,0:T(8,128)(2,1)S(1)} %get-tuple-element.170), channel_id=1, source_target_pairs={{0,6},{1,7},{2,4},{3,5},{4,2},{5,3},{6,0},{7,1},{8,14},{9,15},{10,... | collective-permute-start | bytes 786440 | tf_op jit(solution)/shard_map/ppermute | solution.py:195
  43.8 5.9 %shard_map.88 = (bf16[192,2048]{1,0:T(8,128)(2,1)S(1)}, bf16[192,2048]{1,0:T(8,128)(2,1)S(1)}) custom-call(s32[1]{0:T(128)} %bitcast.1.at_ref, bf16[384,2048]{1,0:T(8,128)(2,1)S(1)} %shard_map.86.left_ref, bf16[2048,16384]{1,0:T(8,128)(2,1)} %right_ref.15), custom_call_target="tpu_custom_call" | custom-call | flops 1000000000 | bytes 1000 | tf_op jit(solution)/shard_map/pallas_call | solution.py:92
  49.7 6.0 %shard_map.89 = (f32[192,2048]{1,0:T(8,128)S(1)}, f32[192,2048]{1,0:T(8,128)S(1)}) custom-call(s32[1]{0:T(128)} %bitcast.9.at_ref, bf16[384,2048]{1,0:T(8,128)(2,1)S(1)} %shard_map.86.left_ref, bf16[2048,16384]{1,0:T(8,128)(2,1)} %right_ref.15), custom_call_target="tpu_custom_call" | custom-call | flops 1000000000 | bytes 1000 | tf_op jit(solution)/shard_map/pallas_call | solution.py:92
  56.4 5.4 %collective-permute-done.9 = bf16[512,256]{1,0:T(8,128)(2,1)S(1)} collective-permute-done((bf16[512,256]{1,0:T(8,128)(2,1)S(1)}, bf16[512,256]{1,0:T(8,128)(2,1)S(1)}, u32[]{:S(2)}, u32[]{:S(2)}) %collective-permute-start.9) | collective-permute-done | bytes 262176 | tf_op jit(solution)/shard_map/ppermute | solution.py:195
  62.4 11.0 %collective-permute-done.7 = bf16[192,2048]{1,0:T(8,128)(2,1)S(1)} collective-permute-done((bf16[192,2048]{1,0:T(8,128)(2,1)S(1)}, bf16[192,2048]{1,0:T(8,128)(2,1)S(1)}, u32[]{:S(2)}, u32[]{:S(2)}) %collective-permute-start.7) | collective-permute-done | bytes 786464 | tf_op jit(solution)/shard_map/ppermute | solution.py:195
  77.1 5.9 %shard_map.92 = (bf16[192,2048]{1,0:T(8,128)(2,1)S(1)}, bf16[192,2048]{1,0:T(8,128)(2,1)S(1)}) custom-call(s32[1]{0:T(128)} %bitcast.23.at_ref, bf16[384,2048]{1,0:T(8,128)(2,1)S(1)} %shard_map.86.left_ref, bf16[2048,16384]{1,0:T(8,128)(2,1)} %right_ref.15), custom_call_target="tpu_custom_call" | custom-call | flops 1000000000 | bytes 1000 | tf_op jit(solution)/shard_map/pallas_call | solution.py:92
  83.7 6.0 %shard_map.90 = (f32[192,2048]{1,0:T(8,128)S(1)}, f32[192,2048]{1,0:T(8,128)S(1)}) custom-call(s32[1]{0:T(128)} %bitcast.13.at_ref, bf16[384,2048]{1,0:T(8,128)(2,1)S(1)} %shard_map.86.left_ref, bf16[2048,16384]{1,0:T(8,128)(2,1)} %right_ref.15), custom_call_target="tpu_custom_call" | custom-call | flops 1000000000 | bytes 1000 | tf_op jit(solution)/shard_map/pallas_call | solution.py:92
  91.3 2.0 collective-permute-done.11
  94.8 12.4 %collective-permute-done.15 = bf16[192,2048]{1,0:T(8,128)(2,1)S(1)} collective-permute-done((bf16[192,2048]{1,0:T(8,128)(2,1)S(1)}, bf16[192,2048]{1,0:T(8,128)(2,1)S(1)}, u32[]{:S(2)}, u32[]{:S(2)}) %collective-permute-start.15) | collective-permute-done | bytes 786464 | tf_op jit(solution)/shard_map/ppermute | solution.py:195
  108.0 3.4 %collective-permute-start.18 = (bf16[192,2048]{1,0:T(8,128)(2,1)S(1)}, bf16[192,2048]{1,0:T(8,128)(2,1)}, u32[]{:S(2)}, u32[]{:S(2)}) collective-permute-start(bf16[192,2048]{1,0:T(8,128)(2,1)S(1)} %fusion.6), channel_id=1, source_target_pairs={{0,2},{1,3},{6,4},{7,5},{8,10},{9,11},{14,12},{15,13},{16,18},{17,... | collective-permute-start | bytes 2359304 | tf_op jit(solution)/shard_map/ppermute | solution.py:195
  113.6 5.9 %shard_map.91 = (bf16[192,2048]{1,0:T(8,128)(2,1)S(1)}, bf16[192,2048]{1,0:T(8,128)(2,1)S(1)}) custom-call(s32[1]{0:T(128)} %bitcast.at_ref, bf16[384,2048]{1,0:T(8,128)(2,1)S(1)} %shard_map.86.left_ref, bf16[2048,16384]{1,0:T(8,128)(2,1)} %right_ref.15), custom_call_target="tpu_custom_call" | custom-call | flops 1000000000 | bytes 1000 | tf_op jit(solution)/shard_map/pallas_call | solution.py:92
  119.5 6.1 %shard_map.93 = (f32[192,2048]{1,0:T(8,128)S(1)}, f32[192,2048]{1,0:T(8,128)S(1)}) custom-call(s32[1]{0:T(128)} %bitcast.24.at_ref, bf16[384,2048]{1,0:T(8,128)(2,1)S(1)} %shard_map.86.left_ref, bf16[2048,16384]{1,0:T(8,128)(2,1)} %right_ref.15), custom_call_target="tpu_custom_call" | custom-call | flops 1000000000 | bytes 1000 | tf_op jit(solution)/shard_map/pallas_call | solution.py:92
  126.0 2.2 %collective-permute-start.24 = (bf16[192,2048]{1,0:T(8,128)(2,1)S(1)}, bf16[192,2048]{1,0:T(8,128)(2,1)S(1)}, u32[]{:S(2)}, u32[]{:S(2)}) collective-permute-start(bf16[192,2048]{1,0:T(8,128)(2,1)S(1)} %fusion.7), channel_id=1, source_target_pairs={{0,2},{1,3},{6,4},{7,5},{8,10},{9,11},{14,12},{15,13},{16,18},{17,... | collective-permute-start | bytes 2359304 | tf_op jit(solution)/shard_map/ppermute | solution.py:195
  130.4 4.1 %collective-permute-done.13.refs_5_ = bf16[2,4,512,256]{3,2,1,0:T(8,128)(2,1)S(1)} collective-permute-done((bf16[2,4,512,256]{3,2,1,0:T(8,128)(2,1)S(1)}, bf16[2,4,512,256]{3,2,1,0:T(8,128)(2,1)S(1)}, u32[]{:S(2)}, u32[]{:S(2)}) %collective-permute-start.13) | collective-permute-done | bytes 2097184 | tf_op jit(solution)/shard_map/ppermute | solution.py:295
  135.3 3.6 %collective-permute-done.22 = bf16[192,2048]{1,0:T(8,128)(2,1)S(1)} collective-permute-done((bf16[192,2048]{1,0:T(8,128)(2,1)S(1)}, bf16[192,2048]{1,0:T(8,128)(2,1)S(1)}, u32[]{:S(2)}, u32[]{:S(2)}) %collective-permute-start.22) | collective-permute-done | bytes 786464 | tf_op jit(solution)/shard_map/ppermute | solution.py:195
  139.6 2.7 %collective-permute-done.24 = bf16[192,2048]{1,0:T(8,128)(2,1)S(1)} collective-permute-done((bf16[192,2048]{1,0:T(8,128)(2,1)S(1)}, bf16[192,2048]{1,0:T(8,128)(2,1)S(1)}, u32[]{:S(2)}, u32[]{:S(2)}) %collective-permute-start.24) | collective-permute-done | bytes 786464 | tf_op jit(solution)/shard_map/ppermute | solution.py:195
  142.2 2.5 %collective-permute-start.19 = (bf16[192,2048]{1,0:T(8,128)(2,1)S(1)}, bf16[192,2048]{1,0:T(8,128)(2,1)S(1)}, u32[]{:S(2)}, u32[]{:S(2)}) collective-permute-start(bf16[192,2048]{1,0:T(8,128)(2,1)S(1)} %add_convert_fusion.6), channel_id=1, source_target_pairs={{0,2},{1,3},{2,0},{3,1},{4,6},{5,7},{6,4},{7,5},{8,10},{9,11},{10,... | collective-permute-start | bytes 2359304 | tf_op jit(solution)/shard_map/ppermute | solution.py:195
  145.8 6.1 %shard_map.94 = (f32[192,2048]{1,0:T(8,128)S(1)}, f32[192,2048]{1,0:T(8,128)S(1)}) custom-call(s32[1]{0:T(128)} %bitcast.14.at_ref, bf16[384,2048]{1,0:T(8,128)(2,1)S(1)} %shard_map.86.left_ref, bf16[2048,16384]{1,0:T(8,128)(2,1)} %right_ref.15), custom_call_target="tpu_custom_call" | custom-call | flops 1000000000 | bytes 1000 | tf_op jit(solution)/shard_map/pallas_call | solution.py:92
  152.3 4.4 %collective-permute-done.12 = bf16[192,2048]{1,0:T(8,128)(2,1)S(1)} collective-permute-done((bf16[192,2048]{1,0:T(8,128)(2,1)S(1)}, bf16[192,2048]{1,0:T(8,128)(2,1)S(1)}, u32[]{:S(2)}, u32[]{:S(2)}) %collective-permute-start.12) | collective-permute-done | bytes 786464 | tf_op jit(solution)/shard_map/ppermute | solution.py:195
  159.2 2.5 %collective-permute-start.25 = (bf16[192,2048]{1,0:T(8,128)(2,1)S(1)}, bf16[192,2048]{1,0:T(8,128)(2,1)S(1)}, u32[]{:S(2)}, u32[]{:S(2)}) collective-permute-start(bf16[192,2048]{1,0:T(8,128)(2,1)S(1)} %add_convert_fusion.2), channel_id=1, source_target_pairs={{0,2},{1,3},{2,0},{3,1},{4,6},{5,7},{6,4},{7,5},{8,10},{9,11},{10,... | collective-permute-start | bytes 2359304 | tf_op jit(solution)/shard_map/ppermute | solution.py:195
  167.2 6.4 %collective-permute-done.21 = bf16[192,2048]{1,0:T(8,128)(2,1)S(1)} collective-permute-done((bf16[192,2048]{1,0:T(8,128)(2,1)S(1)}, bf16[192,2048]{1,0:T(8,128)(2,1)S(1)}, u32[]{:S(2)}, u32[]{:S(2)}) %collective-permute-start.21) | collective-permute-done | bytes 786464 | tf_op jit(solution)/shard_map/ppermute | solution.py:195
  178.6 8.5 %collective-permute-done.29.got_ref = bf16[4,208,256]{2,1,0:T(8,128)(2,1)S(1)} collective-permute-done((bf16[4,208,256]{2,1,0:T(8,128)(2,1)S(1)}, bf16[4,208,256]{2,1,0:T(8,128)(2,1)S(1)}, u32[]{:S(2)}, u32[]{:S(2)}) %collective-permute-start.29) | collective-permute-done | bytes 426016 | tf_op jit(solution)/shard_map/ppermute | solution.py:195
  191.6 2.2 %collective-permute-start.31 = (bf16[208,256]{1,0:T(8,128)(2,1)S(1)}, bf16[208,256]{1,0:T(8,128)(2,1)S(1)}, u32[]{:S(2)}, u32[]{:S(2)}) collective-permute-start(bf16[208,256]{1,0:T(8,128)(2,1)S(1)} %get-tuple-element.154), channel_id=1, source_target_pairs={{0,4},{1,5},{2,6},{3,7},{4,0},{5,1},{6,2},{7,3},{8,12},{9,13},{10,... | collective-permute-start | bytes 319496 | tf_op jit(solution)/shard_map/ppermute | solution.py:195
  199.6 2.0 collective-permute-done.34
  201.6 2.1 %collective-permute-done.35 = bf16[208,256]{1,0:T(8,128)(2,1)S(1)} collective-permute-done((bf16[208,256]{1,0:T(8,128)(2,1)S(1)}, bf16[208,256]{1,0:T(8,128)(2,1)S(1)}, u32[]{:S(2)}, u32[]{:S(2)}) %collective-permute-start.35) | collective-permute-done | bytes 106528 | tf_op jit(solution)/shard_map/ppermute | solution.py:195
  (115 shorter events, 51.3 us)
Async XLA Ops:
  2.9 33.2 %collective-permute-start.1 = (bf16[4,512,256]{2,1,0:T(8,128)(2,1)}, bf16[4,512,256]{2,1,0:T(8,128)(2,1)S(1)}, u32[]{:S(2)}, u32[]{:S(2)}) collective-permute-start(bf16[4,512,256]{2,1,0:T(8,128)(2,1)} %dynamic-slice_bitcast_fusion), channel_id=1, source_target_pairs={{0,1},{1,0},{2,3},{3,2},{4,5},{5,4},{6,7},{7,6},{8,9},{9,8},{10,11... | collective-permute-start | bytes 3145736 | tf_op jit(solution)/shard_map/ppermute | solution.py:195
  6.9 9.5 %collective-permute-start = (bf16[384,256]{1,0:T(8,128)(2,1)S(1)}, bf16[384,256]{1,0:T(8,128)(2,1)S(1)}, u32[]{:S(2)}, u32[]{:S(2)}) collective-permute-start(bf16[384,256]{1,0:T(8,128)(2,1)S(1)} %pad_maximum_fusion.1.k_ref.v_ref), channel_id=1, source_target_pairs={{0,8},{1,9},{2,10},{3,11},{4,12},{5,13},{6,14},{7,15},{16,24},{17,... | collective-permute-start | bytes 589832 | tf_op jit(solution)/shard_map/ppermute | solution.py:333
  10.4 17.0 %collective-permute-start.4 = (bf16[512,256]{1,0:T(8,128)(2,1)}, bf16[512,256]{1,0:T(8,128)(2,1)S(1)}, u32[]{:S(2)}, u32[]{:S(2)}) collective-permute-start(bf16[512,256]{1,0:T(8,128)(2,1)} %get-tuple-element.166), channel_id=1, source_target_pairs={{0,6},{1,7},{2,4},{3,5},{4,2},{5,3},{6,0},{7,1},{8,14},{9,15},{10,... | collective-permute-start | bytes 786440 | tf_op jit(solution)/shard_map/ppermute | solution.py:195
  14.1 22.1 %collective-permute-start.3 = (bf16[512,256]{1,0:T(8,128)(2,1)}, bf16[512,256]{1,0:T(8,128)(2,1)S(1)}, u32[]{:S(2)}, u32[]{:S(2)}) collective-permute-start(bf16[512,256]{1,0:T(8,128)(2,1)} %get-tuple-element.167), channel_id=1, source_target_pairs={{0,4},{1,5},{2,6},{3,7},{4,0},{5,1},{6,2},{7,3},{8,12},{9,13},{10,... | collective-permute-start | bytes 786440 | tf_op jit(solution)/shard_map/ppermute | solution.py:195
  14.1 22.1 %collective-permute-start.2 = (bf16[512,256]{1,0:T(8,128)(2,1)}, bf16[512,256]{1,0:T(8,128)(2,1)}, u32[]{:S(2)}, u32[]{:S(2)}) collective-permute-start(bf16[512,256]{1,0:T(8,128)(2,1)} %get-tuple-element.168), channel_id=1, source_target_pairs={{0,2},{1,3},{2,0},{3,1},{4,6},{5,7},{6,4},{7,5},{8,10},{9,11},{10,... | collective-permute-start | bytes 786440 | tf_op jit(solution)/shard_map/ppermute | solution.py:195
  36.1 37.3 %collective-permute-start.6 = (bf16[192,2048]{1,0:T(8,128)(2,1)S(1)}, bf16[192,2048]{1,0:T(8,128)(2,1)S(1)}, u32[]{:S(2)}, u32[]{:S(2)}) collective-permute-start(bf16[192,2048]{1,0:T(8,128)(2,1)S(1)} %get-tuple-element.86), channel_id=1, source_target_pairs={{0,1},{1,0},{2,3},{3,2},{4,5},{5,4},{6,7},{7,6},{8,9},{9,8},{10,11... | collective-permute-start | bytes 2359304 | tf_op jit(solution)/shard_map/ppermute | solution.py:195
  36.8 36.7 %collective-permute-start.7 = (bf16[192,2048]{1,0:T(8,128)(2,1)S(1)}, bf16[192,2048]{1,0:T(8,128)(2,1)S(1)}, u32[]{:S(2)}, u32[]{:S(2)}) collective-permute-start(bf16[192,2048]{1,0:T(8,128)(2,1)S(1)} %get-tuple-element.87), channel_id=1, source_target_pairs={{0,1},{1,0},{2,3},{3,2},{4,5},{5,4},{6,7},{7,6},{8,9},{9,8},{10,11... | collective-permute-start | bytes 2359304 | tf_op jit(solution)/shard_map/ppermute | solution.py:195
  39.3 16.5 %collective-permute-start.10 = (bf16[512,256]{1,0:T(8,128)(2,1)S(1)}, bf16[512,256]{1,0:T(8,128)(2,1)S(1)}, u32[]{:S(2)}, u32[]{:S(2)}) collective-permute-start(bf16[512,256]{1,0:T(8,128)(2,1)S(1)} %get-tuple-element.170), channel_id=1, source_target_pairs={{0,6},{1,7},{2,4},{3,5},{4,2},{5,3},{6,0},{7,1},{8,14},{9,15},{10,... | collective-permute-start | bytes 786440 | tf_op jit(solution)/shard_map/ppermute | solution.py:195
  41.8 20.0 %collective-permute-start.9 = (bf16[512,256]{1,0:T(8,128)(2,1)S(1)}, bf16[512,256]{1,0:T(8,128)(2,1)S(1)}, u32[]{:S(2)}, u32[]{:S(2)}) collective-permute-start(bf16[512,256]{1,0:T(8,128)(2,1)S(1)} %get-tuple-element.171), channel_id=1, source_target_pairs={{0,4},{1,5},{2,6},{3,7},{4,0},{5,1},{6,2},{7,3},{8,12},{9,13},{10,... | collective-permute-start | bytes 786440 | tf_op jit(solution)/shard_map/ppermute | solution.py:195
  41.8 20.6 %collective-permute-start.8 = (bf16[512,256]{1,0:T(8,128)(2,1)S(1)}, bf16[512,256]{1,0:T(8,128)(2,1)S(1)}, u32[]{:S(2)}, u32[]{:S(2)}) collective-permute-start(bf16[512,256]{1,0:T(8,128)(2,1)S(1)} %get-tuple-element.172), channel_id=1, source_target_pairs={{0,2},{1,3},{2,0},{3,1},{4,6},{5,7},{6,4},{7,5},{8,10},{9,11},{10,... | collective-permute-start | bytes 786440 | tf_op jit(solution)/shard_map/ppermute | solution.py:195
  55.7 34.6 %collective-permute-start.5 = (bf16[192,2048]{1,0:T(8,128)(2,1)S(1)}, bf16[192,2048]{1,0:T(8,128)(2,1)S(1)}, u32[]{:S(2)}, u32[]{:S(2)}) collective-permute-start(bf16[192,2048]{1,0:T(8,128)(2,1)S(1)} %get-tuple-element.85), channel_id=1, source_target_pairs={{0,1},{1,0},{2,3},{3,2},{4,5},{5,4},{6,7},{7,6},{8,9},{9,8},{10,11... | collective-permute-start | bytes 2359304 | tf_op jit(solution)/shard_map/ppermute | solution.py:195
  61.8 45.4 %collective-permute-start.15 = (bf16[192,2048]{1,0:T(8,128)(2,1)S(1)}, bf16[192,2048]{1,0:T(8,128)(2,1)S(1)}, u32[]{:S(2)}, u32[]{:S(2)}) collective-permute-start(bf16[192,2048]{1,0:T(8,128)(2,1)S(1)} %get-tuple-element.107), channel_id=1, source_target_pairs={{0,1},{1,0},{2,3},{3,2},{4,5},{5,4},{6,7},{7,6},{8,9},{9,8},{10,11... | collective-permute-start | bytes 2359304 | tf_op jit(solution)/shard_map/ppermute | solution.py:195
  73.6 19.7 %collective-permute-start.11 = (bf16[192,2048]{1,0:T(8,128)(2,1)S(1)}, bf16[192,2048]{1,0:T(8,128)(2,1)S(1)}, u32[]{:S(2)}, u32[]{:S(2)}) collective-permute-start(bf16[192,2048]{1,0:T(8,128)(2,1)S(1)} %fusion.4), channel_id=1, source_target_pairs={{0,2},{1,3},{6,4},{7,5},{8,10},{9,11},{14,12},{15,13},{16,18},{17,... | collective-permute-start | bytes 2359304 | tf_op jit(solution)/shard_map/ppermute | solution.py:195
  75.6 31.6 %collective-permute-start.16 = (bf16[192,2048]{1,0:T(8,128)(2,1)S(1)}, bf16[192,2048]{1,0:T(8,128)(2,1)S(1)}, u32[]{:S(2)}, u32[]{:S(2)}) collective-permute-start(bf16[192,2048]{1,0:T(8,128)(2,1)S(1)} %fusion.5), channel_id=1, source_target_pairs={{0,2},{1,3},{6,4},{7,5},{8,10},{9,11},{14,12},{15,13},{16,18},{17,... | collective-permute-start | bytes 2359304 | tf_op jit(solution)/shard_map/ppermute | solution.py:195
  83.0 42.9 %collective-permute-start.14 = (bf16[192,2048]{1,0:T(8,128)(2,1)S(1)}, bf16[192,2048]{1,0:T(8,128)(2,1)S(1)}, u32[]{:S(2)}, u32[]{:S(2)}) collective-permute-start(bf16[192,2048]{1,0:T(8,128)(2,1)S(1)} %get-tuple-element.106), channel_id=1, source_target_pairs={{0,1},{1,0},{2,3},{3,2},{4,5},{5,4},{6,7},{7,6},{8,9},{9,8},{10,11... | collective-permute-start | bytes 2359304 | tf_op jit(solution)/shard_map/ppermute | solution.py:195
  90.3 48.6 %collective-permute-start.22 = (bf16[192,2048]{1,0:T(8,128)(2,1)S(1)}, bf16[192,2048]{1,0:T(8,128)(2,1)S(1)}, u32[]{:S(2)}, u32[]{:S(2)}) collective-permute-start(bf16[192,2048]{1,0:T(8,128)(2,1)S(1)} %get-tuple-element.131), channel_id=1, source_target_pairs={{0,1},{1,0},{2,3},{3,2},{4,5},{5,4},{6,7},{7,6},{8,9},{9,8},{10,11... | collective-permute-start | bytes 2359304 | tf_op jit(solution)/shard_map/ppermute | solution.py:195
  93.3 41.1 %collective-permute-start.13 = (bf16[2,4,512,256]{3,2,1,0:T(8,128)(2,1)S(1)}, bf16[2,4,512,256]{3,2,1,0:T(8,128)(2,1)S(1)}, u32[]{:S(2)}, u32[]{:S(2)}) collective-permute-start(bf16[2,4,512,256]{3,2,1,0:T(8,128)(2,1)S(1)} %bitcast.47), channel_id=1, source_target_pairs={{0,16},{16,0},{1,17},{17,1},{2,18},{18,2},{3,19},{19,3},{4,20},{20... | collective-permute-start | bytes 6291464 | tf_op jit(solution)/shard_map/ppermute | solution.py:295
  108.0 20.1 %collective-permute-start.18 = (bf16[192,2048]{1,0:T(8,128)(2,1)S(1)}, bf16[192,2048]{1,0:T(8,128)(2,1)}, u32[]{:S(2)}, u32[]{:S(2)}) collective-permute-start(bf16[192,2048]{1,0:T(8,128)(2,1)S(1)} %fusion.6), channel_id=1, source_target_pairs={{0,2},{1,3},{6,4},{7,5},{8,10},{9,11},{14,12},{15,13},{16,18},{17,... | collective-permute-start | bytes 2359304 | tf_op jit(solution)/shard_map/ppermute | solution.py:195
  112.7 16.2 %collective-permute-start.17 = (bf16[192,2048]{1,0:T(8,128)(2,1)}, bf16[192,2048]{1,0:T(8,128)(2,1)S(1)}, u32[]{:S(2)}, u32[]{:S(2)}) collective-permute-start(bf16[192,2048]{1,0:T(8,128)(2,1)} %add_convert_fusion.7), channel_id=1, source_target_pairs={{2,4},{3,5},{4,2},{5,3},{10,12},{11,13},{12,10},{13,11},{18,20},{1... | collective-permute-start | bytes 2359304 | tf_op jit(solution)/shard_map/ppermute | solution.py:195
  126.0 16.3 %collective-permute-start.24 = (bf16[192,2048]{1,0:T(8,128)(2,1)S(1)}, bf16[192,2048]{1,0:T(8,128)(2,1)S(1)}, u32[]{:S(2)}, u32[]{:S(2)}) collective-permute-start(bf16[192,2048]{1,0:T(8,128)(2,1)S(1)} %fusion.7), channel_id=1, source_target_pairs={{0,2},{1,3},{6,4},{7,5},{8,10},{9,11},{14,12},{15,13},{16,18},{17,... | collective-permute-start | bytes 2359304 | tf_op jit(solution)/shard_map/ppermute | solution.py:195
  128.2 16.6 %collective-permute-start.23 = (bf16[192,2048]{1,0:T(8,128)(2,1)S(1)}, bf16[192,2048]{1,0:T(8,128)(2,1)S(1)}, u32[]{:S(2)}, u32[]{:S(2)}) collective-permute-start(bf16[192,2048]{1,0:T(8,128)(2,1)S(1)} %add_convert_fusion.3), channel_id=1, source_target_pairs={{2,4},{3,5},{4,2},{5,3},{10,12},{11,13},{12,10},{13,11},{18,20},{1... | collective-permute-start | bytes 2359304 | tf_op jit(solution)/shard_map/ppermute | solution.py:195
  134.4 29.1 %collective-permute-start.27 = (bf16[2,4,512,256]{3,2,1,0:T(8,128)(2,1)S(1)}, bf16[2,4,512,256]{3,2,1,0:T(8,128)(2,1)S(1)}, u32[]{:S(2)}, u32[]{:S(2)}) collective-permute-start(bf16[2,4,512,256]{3,2,1,0:T(8,128)(2,1)S(1)} %bitcast.48), channel_id=1, source_target_pairs={{0,8},{8,0},{1,9},{9,1},{2,10},{10,2},{3,11},{11,3},{4,12},{12,4},... | collective-permute-start | bytes 6291464 | tf_op jit(solution)/shard_map/ppermute | solution.py:298
  134.5 29.1 %collective-permute-start.28 = (bf16[2,4,512,256]{3,2,1,0:T(8,128)(2,1)S(1)}, bf16[2,4,512,256]{3,2,1,0:T(8,128)(2,1)S(1)}, u32[]{:S(2)}, u32[]{:S(2)}) collective-permute-start(bf16[2,4,512,256]{3,2,1,0:T(8,128)(2,1)S(1)} %collective-permute-done.13.refs_5_), channel_id=1, source_target_pairs={{0,8},{8,0},{1,9},{9,1},{2,10},{10,2},{3,11},{11,3},{4,12},{12,4},... | collective-permute-start | bytes 6291464 | tf_op jit(solution)/shard_map/ppermute | solution.py:298
  138.9 17.7 %collective-permute-start.12 = (bf16[192,2048]{1,0:T(8,128)(2,1)S(1)}, bf16[192,2048]{1,0:T(8,128)(2,1)S(1)}, u32[]{:S(2)}, u32[]{:S(2)}) collective-permute-start(bf16[192,2048]{1,0:T(8,128)(2,1)S(1)} %get-tuple-element.99), channel_id=1, source_target_pairs={{0,1},{1,0},{2,3},{3,2},{4,5},{5,4},{6,7},{7,6},{8,9},{9,8},{10,11... | collective-permute-start | bytes 2359304 | tf_op jit(solution)/shard_map/ppermute | solution.py:195
  142.2 17.0 %collective-permute-start.19 = (bf16[192,2048]{1,0:T(8,128)(2,1)S(1)}, bf16[192,2048]{1,0:T(8,128)(2,1)S(1)}, u32[]{:S(2)}, u32[]{:S(2)}) collective-permute-start(bf16[192,2048]{1,0:T(8,128)(2,1)S(1)} %add_convert_fusion.6), channel_id=1, source_target_pairs={{0,2},{1,3},{2,0},{3,1},{4,6},{5,7},{6,4},{7,5},{8,10},{9,11},{10,... | collective-permute-start | bytes 2359304 | tf_op jit(solution)/shard_map/ppermute | solution.py:195
  144.7 17.0 %collective-permute-start.20 = (bf16[192,2048]{1,0:T(8,128)(2,1)S(1)}, bf16[192,2048]{1,0:T(8,128)(2,1)S(1)}, u32[]{:S(2)}, u32[]{:S(2)}) collective-permute-start(bf16[192,2048]{1,0:T(8,128)(2,1)S(1)} %add_convert_fusion.5), channel_id=1, source_target_pairs={{2,4},{3,5},{4,2},{5,3},{10,12},{11,13},{12,10},{13,11},{18,20},{1... | collective-permute-start | bytes 2359304 | tf_op jit(solution)/shard_map/ppermute | solution.py:195
  156.6 17.0 %collective-permute-start.21 = (bf16[192,2048]{1,0:T(8,128)(2,1)S(1)}, bf16[192,2048]{1,0:T(8,128)(2,1)S(1)}, u32[]{:S(2)}, u32[]{:S(2)}) collective-permute-start(bf16[192,2048]{1,0:T(8,128)(2,1)S(1)} %get-tuple-element.129), channel_id=1, source_target_pairs={{0,1},{1,0},{2,3},{3,2},{4,5},{5,4},{6,7},{7,6},{8,9},{9,8},{10,11... | collective-permute-start | bytes 2359304 | tf_op jit(solution)/shard_map/ppermute | solution.py:195
  159.2 14.6 %collective-permute-start.25 = (bf16[192,2048]{1,0:T(8,128)(2,1)S(1)}, bf16[192,2048]{1,0:T(8,128)(2,1)S(1)}, u32[]{:S(2)}, u32[]{:S(2)}) collective-permute-start(bf16[192,2048]{1,0:T(8,128)(2,1)S(1)} %add_convert_fusion.2), channel_id=1, source_target_pairs={{0,2},{1,3},{2,0},{3,1},{4,6},{5,7},{6,4},{7,5},{8,10},{9,11},{10,... | collective-permute-start | bytes 2359304 | tf_op jit(solution)/shard_map/ppermute | solution.py:195
  161.7 12.1 %collective-permute-start.26 = (bf16[192,2048]{1,0:T(8,128)(2,1)S(1)}, bf16[192,2048]{1,0:T(8,128)(2,1)S(1)}, u32[]{:S(2)}, u32[]{:S(2)}) collective-permute-start(bf16[192,2048]{1,0:T(8,128)(2,1)S(1)} %add_convert_fusion.1), channel_id=1, source_target_pairs={{2,4},{3,5},{4,2},{5,3},{10,12},{11,13},{12,10},{13,11},{18,20},{1... | collective-permute-start | bytes 2359304 | tf_op jit(solution)/shard_map/ppermute | solution.py:195
  174.4 12.7 %collective-permute-start.29 = (bf16[4,208,256]{2,1,0:T(8,128)(2,1)S(1)}, bf16[4,208,256]{2,1,0:T(8,128)(2,1)S(1)}, u32[]{:S(2)}, u32[]{:S(2)}) collective-permute-start(bf16[4,208,256]{2,1,0:T(8,128)(2,1)S(1)} %shard_map.96), channel_id=1, source_target_pairs={{0,1},{1,0},{2,3},{3,2},{4,5},{5,4},{6,7},{7,6},{8,9},{9,8},{10,11... | collective-permute-start | bytes 1277960 | tf_op jit(solution)/shard_map/ppermute | solution.py:195
  177.9 16.9 %collective-permute-start.33 = (bf16[4,208,256]{2,1,0:T(8,128)(2,1)S(1)}, bf16[4,208,256]{2,1,0:T(8,128)(2,1)S(1)}, u32[]{:S(2)}, u32[]{:S(2)}) collective-permute-start(bf16[4,208,256]{2,1,0:T(8,128)(2,1)S(1)} %shard_map.99), channel_id=1, source_target_pairs={{0,1},{1,0},{2,3},{3,2},{4,5},{5,4},{6,7},{7,6},{8,9},{9,8},{10,11... | collective-permute-start | bytes 1277960 | tf_op jit(solution)/shard_map/ppermute | solution.py:195
  187.2 10.2 %collective-permute-start.30 = (bf16[208,256]{1,0:T(8,128)(2,1)S(1)}, bf16[208,256]{1,0:T(8,128)(2,1)S(1)}, u32[]{:S(2)}, u32[]{:S(2)}) collective-permute-start(bf16[208,256]{1,0:T(8,128)(2,1)S(1)} %get-tuple-element.153), channel_id=1, source_target_pairs={{0,6},{1,7},{2,4},{3,5},{4,2},{5,3},{6,0},{7,1},{8,14},{9,15},{10,... | collective-permute-start | bytes 319496 | tf_op jit(solution)/shard_map/ppermute | solution.py:195
  (13 other events, 85.4 us)
